TPU v7x, 32 devices: a whole 2x2x4 slice. The times are simulated.
32 devices in a mesh: dp: 8 (over z, y), seq: 4 (over x, core).
Axes of the slice: x: 2, y: 2, z: 4, core: 2. Of those that a mesh axis runs over, the one named last changes fastest.
Arguments:
- tokens: bfloat16 [24, 1024, 384], P('dp', 'seq'), may hold values from -6 to 6
- timestep: bfloat16 [24, 384], P('dp'), may hold values from -6 to 6
- counts: int32 [8], P('dp'), may hold values from 1 to 3, as said below
- token_mask: int32 [24, 1024], P('dp', 'seq'), may hold values 0 or 1
- ada_weight: bfloat16 [384, 1152], replicated, may hold values from -0.3125 to 0.3125
- ada_bias: float32 [1152], replicated, may hold values from -1.5 to 1.5
- input_weight: bfloat16 [384, 1536], replicated, may hold values from -0.3125 to 0.3125
- conv_weight: float32 [2, 4, 768], replicated, may hold values from -2.5 to 2.5
- conv_bias: float32 [2, 768], replicated, may hold values from -1.5 to 1.5
- x_weight: bfloat16 [2, 768, 56], replicated, may hold values from -0.109375 to 0.109375
- dt_weight: bfloat16 [2, 24, 768], replicated, may hold values from -6 to 6
- dt_bias: float32 [2, 768], replicated, may hold values from -2 to 0.5
- decay_rate: float32 [2, 16, 768], replicated, may hold values from 0.0001 to 0.05
- skip_gain: float32 [2, 768], replicated, may hold values from 0.5 to 1.5
- output_weight: bfloat16 [768, 384], replicated, may hold values from -0.21875 to 0.21875
- cotangent: bfloat16 [24, 1024, 384], P('dp', 'seq'), may hold values from -6 to 6
Outputs:
- mixed: bfloat16 [24, 1024, 384], P('dp', 'seq')
- grad_tokens: float32 [24, 1024, 384], P('dp', 'seq')
- grad_time: float32 [24, 384], P('dp')
- grad_ada: float32 [384, 1152], replicated
- grad_ada_bias: float32 [1152], replicated
- input_weight_gradient: float32 [384, 1536], replicated
- grad_conv: float32 [2, 4, 768], replicated
- grad_conv_bias: float32 [2, 768], replicated
- grad_xproj: float32 [2, 768, 56], replicated
- grad_dtproj: float32 [2, 24, 768], replicated
- grad_dt_bias: float32 [2, 768], replicated
- grad_rate: float32 [2, 16, 768], replicated
- grad_skip: float32 [2, 768], replicated
- output_weight_gradient: float32 [768, 384], replicated
Inputs may be any that keep to these rules, and one draw needn't show every extreme that they name: `counts`: number of live item slots of each dp index; padding slots are the highest ones; every draw has an index with 3 and one with 1. `token_mask`: 1 for a valid token, 0 for a dropped one.
All inputs are finite; a program needn't handle non-finite values. No bound on the sum of `token_mask` on one device may be relied on, other than what follows from the above.
Results may differ from a plain program's by a relative error of at most 0.008.
The roundings to bfloat16 on the way count: a program that leaves them out, or rounds other values in their place, can miss the bound.
Values may be sent and summed in bfloat16 or wider, within the bound.
A program may use at most 192 MiB of HBM per device.

v0:
```python
import functools
import math

import jax
import jax.numpy as jnp
from jax import lax
from jax.experimental import pallas as pl
from jax.experimental.pallas import tpu as pltpu
from jax.sharding import PartitionSpec as P

EPSILON = 1e-06
BLK = 16
HALO = 16
LOG2E = math.log2(math.e)
F32, BF16 = jnp.float32, jnp.bfloat16
NT = (((1,), (1,)), ((), ()))
TN = (((0,), (0,)), ((), ()))
VMEM_LIMIT = 60 << 20


def dot(a, b):
    return jnp.dot(a, b, preferred_element_type=F32)


def dot_nt(a, b):
    return lax.dot_general(a, b, NT, preferred_element_type=F32)


def dot_tn(a, b):
    return lax.dot_general(a, b, TN, preferred_element_type=F32)


def reversal(size):
    rows = lax.broadcasted_iota(jnp.int32, (size, size), 0)
    cols = lax.broadcasted_iota(jnp.int32, (size, size), 1)
    return (rows + cols == size - 1).astype(BF16)


def flip_low(value):
    return dot(reversal(value.shape[0]), value).astype(BF16)


def flip_full(value):
    order = reversal(value.shape[0])
    high = value.astype(BF16)
    return dot(order, high) + dot(order, (value - high.astype(F32)).astype(BF16))


def normalise(tokens_f):
    centered = tokens_f - jnp.mean(tokens_f, axis=-1, keepdims=True)
    inv_std = lax.rsqrt(jnp.mean(centered * centered, axis=-1, keepdims=True) + EPSILON)
    return centered * inv_std, inv_std


def enter_kernel(tok, prev, nxt, cot, mod, valid, win, wout, xe, dy, z_out, hid_out):
    dim = tok.shape[-1]
    inner = wout.shape[0]
    shift, scale, gate = mod[:, :dim], mod[:, dim : 2 * dim], mod[:, 2 * dim :]

    def hidden_of(part):
        normed, _ = normalise(part.astype(F32))
        return (normed * (1.0 + scale) + shift).astype(BF16)

    hid = hidden_of(tok[...])
    hid_out[...] = hid
    xz = dot(hid, win[...]) * valid[...]
    x_low = xz[:, :inner].astype(BF16)
    z = xz[:, inner:]
    z_out[...] = z
    rims = jnp.concatenate([prev[...], nxt[...]], axis=0)
    rim_x = dot(hidden_of(rims[:, :dim]), win[:, :inner]) * rims[:, dim : dim + 1].astype(F32)
    rim_x = rim_x.astype(BF16)
    xe[0, :HALO, :] = rim_x[:HALO]
    xe[0, HALO:, :] = x_low
    xe[1, :HALO, :] = flip_low(rim_x[HALO:])
    xe[1, HALO:, :] = flip_low(x_low)
    d_branch = (cot[...].astype(F32) * gate).astype(BF16)
    d_summed = dot_nt(d_branch, wout[...]) * z * jax.nn.sigmoid(z)
    dy[0] = d_summed
    dy[1] = flip_full(d_summed)


def twice(row8):
    return jnp.concatenate([row8, row8], axis=0)


def spread(ref, index):
    return twice(ref[pl.ds(index, 8, stride=0), :])


def columns(ref, block, first, count):
    lane = pl.multiple_of((block // 8) * 128, 128)
    return pltpu.roll(ref[first : first + count, pl.ds(lane, 128)], (128 - (block % 8) * BLK) % 128, 1)


def first_kernel(
    xe, dy, taps, tap_bias, xwt, dtw, dt_bias, rate2,
    act_out, dsilu_out, delta_out, sig_out, proj_out, end_out, back_out, total_out, starts_out, sums_out,
    xf, dl, dx, drow, xrow, yrow, decay, through,
):
    toks, inner = dy.shape
    states = rate2.shape[0]
    blocks = toks // BLK
    rank = dtw.shape[0]
    tap_count = taps.shape[0]
    xf[...] = xe[...].astype(F32)
    conv = tap_bias[...] + jnp.zeros((toks, inner), F32)
    for k in range(tap_count):
        conv = conv + taps[k : k + 1, :] * xf[HALO - tap_count + 1 + k : HALO - tap_count + 1 + k + toks, :]
    sig = jax.nn.sigmoid(conv)
    act = (conv * sig).astype(BF16)
    dsilu_out[...] = sig * (1.0 + conv * (1.0 - sig))
    act_out[...] = act
    proj = dot_nt(xwt[...], act)
    proj_out[...] = proj
    pre = dot_tn(proj[:rank, :].astype(BF16), dtw[...]) + dt_bias[...]
    delta = jnp.maximum(pre, 0.0) + jnp.log1p(jnp.exp(-jnp.abs(pre)))
    delta_out[...] = delta
    sig_out[...] = jax.nn.sigmoid(pre)
    dl[...] = delta
    dx[...] = delta * act.astype(F32)
    end_out[...] = jnp.zeros((states, inner), F32)
    back_out[...] = jnp.zeros((states, inner), F32)
    through[...] = jnp.zeros((8, inner), F32)

    def block_step(j, _):
        t0 = pl.multiple_of(j * BLK, BLK)
        drow[...] = dl[pl.ds(t0, BLK), :]
        xrow[...] = dx[pl.ds(t0, BLK), :]
        yrow[...] = dy[pl.ds(t0, BLK), :]
        bt = columns(proj_out, j, rank, states)
        ct = columns(proj_out, j, rank + states, states)
        rate = rate2[...]
        s = end_out[...]
        starts_out[j] = s
        before = through[...]
        sums_out[j] = before[:1, :]
        for i in range(BLK):
            a = jnp.exp2(spread(drow, i) * rate)
            decay[i] = a
            s = a * s + spread(xrow, i) * jnp.broadcast_to(bt[:, i : i + 1], (states, inner))
        end_out[...] = s
        m = jnp.zeros((states, inner), F32)
        for i in reversed(range(BLK)):
            m = decay[i] * (m + spread(yrow, i) * jnp.broadcast_to(ct[:, i : i + 1], (states, inner)))
        back_out[...] = back_out[...] + m * jnp.exp2(twice(before) * rate)
        through[...] = before + jnp.sum(drow[...], axis=0, keepdims=True)
        return 0

    lax.fori_loop(0, blocks, block_step, 0)
    total_out[...] = through[:1, :]


def second_kernel(
    place, ends, backs, totals, starts, sums, rate2, rate, xe, act, dsilu, delta, sig, dy, proj, xwt, bwide, cwide, dtw, taps, skip,
    y_out, dxe_out, rate_grad, skip_grad, dtb_grad, dtp_grad, xp_grad, tap_grad, tapb_grad,
    enter, carry, dxs, bdiag, cdiag, drow, xrow, yrow, decay, states_low, lam_low, rq_low, racc, gsum, hsum, db, dc, pads, xf,
):
    toks, inner = dy.shape
    states = rate2.shape[0]
    blocks = toks // BLK
    rank = dtw.shape[0]
    tap_count = taps.shape[0]
    branch = pl.program_id(0)
    item = pl.program_id(1)
    runs = ends.shape[0]
    me = place[0]
    r2 = rate2[...]
    mine = jnp.where(branch == 0, me, runs - 1 - me)
    s_in = jnp.zeros((states, inner), F32)
    lam_in = jnp.zeros((states, inner), F32)
    for position in range(runs):
        run = jnp.where(branch == 0, position, runs - 1 - position)
        passing = jnp.exp2(twice(jnp.broadcast_to(totals[run], (8, inner))) * r2)
        s_in = jnp.where(position < mine, passing * s_in + ends[run], s_in)
    for position in reversed(range(runs)):
        run = jnp.where(branch == 0, position, runs - 1 - position)
        passing = jnp.exp2(twice(jnp.broadcast_to(totals[run], (8, inner))) * r2)
        lam_in = jnp.where(position > mine, passing * lam_in + backs[run], lam_in)
    enter[...] = s_in
    carry[...] = lam_in
    act_low = act[...]
    act_f = act_low.astype(F32)
    dxs[...] = delta[...] * act_f
    width = bwide.shape[1]
    own = lax.broadcasted_iota(jnp.int32, (toks, width), 0) % BLK == lax.broadcasted_iota(jnp.int32, (toks, width), 1) // states
    bdiag[...] = jnp.where(own, dot(act_low, bwide[...]), 0.0).astype(BF16)
    cdiag[...] = jnp.where(own, dot(act_low, cwide[...]), 0.0).astype(BF16)
    racc[...] = jnp.zeros((states, inner), F32)

    def block_step(step, _):
        j = blocks - 1 - step
        t0 = pl.multiple_of(j * BLK, BLK)
        drow[...] = delta[pl.ds(t0, BLK), :]
        xrow[...] = dxs[pl.ds(t0, BLK), :]
        yrow[...] = dy[pl.ds(t0, BLK), :]
        bt = columns(proj, j, rank, states)
        ct = columns(proj, j, rank + states, states)
        r2 = rate2[...]
        rr = rate[...]
        s = starts[j] + enter[...] * jnp.exp2(twice(jnp.broadcast_to(sums[j], (8, inner))) * r2)
        states_low[:states, :] = s.astype(BF16)
        for i in range(BLK):
            a = jnp.exp2(spread(drow, i) * r2)
            decay[i] = a
            s = a * s + spread(xrow, i) * jnp.broadcast_to(bt[:, i : i + 1], (states, inner))
            states_low[(i + 1) * states : (i + 2) * states, :] = s.astype(BF16)
        cr = carry[...]
        ra = racc[...]
        for i in reversed(range(BLK)):
            lam = cr + spread(yrow, i) * jnp.broadcast_to(ct[:, i : i + 1], (states, inner))
            lam_low[i * states : (i + 1) * states, :] = lam.astype(BF16)
            cr = decay[i] * lam
            q = cr * states_low[i * states : (i + 1) * states, :].astype(F32)
            rq_low[i * states : (i + 1) * states, :] = (q * rr).astype(BF16)
            ra = ra + q * spread(drow, i)
        carry[...] = cr
        racc[...] = ra
        after = states_low[states:, :]
        lam_all = lam_low[...]
        y_out[pl.ds(t0, BLK), :] = dot(cdiag[pl.ds(t0, BLK), :], after)
        gsum[pl.ds(t0, BLK), :] = dot(bdiag[pl.ds(t0, BLK), :], lam_all)
        ones = (
            lax.broadcasted_iota(jnp.int32, (BLK, BLK * states), 1) // states
            == lax.broadcasted_iota(jnp.int32, (BLK, BLK * states), 0)
        )
        hsum[pl.ds(t0, BLK), :] = dot(ones.astype(BF16), rq_low[...])
        dc[pl.ds(t0, BLK), :] = jnp.where(ones, dot_nt(yrow[...].astype(BF16), after), 0.0).astype(BF16)
        db[pl.ds(t0, BLK), :] = jnp.where(ones, dot_nt(xrow[...].astype(BF16), lam_all), 0.0).astype(BF16)
        return 0

    lax.fori_loop(0, blocks, block_step, 0)

    @pl.when(item == 0)
    def _():
        for ref in (rate_grad, skip_grad, dtb_grad, dtp_grad, xp_grad, tap_grad, tapb_grad):
            ref[...] = jnp.zeros(ref.shape, ref.dtype)

    rate_grad[...] += -racc[...]
    d_summed = dy[...]
    g = gsum[...]
    skip_grad[...] += jnp.sum(d_summed * act_f, axis=0, keepdims=True)
    y_out[...] += skip[...] * act_f
    d_pre = (act_f * g - hsum[...]) * sig[...]
    dtb_grad[...] += jnp.sum(d_pre, axis=0, keepdims=True)
    d_pre_low = d_pre.astype(BF16)
    dtp_grad[...] += dot(proj[:rank, :].astype(BF16), d_pre_low)
    fold = (
        lax.broadcasted_iota(jnp.int32, (states, width), 1) % states == lax.broadcasted_iota(jnp.int32, (states, width), 0)
    ).astype(BF16)
    d_proj = jnp.concatenate(
        [dot_nt(dtw[...], d_pre_low), dot_nt(fold, db[...]), dot_nt(fold, dc[...])], axis=0
    ).astype(BF16)
    xp_grad[...] += dot(d_proj, act_low)
    d_act = delta[...] * g + skip[...] * d_summed + dot_tn(d_proj, xwt[...])
    d_conv = d_act * dsilu[...]
    tapb_grad[...] += jnp.sum(d_conv, axis=0, keepdims=True)
    xf[...] = xe[...].astype(F32)
    pads[:HALO, :] = jnp.zeros((HALO, inner), F32)
    pads[HALO : HALO + toks, :] = d_conv
    pads[HALO + toks :, :] = jnp.zeros((HALO, inner), F32)
    d_window = jnp.zeros((HALO + toks, inner), F32)
    first = HALO - tap_count + 1
    for k in range(tap_count):
        tap_grad[k : k + 1, :] += jnp.sum(d_conv * xf[first + k : first + k + toks, :], axis=0, keepdims=True)
        d_window = d_window + taps[k : k + 1, :] * pads[tap_count - 1 - k : tap_count - 1 - k + HALO + toks, :]
    dxe_out[...] = d_window


def third_kernel(
    tok, cot, mod, valid, hid, z_in, y, dxe, late, win, wout,
    mixed, d_tokens, d_mod, out_grad, in_grad,
):
    dim = tok.shape[-1]
    toks, inner = z_in.shape
    shift, scale, gate = mod[:, :dim], mod[:, dim : 2 * dim], mod[:, 2 * dim :]
    tok_f = tok[...].astype(F32)
    normed, inv_std = normalise(tok_f)
    cot_f = cot[...].astype(F32)
    z = z_in[...]
    z_sig = jax.nn.sigmoid(z)
    summed = y[0] + flip_full(y[1])
    gated = (summed * z * z_sig).astype(BF16)
    branch_out = dot(gated, wout[...])
    mixed[...] = (tok_f + gate * branch_out).astype(BF16)
    d_branch = (cot_f * gate).astype(BF16)
    d_gated = dot_nt(d_branch, wout[...])
    d_zgate = d_gated * summed * z_sig * (1.0 + z * (1.0 - z_sig))
    edge = late.shape[1]

    def with_late(part, extra):
        return jnp.concatenate([part[: toks - edge], part[toks - edge :] + extra], axis=0)

    d_x = with_late(dxe[0, HALO:, :], late[0]) + flip_full(with_late(dxe[1, HALO:, :], late[1]))
    d_xz = (jnp.concatenate([d_x, d_zgate], axis=1) * valid[...]).astype(BF16)
    d_hidden = dot_nt(d_xz, win[...])

    @pl.when(pl.program_id(0) == 0)
    def _():
        out_grad[...] = jnp.zeros(out_grad.shape, F32)
        in_grad[...] = jnp.zeros(in_grad.shape, F32)

    out_grad[...] += dot_tn(gated, d_branch)
    in_grad[...] += dot_tn(hid[...], d_xz)
    d_mod[:, :dim] = jnp.sum(d_hidden, axis=0, keepdims=True)
    d_mod[:, dim : 2 * dim] = jnp.sum(d_hidden * normed, axis=0, keepdims=True)
    d_mod[:, 2 * dim :] = jnp.sum(cot_f * branch_out, axis=0, keepdims=True)
    d_normed = d_hidden * (1.0 + scale)
    d_tokens[...] = cot_f + inv_std * (
        d_normed
        - jnp.mean(d_normed, axis=-1, keepdims=True)
        - normed * jnp.mean(d_normed * normed, axis=-1, keepdims=True)
    )


def params(**more):
    return pltpu.CompilerParams(vmem_limit_bytes=VMEM_LIMIT, **more)


def spec(block, index):
    return pl.BlockSpec(block, index)


def per_device(
    tokens, timestep, counts, token_mask, ada_weight, ada_bias, input_weight, conv_weight, conv_bias, x_weight, dt_weight,
    dt_bias, decay_rate, skip_gain, output_weight, cotangent,
):
    slots, toks, dim = tokens.shape
    inner = output_weight.shape[0]
    rank = dt_weight.shape[1]
    states = decay_rate.shape[1]
    tap_count = conv_weight.shape[1]
    wide_rank = 32
    proj_rows = wide_rank + 2 * states
    blocks = toks // BLK
    runs = lax.axis_size("seq")
    place = lax.axis_index("seq")
    live = (jnp.arange(slots) < counts[0]).astype(F32)
    valid = (token_mask.astype(F32) * live[:, None])[:, :, None]
    time_f = timestep.astype(F32)
    time_sig = jax.nn.sigmoid(time_f)
    time_low = (time_f * time_sig).astype(BF16)
    modulate = (dot(time_low, ada_weight) + ada_bias)[:, None, :]

    rim = jnp.concatenate([tokens, jnp.broadcast_to(valid, (slots, toks, 128)).astype(BF16)], axis=2)
    up = [(i, i + 1) for i in range(runs - 1)]
    down = [(i + 1, i) for i in range(runs - 1)]
    from_prev = lax.ppermute(rim[:, toks - HALO :], "seq", up)
    from_next = lax.ppermute(rim[:, :HALO], "seq", down)

    xwt = jnp.swapaxes(x_weight, 1, 2)
    xwt = jnp.concatenate(
        [xwt[:, :rank], jnp.zeros((2, wide_rank - rank, inner), BF16), xwt[:, rank:]], axis=1
    )
    dtw = jnp.concatenate([dt_weight, jnp.zeros((2, wide_rank - rank, inner), BF16)], axis=1)
    bwide = jnp.tile(x_weight[:, :, rank : rank + states], (1, 1, BLK))
    cwide = jnp.tile(x_weight[:, :, rank + states :], (1, 1, BLK))
    rate2 = -LOG2E * decay_rate
    vec = lambda a: a[:, None, :]

    def item(*block):
        return spec((None,) + block, lambda i: (i,) + (0,) * len(block))

    def whole(*block):
        return spec(block, lambda *_: (0,) * len(block))

    xe, dy, z_gate, hid = pl.pallas_call(
        enter_kernel,
        grid=(slots,),
        in_specs=[
            item(toks, dim), item(HALO, dim + 128), item(HALO, dim + 128), item(toks, dim), item(1, 3 * dim), item(toks, 1),
            whole(dim, 2 * inner), whole(inner, dim),
        ],
        out_specs=[item(2, HALO + toks, inner), item(2, toks, inner), item(toks, inner), item(toks, dim)],
        out_shape=[
            jax.ShapeDtypeStruct((slots, 2, HALO + toks, inner), BF16),
            jax.ShapeDtypeStruct((slots, 2, toks, inner), F32),
            jax.ShapeDtypeStruct((slots, toks, inner), F32),
            jax.ShapeDtypeStruct((slots, toks, dim), BF16),
        ],
        compiler_params=params(),
        name="enter",
    )(tokens, from_prev, from_next, cotangent, modulate, valid, input_weight, output_weight)

    def unit(*block):
        return spec((None, None) + block, lambda b, i: (i, b) + (0,) * len(block))

    def branch(*block):
        return spec((None,) + block, lambda b, i: (b,) + (0,) * len(block))

    def unit_shape(*block, kind=F32):
        return jax.ShapeDtypeStruct((slots, 2) + block, kind)

    act, dsilu, delta, sig, proj, end, back, total, starts, sums = pl.pallas_call(
        first_kernel,
        grid=(2, slots),
        in_specs=[
            unit(HALO + toks, inner), unit(toks, inner), branch(tap_count, inner), branch(1, inner), branch(proj_rows, inner),
            branch(wide_rank, inner), branch(1, inner), branch(states, inner),
        ],
        out_specs=[
            unit(toks, inner), unit(toks, inner), unit(toks, inner), unit(toks, inner), unit(proj_rows, toks),
            unit(states, inner), unit(states, inner), unit(1, inner), unit(blocks, states, inner), unit(blocks, 1, inner),
        ],
        out_shape=[
            unit_shape(toks, inner, kind=BF16), unit_shape(toks, inner), unit_shape(toks, inner), unit_shape(toks, inner),
            unit_shape(proj_rows, toks), unit_shape(states, inner), unit_shape(states, inner), unit_shape(1, inner),
            unit_shape(blocks, states, inner), unit_shape(blocks, 1, inner),
        ],
        scratch_shapes=[
            pltpu.VMEM((HALO + toks, inner), F32), pltpu.VMEM((toks, inner), F32), pltpu.VMEM((toks, inner), F32),
            pltpu.VMEM((BLK, inner), F32), pltpu.VMEM((BLK, inner), F32), pltpu.VMEM((BLK, inner), F32),
            pltpu.VMEM((BLK, states, inner), F32), pltpu.VMEM((8, inner), F32),
        ],
        compiler_params=params(),
        name="first",
    )(xe, dy, conv_weight, vec(conv_bias), xwt, dtw, vec(dt_bias), rate2)

    ends, backs, totals = (lax.all_gather(a, "seq") for a in (end, back, total))

    def gathered(*block):
        return spec((runs, None, None) + block, lambda b, i: (0, i, b) + (0,) * len(block))

    y, dxe, rate_grad, skip_grad, dtb_grad, dtp_grad, xp_grad, tap_grad, tapb_grad = pl.pallas_call(
        second_kernel,
        grid=(2, slots),
        in_specs=[
            pl.BlockSpec(memory_space=pltpu.SMEM),
            gathered(states, inner), gathered(states, inner), gathered(1, inner), unit(blocks, states, inner),
            unit(blocks, 1, inner), branch(states, inner), branch(states, inner), unit(HALO + toks, inner), unit(toks, inner),
            unit(toks, inner), unit(toks, inner), unit(toks, inner), unit(toks, inner), unit(proj_rows, toks),
            branch(proj_rows, inner), branch(inner, BLK * states), branch(inner, BLK * states), branch(wide_rank, inner),
            branch(tap_count, inner), branch(1, inner),
        ],
        out_specs=[
            unit(toks, inner), unit(HALO + toks, inner), branch(states, inner), branch(1, inner), branch(1, inner),
            branch(wide_rank, inner), branch(proj_rows, inner), branch(tap_count, inner), branch(1, inner),
        ],
        out_shape=[
            unit_shape(toks, inner), unit_shape(HALO + toks, inner),
        ] + [
            jax.ShapeDtypeStruct((2, rows, inner), F32) for rows in (states, 1, 1, wide_rank, proj_rows, tap_count, 1)
        ],
        scratch_shapes=[
            pltpu.VMEM((states, inner), F32), pltpu.VMEM((states, inner), F32), pltpu.VMEM((toks, inner), F32),
            pltpu.VMEM((toks, BLK * states), BF16), pltpu.VMEM((toks, BLK * states), BF16),
            pltpu.VMEM((BLK, inner), F32), pltpu.VMEM((BLK, inner), F32), pltpu.VMEM((BLK, inner), F32),
            pltpu.VMEM((BLK, states, inner), F32), pltpu.VMEM(((BLK + 1) * states, inner), BF16),
            pltpu.VMEM((BLK * states, inner), BF16), pltpu.VMEM((BLK * states, inner), BF16),
            pltpu.VMEM((states, inner), F32), pltpu.VMEM((toks, inner), F32), pltpu.VMEM((toks, inner), F32),
            pltpu.VMEM((toks, BLK * states), BF16), pltpu.VMEM((toks, BLK * states), BF16),
            pltpu.VMEM((toks + 2 * HALO, inner), F32), pltpu.VMEM((toks + HALO, inner), F32),
        ],
        compiler_params=params(),
        name="second",
    )(
        jnp.reshape(place, (1,)).astype(jnp.int32), ends, backs, totals, starts, sums, rate2, decay_rate, xe, act, dsilu, delta,
        sig, dy, proj, xwt, bwide, cwide, dtw, conv_weight, vec(skip_gain),
    )

    late = jnp.stack(
        [
            lax.ppermute(dxe[:, 0, HALO - 8 : HALO], "seq", down),
            lax.ppermute(dxe[:, 1, HALO - 8 : HALO], "seq", up),
        ],
        axis=1,
    )

    mixed, d_tokens, d_mod, out_grad, in_grad = pl.pallas_call(
        third_kernel,
        grid=(slots,),
        in_specs=[
            item(toks, dim), item(toks, dim), item(1, 3 * dim), item(toks, 1), item(toks, dim), item(toks, inner),
            item(2, toks, inner), item(2, HALO + toks, inner), item(2, 8, inner), whole(dim, 2 * inner), whole(inner, dim),
        ],
        out_specs=[item(toks, dim), item(toks, dim), item(1, 3 * dim), whole(inner, dim), whole(dim, 2 * inner)],
        out_shape=[
            jax.ShapeDtypeStruct((slots, toks, dim), BF16), jax.ShapeDtypeStruct((slots, toks, dim), F32),
            jax.ShapeDtypeStruct((slots, 1, 3 * dim), F32), jax.ShapeDtypeStruct((inner, dim), F32),
            jax.ShapeDtypeStruct((dim, 2 * inner), F32),
        ],
        compiler_params=params(),
        name="third",
    )(tokens, cotangent, modulate, valid, hid, z_gate, y, dxe, late, input_weight, output_weight)

    d_mod_low = lax.psum(d_mod[:, 0], "seq").astype(BF16)
    d_time = dot_nt(d_mod_low, ada_weight) * time_sig * (1.0 + time_f * (1.0 - time_sig))
    factors = lax.all_gather(jnp.concatenate([time_low, d_mod_low], axis=1), "dp", tiled=True)
    all_time, all_mod = factors[:, :dim], factors[:, dim:]
    grad_ada = dot_tn(all_time, all_mod)
    grad_ada_bias = jnp.sum(all_mod.astype(F32), axis=0)
    summed = lax.psum(
        (in_grad, out_grad, rate_grad, skip_grad, dtb_grad, dtp_grad, xp_grad, tap_grad, tapb_grad), ("dp", "seq")
    )
    in_grad, out_grad, rate_grad, skip_grad, dtb_grad, dtp_grad, xp_grad, tap_grad, tapb_grad = summed
    xp_grad = jnp.swapaxes(jnp.concatenate([xp_grad[:, :rank], xp_grad[:, wide_rank:]], axis=1), 1, 2)
    return (
        mixed, d_tokens, d_time, grad_ada, grad_ada_bias, in_grad, tap_grad, tapb_grad[:, 0], xp_grad, dtp_grad[:, :rank],
        dtb_grad[:, 0], rate_grad, skip_grad[:, 0], out_grad,
    )


def solution(mesh):
    runs = P("dp", "seq", None)
    return jax.shard_map(
        per_device,
        mesh=mesh,
        in_specs=(runs, P("dp", None), P("dp"), P("dp", "seq")) + (P(),) * 11 + (runs,),
        out_specs=(runs, runs, P("dp", None)) + (P(),) * 11,
        check_vma=False,
    )
```

profile of v0, /device:TPU:0, one launch (start us, length us, event | category | flops | bytes accessed | tf_op | source)
XLA Modules:
  0.0 405.7 jit_solution(12870546634059505831)
XLA Ops:
  8.0 0.8 fusion.9
  8.9 0.8 pad_maximum_fusion.2
  9.8 2.4 collective-permute-start
  12.1 1.3 collective-permute-start.1
  13.4 0.9 slice.53
  14.3 0.9 slice.52
  15.3 0.9 convolution_add_fusion
  16.2 0.8 pad_maximum_fusion.xwt
  17.0 0.7 broadcast_multiply_fusion.rate2
  17.7 0.6 broadcast_in_dim.22.mod
  18.3 0.9 copy.46.valid
  19.2 0.6 broadcast_in_dim.25.tap_bias
  19.8 0.6 concatenate.17.dtw
  20.5 0.6 broadcast_in_dim.26.dt_bias
  21.1 0.6 copy-done.6
  21.7 0.6 copy-done.7
  22.3 8.4 %enter.1 = (bf16[3,2,272,768]{3,2,1,0:T(8,128)(2,1)}, f32[3,2,256,768]{3,2,1,0:T(8,128)}, f32[3,256,768]{2,1,0:T(8,128)}, bf16[3,256,384]{2,1,0:T(8,128)(2,1)}) custom-call(bf16[3,256,384]{2,1,0:T(8,128)(2,1)} %tok.3, bf16[3,16,512]{2,1,0:T(8,128)(2,1)} %copy-done.6, bf16[3,16,512]{2,1,0:T(8,128)(2,1)} %copy-done.7, bf16[3,256,384]{2,1,0:T(8,128)(2,1)} %cot.3, ...), custom_call_target="tpu_custom_call" | custom-call | tf_op jit(solution)/shard_map/enter/pallas_call | solution.py:367
  30.8 45.8 %first.1 = (bf16[3,2,256,768]{3,2,1,0:T(8,128)(2,1)}, f32[3,2,256,768]{3,2,1,0:T(8,128)}, f32[3,2,256,768]{3,2,1,0:T(8,128)}, f32[3,2,256,768]{3,2,1,0:T(8,128)}...) custom-call(bf16[3,2,272,768]{3,2,1,0:T(8,128)(2,1)} %get-tuple-elem, ...), custom_call_target="tpu_custom_call" | custom-call | tf_op jit(solution)/shard_map/first/pallas_call | solution.py:394
  76.7 0.7 all-gather.9.cloned.1.call-update
  77.5 1.2 copy.42.bwide
  78.8 1.2 copy.43.cwide
  79.9 0.6 broadcast_in_dim.27.skip
  80.5 8.1 %all-gather.2 = f32[12,2,1,768]{3,1,2,0:T(2,128)S(1)} all-gather(f32[3,2,1,768]{3,1,2,0:T(2,128)S(1)} %copy.41), channel_id=4, replica_groups=mesh['dp'=8,'seq'=4] {'seq'}, dimensions={0}, use_global_device_ids=true | all-gather | bytes 92160 | tf_op jit(solution)/shard_map/all_gather | solution.py:419
  88.6 0.7 reshape.49.totals
  89.4 9.5 %all-gather.7.cloned.1.call-done = f32[12,2,16,768]{3,2,1,0:T(8,128)} async-done(((f32[3,2,16,768]{3,2,1,0:T(8,128)}), f32[12,2,16,768]{3,2,1,0:T(8,128)}) %all-gather.7.cloned.1.call-update) | async-done | bytes 1179664 | tf_op jit(solution)/shard_map/all_gather | solution.py:419
  98.9 19.1 %all-gather.9.cloned.1.call-done = f32[12,2,16,768]{3,2,1,0:T(8,128)} async-done(((f32[3,2,16,768]{3,2,1,0:T(8,128)}), f32[12,2,16,768]{3,2,1,0:T(8,128)}) %all-gather.9.cloned.1.call-update) | async-done | bytes 1179664 | tf_op jit(solution)/shard_map/all_gather | solution.py:419
  117.9 104.4 %second.1 = (f32[3,2,256,768]{3,2,1,0:T(8,128)}, f32[3,2,272,768]{3,2,1,0:T(8,128)}, f32[2,16,768]{2,1,0:T(8,128)}, f32[2,1,768]{2,1,0:T(1,128)}, f32[2,1,768]{2...) custom-call(s32[1]{0:T(128)} %bitcast.2.place, ...), custom_call_target="tpu_custom_call" | custom-call | tf_op jit(solution)/shard_map/second/pallas_call | solution.py:424
  222.4 0.9 slice_bitcast_fusion.1
  223.3 2.1 collective-permute-start.3
  225.4 1.3 collective-permute-start.2
  226.8 1.8 collective-permute-done.2
  228.6 0.7 pad_maximum_fusion.1.late
  229.3 12.9 %third.1 = (bf16[3,256,384]{2,1,0:T(8,128)(2,1)}, f32[3,256,384]{2,1,0:T(8,128)}, f32[3,1,1152]{2,1,0:T(1,128)}, f32[768,384]{1,0:T(8,128)}, f32[384,1536]{1,0:T(8,128)}) custom-call(bf16[3,256,384]{2,1,0:T(8,128)(2,1)} %tok.3, bf16[3,256,384]{2,1,0:T(8,128)(2,1)} %cot.3, f32[3,1,1152]{2,1,0:T(1,128)} %broadcast_in_dim.22.mod, f32[3,256,1]{2,1,0:T(8,128)} %copy.46.valid, ...), custom_call_target="tpu_custom_call" | custom-call | tf_op jit(solution)/shard_map/third/pallas_call | solution.py:469
  242.3 0.6 copy-done.8
  243.0 43.3 %all-reduce.1 = (f32[2,4,768]{2,1,0:T(4,128)}, f32[2,768]{1,0:T(2,128)}, f32[2,768]{1,0:T(2,128)}, f32[2,768]{1,0:T(2,128)}) all-reduce(f32[2,4,768]{2,1,0:T(4,128)S(1)} %copy-done.9, f32[2,768]{1,0:T(2,128)S(1)} %bitcast.44, f32[2,768]{1,0:T(2,128)S(1)} %get-tuple-element.88, ...), channel_id=1, replica_groups=mesh['dp'=8,'seq'=4] {'dp','seq'}, use_global_device_ids=true, to_apply=%region_3.0 | all-reduce | flops 10752 | bytes 86016 | tf_op jit(solution)/shard_map/psum | solution.py:492
  286.4 10.8 %psum.70 = bf16[3,1152]{1,0:T(4,128)(2,1)S(1)} all-reduce(f32[3,1152]{1,0:T(4,128)S(1)} %bitcast.41), channel_id=1, replica_groups=mesh['dp'=8,'seq'=4] {'seq'}, use_global_device_ids=true, to_apply=%region_0.0 | all-reduce | flops 3456 | bytes 20736 | tf_op jit(solution)/shard_map/psum | solution.py:486
  297.2 30.6 %all-gather.3 = bf16[8,3,1536]{2,1,0:T(4,128)(2,1)S(1)} all-gather(bf16[1,3,1536]{2,1,0:T(4,128)(2,1)S(1)} %maximum_bitcast_fusion.1), channel_id=1, replica_groups=mesh['dp'=8,'seq'=4] {'dp'}, dimensions={0}, use_global_device_ids=true | all-gather | bytes 82944 | tf_op jit(solution)/shard_map/all_gather | solution.py:488
  327.8 0.6 convert_reduce_fusion
  328.4 0.9 fusion
  329.4 1.6 fusion.1
  331.0 59.0 %all-reduce.5.cloned.1.call-done = (f32[384,1536]{1,0:T(8,128)}, f32[2,64,768]{2,1,0:T(8,128)}, f32[2,32,768]{2,1,0:T(8,128)}, f32[2,16,768]{2,1,0:T(8,128)}, f32[768,384]{1,0:T(8,128)}) async-done(((f32[384,1536]{1,0:T(8,128)}, f32[2,64,768]{2,1,0:T(8,128)}, f32[2,32,768]{2,1,0:T(8,128)}, f32[2,16,768]{2,1,0:T(8,128)}, f32[768,384]{1,0:T(8,128)}), (f32[384,1536]{1,0:T(8,128)}, f32[2,64,768]{2,1,0:T(8,128)}, ...) | async-done | bytes 4227088 | tf_op jit(solution)/shard_map/psum | solution.py:492
  390.0 0.9 slice.59
  390.9 0.9 slice.58
  391.9 1.6 slice.60
  393.4 0.8 maximum_bitcast_fusion
  394.2 3.3 copy.65
  397.5 0.6 copy.66
  398.2 1.0 copy.67
  (55 shorter events, 0.8 us)
Async XLA Ops:
  7.2 8.1 %copy-start = (bf16[384,1152]{1,0:T(8,128)(2,1)S(1)}, bf16[384,1152]{1,0:T(8,128)(2,1)}, u32[]{:S(2)}) copy-start(bf16[384,1152]{1,0:T(8,128)(2,1)} %param.20) | copy-start | bytes 2654212
  7.2 9.8 %copy-start.3 = (f32[2,16,768]{2,1,0:T(8,128)S(1)}, f32[2,16,768]{2,1,0:T(8,128)}, u32[]{:S(2)}) copy-start(f32[2,16,768]{2,1,0:T(8,128)} %rate.1) | copy-start | bytes 294916
  7.2 12.0 %copy-start.12 = (f32[2,768]{1,0:T(2,128)S(1)}, f32[2,768]{1,0:T(2,128)}, u32[]{:S(2)}) copy-start(f32[2,768]{1,0:T(2,128)} %param.24) | copy-start | bytes 18436
  7.2 12.6 %copy-start.5 = (bf16[2,24,768]{2,1,0:T(8,128)(2,1)S(1)}, bf16[2,24,768]{2,1,0:T(8,128)(2,1)}, u32[]{:S(2)}) copy-start(bf16[2,24,768]{2,1,0:T(8,128)(2,1)} %param.26) | copy-start | bytes 221188
  7.2 13.3 %copy-start.13 = (f32[2,768]{1,0:T(2,128)S(1)}, f32[2,768]{1,0:T(2,128)}, u32[]{:S(2)}) copy-start(f32[2,768]{1,0:T(2,128)} %param.27) | copy-start | bytes 18436
  7.2 91.6 %all-gather.7.cloned.1.call-start = ((), (), s32[]{:S(2)}) async-start(), calls=%async_computation | async-start | bytes 1474560 | tf_op jit(solution)/shard_map/all_gather | solution.py:419
  9.8 11.3 %collective-permute-start = (bf16[3,16,512]{2,1,0:T(8,128)(2,1)S(1)}, bf16[3,16,512]{2,1,0:T(8,128)(2,1)S(1)}, u32[]{:S(2)}, u32[]{:S(2)}) collective-permute-start(bf16[3,16,512]{2,1,0:T(8,128)(2,1)S(1)} %get-tuple-element.82), channel_id=1, source_target_pairs={{0,1},{1,2},{2,3},{4,5},{5,6},{6,7},{8,9},{9,10},{10,11},{12,13},{... | collective-permute-start | bytes 147464 | tf_op jit(solution)/shard_map/ppermute | solution.py:348
  12.1 9.0 %collective-permute-start.1 = (bf16[3,16,512]{2,1,0:T(8,128)(2,1)S(1)}, bf16[3,16,512]{2,1,0:T(8,128)(2,1)S(1)}, u32[]{:S(2)}, u32[]{:S(2)}) collective-permute-start(bf16[3,16,512]{2,1,0:T(8,128)(2,1)S(1)} %get-tuple-element.81), channel_id=1, source_target_pairs={{1,0},{2,1},{3,2},{5,4},{6,5},{7,6},{9,8},{10,9},{11,10},{13,12},{... | collective-permute-start | bytes 147464 | tf_op jit(solution)/shard_map/ppermute | solution.py:349
  21.1 0.6 copy-start.6
  21.7 0.6 copy-start.7
  30.8 46.7 %copy-start.2 = (bf16[2,768,56]{1,2,0:T(8,128)(2,1)S(1)}, bf16[2,768,56]{1,2,0:T(8,128)(2,1)}, u32[]{:S(2)}) copy-start(bf16[2,768,56]{1,2,0:T(8,128)(2,1)} %param.25) | copy-start | bytes 516100
  76.6 41.3 %all-gather.9.cloned.1.call-start = ((), (), s32[]{:S(2)}) async-start(), calls=%async_computation.1 | async-start | bytes 1474560 | tf_op jit(solution)/shard_map/all_gather | solution.py:419
  77.4 312.6 %all-reduce.5.cloned.1.call-start = ((), (), s32[]{:S(2)}) async-start(), calls=%async_computation.2 | async-start | bytes 8454144 | tf_op jit(solution)/shard_map/psum | solution.py:492
  77.5 2.5 copy-start.14
  77.5 3.0 copy-start.10
  223.3 3.5 collective-permute-start.3
  225.4 3.2 collective-permute-start.2
  242.2 0.7 copy-start.8
  242.2 0.7 copy-start.15
  242.2 0.7 copy-start.16
  242.3 0.7 copy-start.17
  242.3 0.8 copy-start.9
  242.3 44.1 %copy-start.11 = (f32[3,1,1152]{2,1,0:T(1,128)S(1)}, f32[3,1,1152]{2,1,0:T(1,128)}, u32[]{:S(2)}) copy-start(f32[3,1,1152]{2,1,0:T(1,128)} %get-tuple-element.60) | copy-start | bytes 41476
  394.2 3.3 copy-start.4
  394.2 4.0 copy-start.1
Sparse Core Ops, SparseCore 0:
  76.8 22.0 all-gather.6
  100.4 17.4 all-gather.8
  242.4 147.4 all-reduce.4
where the time goes:
time: 406 us
  Pallas kernels  172 us (42%)
  blocking collectives  92.8 us (23%)
  waiting for transfers between devices  90.1 us (22%)
  local copies, waits for them, and re-layouts  20.6 us (5%)
  between operations  14.8 us (4%)
  starting transfers between devices  7.2 us (2%)
  other arithmetic  5.08 us (1%)
    pallas_call x1, Pallas kernels, per_device(): pl.pallas_call(second_kernel, grid=(2, slots), in_specs=[pl.BlockSpec(mem...  104 us
    psum x1, waiting for transfers between devices, per_device(): lax.psum((in_grad, out_grad, rate_grad, skip_grad, dtb_grad, dtp_grad, xp...  59 us
    pallas_call x1, Pallas kernels, per_device(): pl.pallas_call(first_kernel, grid=(2, slots), in_specs=[unit(HALO + toks,...  45.8 us
    psum x1, blocking collectives, per_device(): lax.psum((in_grad, out_grad, rate_grad, skip_grad, dtb_grad, dtp_grad, xp...  43.3 us
    all_gather x1, blocking collectives, per_device(): lax.all_gather(jnp.concatenate([time_low, d_mod_low], axis=1), 'dp', tile...  30.6 us
    all_gather x2, waiting for transfers between devices, per_device(): ends, backs, totals = (lax.all_gather(a, 'seq') for a in (end, back, total))  28.5 us
    pallas_call x1, Pallas kernels, per_device(): pl.pallas_call(third_kernel, grid=(slots,), in_specs=[item(toks, dim), it...  12.9 us
    psum x1, blocking collectives, per_device(): d_mod_low = lax.psum(d_mod[:, 0], 'seq').astype(BF16)  10.8 us
  transfers between devices with their start and end apart: 7, of which 4 were waited for; matrix products, arithmetic and copies ran while one was open for 4% of the time, Pallas kernels for 0%

commit v1 on v0

--- a/solution.py
+++ b/solution.py
@@ -16,6 +16,7 @@
 NT = (((1,), (1,)), ((), ()))
 TN = (((0,), (0,)), ((), ()))
 VMEM_LIMIT = 60 << 20
+MESH = pl.DeviceIdType.MESH
 
 
 def dot(a, b):
@@ -52,32 +53,139 @@
     return centered * inv_std, inv_std
 
 
-def enter_kernel(tok, prev, nxt, cot, mod, valid, win, wout, xe, dy, z_out, hid_out):
-    dim = tok.shape[-1]
+def eye(size):
+    rows = lax.broadcasted_iota(jnp.int32, (size, size), 0)
+    cols = lax.broadcasted_iota(jnp.int32, (size, size), 1)
+    return (rows == cols).astype(BF16)
+
+
+def as_column(row):
+    return dot_nt(eye(row.shape[1]), jnp.broadcast_to(row.astype(F32).astype(BF16), (8, row.shape[1])))[:, :1]
+
+
+def remote(src, dst, send_sem, recv_sem, target):
+    return pltpu.make_async_remote_copy(
+        src_ref=src, dst_ref=dst, send_sem=send_sem, recv_sem=recv_sem, device_id=target, device_id_type=MESH
+    )
+
+
+def greet(targets):
+    barrier = pltpu.get_barrier_semaphore()
+    for target in targets:
+        pl.semaphore_signal(barrier, inc=1, device_id=target, device_id_type=MESH)
+    pl.semaphore_wait(barrier, len(targets))
+
+
+def greet_line(me, runs):
+    barrier = pltpu.get_barrier_semaphore()
+
+    @pl.when(me > 0)
+    def _():
+        pl.semaphore_signal(barrier, inc=1, device_id={"seq": me - 1}, device_id_type=MESH)
+
+    @pl.when(me < runs - 1)
+    def _():
+        pl.semaphore_signal(barrier, inc=1, device_id={"seq": me + 1}, device_id_type=MESH)
+
+    neighbours = (me + runs - 1) // runs + (2 * runs - 2 - me) // runs
+    pl.semaphore_wait(barrier, neighbours)
+
+
+def swap_along_line(me, runs, ups, downs, start):
+    up = [remote(src, dst, ss, rs, {"seq": me + 1}) for src, dst, ss, rs in ups]
+    down = [remote(src, dst, ss, rs, {"seq": me - 1}) for src, dst, ss, rs in downs]
+
+    @pl.when(me < runs - 1)
+    def _():
+        for copy in up:
+            if start:
+                copy.start()
+            else:
+                copy.wait_send()
+        if not start:
+            for copy in down:
+                copy.wait_recv()
+
+    @pl.when(me > 0)
+    def _():
+        for copy in down:
+            if start:
+                copy.start()
+            else:
+                copy.wait_send()
+        if not start:
+            for copy in up:
+                copy.wait_recv()
+
+
+def enter_kernel(
+    runs, tok, cot, mask, counts, step, ada, ada_bias, win, wout,
+    xe, dy, z_out, hid_out, mod_out,
+    prev_tok, next_tok, prev_mask, next_mask, send_sem, recv_sem,
+):
+    slots, toks, dim = tok.shape
     inner = wout.shape[0]
+    me = lax.axis_index("seq")
+    i = pl.program_id(0)
+    ups = [
+        (tok.at[:, pl.ds(toks - HALO, HALO), :], prev_tok, send_sem.at[0], recv_sem.at[0]),
+        (mask, prev_mask, send_sem.at[1], recv_sem.at[1]),
+    ]
+    downs = [
+        (tok.at[:, pl.ds(0, HALO), :], next_tok, send_sem.at[2], recv_sem.at[2]),
+        (mask, next_mask, send_sem.at[3], recv_sem.at[3]),
+    ]
+
+    @pl.when(i == 0)
+    def _():
+        greet_line(me, runs)
+        swap_along_line(me, runs, ups, downs, True)
+
+        @pl.when(me == 0)
+        def _():
+            prev_tok[...] = jnp.zeros(prev_tok.shape, BF16)
+            prev_mask[...] = jnp.zeros(prev_mask.shape, jnp.int32)
+
+        @pl.when(me == runs - 1)
+        def _():
+            next_tok[...] = jnp.zeros(next_tok.shape, BF16)
+            next_mask[...] = jnp.zeros(next_mask.shape, jnp.int32)
+
+    live = (counts[...] > i).astype(F32)
+    time_f = step[...].astype(F32)
+    time_low = (time_f * jax.nn.sigmoid(time_f)).astype(BF16)
+    mod = dot(time_low, ada[...]) + ada_bias[...]
+    mod_out[...] = mod
     shift, scale, gate = mod[:, :dim], mod[:, dim : 2 * dim], mod[:, 2 * dim :]
 
     def hidden_of(part):
         normed, _ = normalise(part.astype(F32))
         return (normed * (1.0 + scale) + shift).astype(BF16)
 
-    hid = hidden_of(tok[...])
+    hid = hidden_of(tok[i])
     hid_out[...] = hid
-    xz = dot(hid, win[...]) * valid[...]
+    xz = dot(hid, win[...]) * (as_column(mask[pl.ds(i, 1), :]) * live)
     x_low = xz[:, :inner].astype(BF16)
     z = xz[:, inner:]
     z_out[...] = z
-    rims = jnp.concatenate([prev[...], nxt[...]], axis=0)
-    rim_x = dot(hidden_of(rims[:, :dim]), win[:, :inner]) * rims[:, dim : dim + 1].astype(F32)
-    rim_x = rim_x.astype(BF16)
-    xe[0, :HALO, :] = rim_x[:HALO]
-    xe[0, HALO:, :] = x_low
-    xe[1, :HALO, :] = flip_low(rim_x[HALO:])
-    xe[1, HALO:, :] = flip_low(x_low)
     d_branch = (cot[...].astype(F32) * gate).astype(BF16)
     d_summed = dot_nt(d_branch, wout[...]) * z * jax.nn.sigmoid(z)
     dy[0] = d_summed
     dy[1] = flip_full(d_summed)
+    xe[0, HALO:, :] = x_low
+    xe[1, HALO:, :] = flip_low(x_low)
+
+    @pl.when(i == 0)
+    def _():
+        swap_along_line(me, runs, ups, downs, False)
+
+    rims = jnp.concatenate([prev_tok[i], next_tok[i]], axis=0)
+    prev_col = as_column(prev_mask[pl.ds(i, 1), :])[toks - HALO :]
+    next_col = as_column(next_mask[pl.ds(i, 1), :])[:HALO]
+    rim_x = dot(hidden_of(rims), win[:, :inner]) * (jnp.concatenate([prev_col, next_col], axis=0) * live)
+    rim_x = rim_x.astype(BF16)
+    xe[0, :HALO, :] = rim_x[:HALO]
+    xe[1, :HALO, :] = flip_low(rim_x[HALO:])
 
 
 def twice(row8):
@@ -152,33 +260,17 @@
 
 
 def second_kernel(
-    place, ends, backs, totals, starts, sums, rate2, rate, xe, act, dsilu, delta, sig, dy, proj, xwt, bwide, cwide, dtw, taps, skip,
-    y_out, dxe_out, rate_grad, skip_grad, dtb_grad, dtp_grad, xp_grad, tap_grad, tapb_grad,
-    enter, carry, dxs, bdiag, cdiag, drow, xrow, yrow, decay, states_low, lam_low, rq_low, racc, gsum, hsum, db, dc, pads, xf,
+    s_in, lam_in, starts, sums, rate2, rate, xe, act, dsilu, delta, sig, dy, proj, xwt, bwide, cwide, dtw, taps, skip,
+    y_out, dx_out, rim_out, rate_grad, skip_grad, dtb_grad, dtp_grad, xp_grad, tap_grad, tapb_grad,
+    carry, dxs, bdiag, cdiag, drow, xrow, yrow, decay, states_low, lam_low, rq_low, racc, gsum, hsum, db, dc, pads, xf,
 ):
     toks, inner = dy.shape
     states = rate2.shape[0]
     blocks = toks // BLK
     rank = dtw.shape[0]
     tap_count = taps.shape[0]
-    branch = pl.program_id(0)
     item = pl.program_id(1)
-    runs = ends.shape[0]
-    me = place[0]
-    r2 = rate2[...]
-    mine = jnp.where(branch == 0, me, runs - 1 - me)
-    s_in = jnp.zeros((states, inner), F32)
-    lam_in = jnp.zeros((states, inner), F32)
-    for position in range(runs):
-        run = jnp.where(branch == 0, position, runs - 1 - position)
-        passing = jnp.exp2(twice(jnp.broadcast_to(totals[run], (8, inner))) * r2)
-        s_in = jnp.where(position < mine, passing * s_in + ends[run], s_in)
-    for position in reversed(range(runs)):
-        run = jnp.where(branch == 0, position, runs - 1 - position)
-        passing = jnp.exp2(twice(jnp.broadcast_to(totals[run], (8, inner))) * r2)
-        lam_in = jnp.where(position > mine, passing * lam_in + backs[run], lam_in)
-    enter[...] = s_in
-    carry[...] = lam_in
+    carry[...] = lam_in[...]
     act_low = act[...]
     act_f = act_low.astype(F32)
     dxs[...] = delta[...] * act_f
@@ -198,7 +290,7 @@
         ct = columns(proj, j, rank + states, states)
         r2 = rate2[...]
         rr = rate[...]
-        s = starts[j] + enter[...] * jnp.exp2(twice(jnp.broadcast_to(sums[j], (8, inner))) * r2)
+        s = starts[j] + s_in[...] * jnp.exp2(twice(jnp.broadcast_to(sums[j], (8, inner))) * r2)
         states_low[:states, :] = s.astype(BF16)
         for i in range(BLK):
             a = jnp.exp2(spread(drow, i) * r2)
@@ -264,16 +356,40 @@
     for k in range(tap_count):
         tap_grad[k : k + 1, :] += jnp.sum(d_conv * xf[first + k : first + k + toks, :], axis=0, keepdims=True)
         d_window = d_window + taps[k : k + 1, :] * pads[tap_count - 1 - k : tap_count - 1 - k + HALO + toks, :]
-    dxe_out[...] = d_window
+    rim_out[...] = d_window[HALO - 8 : HALO]
+    dx_out[...] = d_window[HALO:]
 
 
 def third_kernel(
-    tok, cot, mod, valid, hid, z_in, y, dxe, late, win, wout,
+    runs, tok, cot, mod, mask, counts, hid, z_in, y, dx, rims, win, wout,
     mixed, d_tokens, d_mod, out_grad, in_grad,
+    late_up, late_down, send_sem, recv_sem,
 ):
     dim = tok.shape[-1]
     toks, inner = z_in.shape
+    me = lax.axis_index("seq")
+    i = pl.program_id(0)
+    ups = [(rims.at[1], late_up, send_sem.at[0], recv_sem.at[0])]
+    downs = [(rims.at[0], late_down, send_sem.at[1], recv_sem.at[1])]
+
+    @pl.when(i == 0)
+    def _():
+        greet_line(me, runs)
+        swap_along_line(me, runs, ups, downs, True)
+
+        @pl.when(me == 0)
+        def _():
+            late_up[...] = jnp.zeros(late_up.shape, F32)
+
+        @pl.when(me == runs - 1)
+        def _():
+            late_down[...] = jnp.zeros(late_down.shape, F32)
+
+        out_grad[...] = jnp.zeros(out_grad.shape, F32)
+        in_grad[...] = jnp.zeros(in_grad.shape, F32)
+
     shift, scale, gate = mod[:, :dim], mod[:, dim : 2 * dim], mod[:, 2 * dim :]
+    valid = as_column(mask[pl.ds(i, 1), :]) * (counts[...] > i).astype(F32)
     tok_f = tok[...].astype(F32)
     normed, inv_std = normalise(tok_f)
     cot_f = cot[...].astype(F32)
@@ -286,31 +402,328 @@
     d_branch = (cot_f * gate).astype(BF16)
     d_gated = dot_nt(d_branch, wout[...])
     d_zgate = d_gated * summed * z_sig * (1.0 + z * (1.0 - z_sig))
-    edge = late.shape[1]
+    out_grad[...] += dot_tn(gated, d_branch)
+
+    @pl.when(i == 0)
+    def _():
+        swap_along_line(me, runs, ups, downs, False)
+
+    edge = late_up.shape[1]
 
     def with_late(part, extra):
         return jnp.concatenate([part[: toks - edge], part[toks - edge :] + extra], axis=0)
 
-    d_x = with_late(dxe[0, HALO:, :], late[0]) + flip_full(with_late(dxe[1, HALO:, :], late[1]))
-    d_xz = (jnp.concatenate([d_x, d_zgate], axis=1) * valid[...]).astype(BF16)
+    d_x = with_late(dx[0], late_down[i]) + flip_full(with_late(dx[1], late_up[i]))
+    d_xz = (jnp.concatenate([d_x, d_zgate], axis=1) * valid).astype(BF16)
     d_hidden = dot_nt(d_xz, win[...])
-
-    @pl.when(pl.program_id(0) == 0)
-    def _():
-        out_grad[...] = jnp.zeros(out_grad.shape, F32)
-        in_grad[...] = jnp.zeros(in_grad.shape, F32)
-
-    out_grad[...] += dot_tn(gated, d_branch)
     in_grad[...] += dot_tn(hid[...], d_xz)
-    d_mod[:, :dim] = jnp.sum(d_hidden, axis=0, keepdims=True)
-    d_mod[:, dim : 2 * dim] = jnp.sum(d_hidden * normed, axis=0, keepdims=True)
-    d_mod[:, 2 * dim :] = jnp.sum(cot_f * branch_out, axis=0, keepdims=True)
+    d_mod[0:1, :] = jnp.sum(d_hidden, axis=0, keepdims=True)
+    d_mod[1:2, :] = jnp.sum(d_hidden * normed, axis=0, keepdims=True)
+    d_mod[2:3, :] = jnp.sum(cot_f * branch_out, axis=0, keepdims=True)
     d_normed = d_hidden * (1.0 + scale)
     d_tokens[...] = cot_f + inv_std * (
         d_normed
         - jnp.mean(d_normed, axis=-1, keepdims=True)
         - normed * jnp.mean(d_normed * normed, axis=-1, keepdims=True)
     )
+
+
+def bit_of(index, bit):
+    return (index // (1 << bit)) % 2
+
+
+def across(axis, bit):
+    me = lax.axis_index(axis)
+    mine = bit_of(me, bit)
+    return mine, {axis: me + (1 - 2 * mine) * (1 << bit)}
+
+
+def exchange_kernel(runs, end, back, total, rate2, s_in, lam_in, group, span, pre, pre_span, sends, arrivals, send_sem, recv_sem):
+    slots, _, states, inner = end.shape
+    bits = int(math.log2(runs))
+    links = [across("seq", bit) for bit in range(bits)]
+    greet([target for _, target in links])
+    flows = (((end, 0), (back, 1)), ((end, 1), (back, 0)))
+    units = 2 * slots
+    rows = units * states
+    pre[...] = jnp.zeros(pre.shape, F32)
+    pre_span[...] = jnp.zeros(pre_span.shape, F32)
+    for flow in range(2):
+        for kind, (array, branch) in enumerate(flows[flow]):
+            for i in range(slots):
+                group[flow, kind * slots + i] = array[i, branch]
+                span[flow, kind * slots + i] = jnp.broadcast_to(total[i, branch], (8, inner))
+
+    def load(flow, slot):
+        for unit in range(units):
+            sends[slot, unit * states : (unit + 1) * states, :] = group[flow, unit].astype(BF16)
+            high = span[flow, unit].astype(BF16)
+            low = (span[flow, unit] - high.astype(F32)).astype(BF16)
+            at = rows + unit * 16
+            sends[slot, at : at + 16, :] = jnp.concatenate([high.astype(F32), low.astype(F32)], axis=0).astype(BF16)
+
+    def join(flow, slot, earlier, last):
+        for unit in range(units):
+            rate = rate2[flows[flow][unit // slots][1]]
+            state = arrivals[slot, unit * states : (unit + 1) * states, :].astype(F32)
+            at = rows + unit * 16
+            both = arrivals[slot, at : at + 16, :].astype(F32)
+            length = both[:8] + both[8:]
+            mine, mine_span = pre[flow, unit], pre_span[flow, unit]
+            joined = state * jnp.exp2(rate * twice(mine_span)) + mine
+            pre[flow, unit] = jnp.where(earlier, joined, mine)
+            pre_span[flow, unit] = jnp.where(earlier, length + mine_span, mine_span)
+            if not last:
+                own, own_span = group[flow, unit], span[flow, unit]
+                first = jnp.where(earlier, state, own)
+                second = jnp.where(earlier, own, state)
+                second_span = jnp.where(earlier, own_span, length)
+                group[flow, unit] = first * jnp.exp2(rate * twice(second_span)) + second
+                span[flow, unit] = own_span + length
+
+    for stage, (mine, target) in enumerate(links):
+        last = stage == bits - 1
+        if last:
+            slot = 2 * stage
+
+            @pl.when(mine == 0)
+            def _():
+                load(0, slot)
+
+            @pl.when(mine == 1)
+            def _():
+                load(1, slot)
+
+            copies = [remote(sends.at[slot], arrivals.at[slot], send_sem.at[slot], recv_sem.at[slot], target)]
+        else:
+            copies = []
+            for flow in range(2):
+                slot = 2 * stage + flow
+                load(flow, slot)
+                copies.append(
+                    remote(sends.at[slot], arrivals.at[slot], send_sem.at[slot], recv_sem.at[slot], target)
+                )
+        for copy in copies:
+            copy.start()
+        for copy in copies:
+            copy.wait()
+        if last:
+
+            @pl.when(mine == 1)
+            def _():
+                join(0, 2 * stage, True, True)
+
+            @pl.when(mine == 0)
+            def _():
+                join(1, 2 * stage, True, True)
+        else:
+            join(0, 2 * stage, mine == 1, False)
+            join(1, 2 * stage + 1, mine == 0, False)
+    for flow in range(2):
+        for kind, (_, branch) in enumerate(flows[flow]):
+            result = (s_in, lam_in)[kind]
+            for i in range(slots):
+                result[i, branch] = pre[flow, kind * slots + i]
+
+
+PARTS = 3
+LAST_ROWS = 16
+
+
+def reduce_rows(dim, inner, small):
+    rows = 3 * dim + small
+    unit = PARTS * LAST_ROWS * 32
+    return -(-rows // unit) * unit
+
+
+def reduce_kernel(
+    plan, in_grad, out_grad, xp_grad, dtp_grad, rate_grad, tap_grad, tapb_grad, skip_grad, dtb_grad, d_mod, step,
+    result, factors,
+    acc, sends, arrivals, gathered, mod_sum, mod_in, table, send_sem, recv_sem, small_send, small_recv,
+):
+    runs, groups, total_rows = plan
+    dim = in_grad.shape[0]
+    inner = out_grad.shape[0]
+    slots = step.shape[0]
+    seq_bits = [("seq", bit) for bit in range(int(math.log2(runs)))]
+    dp_bits = [("dp", bit) for bit in range(int(math.log2(groups)))]
+    all_bits = seq_bits + dp_bits
+    links = {key: across(*key) for key in all_bits}
+    greet([links[key][1] for key in all_bits])
+    middle = all_bits[1:-1]
+    orders = [
+        all_bits[:1] + middle[part % max(len(middle), 1) :] + middle[: part % max(len(middle), 1)] + all_bits[1:][-1:]
+        for part in range(PARTS)
+    ]
+    part_rows = total_rows // PARTS
+
+    mod_sum[...] = jnp.zeros(mod_sum.shape, F32)
+    for i in range(slots):
+        mod_sum[3 * i : 3 * i + 3, :] = d_mod[i]
+
+    def small_copy(stage):
+        axis, bit = all_bits[stage]
+        target = links[(axis, bit)][1]
+        if axis == "seq":
+            return remote(mod_sum, mod_in.at[stage], small_send.at[stage], small_recv.at[stage], target)
+        size = 16 << bit
+        at = pl.multiple_of(lax.axis_index("dp") // (1 << bit) * size, 16)
+        here = table.at[pl.ds(at, size), :]
+        return remote(here, here, small_send.at[stage], small_recv.at[stage], target)
+
+    def fill_table():
+        time_f = step[...].astype(F32)
+        time_low = time_f * jax.nn.sigmoid(time_f)
+        at = pl.multiple_of(lax.axis_index("dp") * 16, 16)
+        own = jnp.concatenate([mod_sum[: 3 * slots, :], time_low, mod_sum[4 * slots :, :]], axis=0)
+        table[pl.ds(at, 16), :] = own.astype(BF16)
+
+    half = dim
+    acc[0:dim, :] = in_grad[:, :inner]
+    acc[dim : 2 * dim, :] = in_grad[:, inner:]
+    acc[2 * dim : 3 * dim, :] = jnp.concatenate([out_grad[:half, :], out_grad[half:, :]], axis=1)
+    at = 3 * dim
+    for ref in (xp_grad, dtp_grad, rate_grad, tap_grad):
+        for branch in range(2):
+            size = ref.shape[1]
+            acc[at : at + size, :] = ref[branch]
+            at += size
+    tail = [ref[branch] for ref in (tapb_grad, skip_grad, dtb_grad) for branch in range(2)]
+    acc[at : at + 8, :] = jnp.concatenate(tail + [jnp.zeros((2, inner), F32)], axis=0)
+    at += 8
+    acc[at:, :] = jnp.zeros((total_rows - at, inner), F32)
+
+    starts = [part * part_rows for part in range(PARTS)]
+    sizes = [part_rows] * PARTS
+    history = [[] for _ in range(PARTS)]
+    offsets = [part * part_rows for part in range(PARTS)]
+    count = len(all_bits)
+    for stage in range(count):
+        copies = []
+        for part in range(PARTS):
+            mine, target = links[orders[part][stage]]
+            start, size = starts[part], sizes[part]
+            split = size >= 2 * LAST_ROWS
+            moved = size // 2 if split else size
+            if split:
+                away = pl.multiple_of(start + (1 - mine) * moved, LAST_ROWS)
+                keep = pl.multiple_of(start + mine * moved, LAST_ROWS)
+            else:
+                away = keep = start
+            history[part].append((start, size, split))
+            at = offsets[part]
+            offsets[part] += moved
+            here = sends.at[pl.ds(at, moved), :]
+            sends[at : at + moved, :] = acc[pl.ds(away, moved), :].astype(BF16)
+            copy = remote(
+                here, arrivals.at[pl.ds(at, moved), :], send_sem.at[part, stage], recv_sem.at[part, stage], target
+            )
+            copy.start()
+            copies.append((copy, part, keep, moved, at, split))
+            starts[part], sizes[part] = keep, moved
+        if stage == len(seq_bits):
+            fill_table()
+        small = small_copy(stage)
+        small.start()
+        for copy, part, keep, moved, at, split in copies:
+            copy.wait()
+            held = acc[pl.ds(keep, moved), :]
+            if not split:
+                held = held.astype(BF16).astype(F32)
+            acc[pl.ds(keep, moved), :] = held + arrivals[at : at + moved, :].astype(F32)
+        small.wait()
+        if all_bits[stage][0] == "seq":
+            mod_sum[...] += mod_in[stage]
+    if not dp_bits:
+        fill_table()
+    factors[...] = table[...]
+    for part in range(PARTS):
+        where = pl.ds(starts[part], sizes[part])
+        gathered[where, :] = acc[where, :].astype(BF16)
+    for stage in reversed(range(count)):
+        copies = []
+        for part in range(PARTS):
+            start, size, split = history[part][stage]
+            if not split:
+                continue
+            target = links[orders[part][stage]][1]
+            here = gathered.at[pl.ds(starts[part], sizes[part]), :]
+            copy = remote(
+                here, here, send_sem.at[part, count + stage], recv_sem.at[part, count + stage], target
+            )
+            copy.start()
+            copies.append(copy)
+            starts[part], sizes[part] = start, size
+        for copy in copies:
+            copy.wait()
+    result[...] = gathered[...]
+
+
+def finish_kernel(
+    ranks, result, factors, own, step, ada,
+    grad_time, grad_ada, grad_ada_bias, in_grad, tap_grad, tapb_grad, xp_grad, dtp_grad, dtb_grad, rate_grad, skip_grad, out_grad,
+):
+    rank, wide_rank = ranks
+    dim = in_grad.shape[0]
+    inner = out_grad.shape[0]
+    slots = step.shape[0]
+    states = rate_grad.shape[1]
+    taps = tap_grad.shape[1]
+
+    def rows(at, size):
+        return result[at : at + size, :].astype(F32)
+
+    in_grad[:, :inner] = rows(0, dim)
+    in_grad[:, inner:] = rows(dim, dim)
+    both = rows(2 * dim, dim)
+    out_grad[:dim, :] = both[:, :dim]
+    out_grad[dim:, :] = both[:, dim:]
+    at = 3 * dim
+    wide = wide_rank + 2 * states
+    for branch in range(2):
+        part = rows(at, wide)
+        part = jnp.concatenate([part[:rank], part[wide_rank:], part[rank:wide_rank]], axis=0)
+        part = jnp.concatenate([part, jnp.zeros((128 - wide, inner), F32)], axis=0)
+        xp_grad[branch] = part.T[:, : rank + 2 * states]
+        at += wide
+    for branch in range(2):
+        dtp_grad[branch] = rows(at, wide_rank)[:rank]
+        at += wide_rank
+    for branch in range(2):
+        rate_grad[branch] = rows(at, states)
+        at += states
+    tail = rows(at, 16)
+    for branch in range(2):
+        tap_grad[branch] = tail[branch * taps : (branch + 1) * taps]
+    tapb_grad[...] = tail[2 * taps : 2 * taps + 2]
+    skip_grad[...] = tail[2 * taps + 2 : 2 * taps + 4]
+    dtb_grad[...] = tail[2 * taps + 4 : 2 * taps + 6]
+
+    table = factors[...]
+    length = table.shape[0]
+    groups = length // 16
+    items = groups * 8
+
+    def pick(place):
+        row = lax.broadcasted_iota(jnp.int32, (items, length), 0)
+        col = lax.broadcasted_iota(jnp.int32, (items, length), 1)
+        slot = row % 8
+        wanted = row // 8 * 16 + place(slot)
+        return dot(((col == wanted) & (slot < slots)).astype(BF16), table)
+
+    times = pick(lambda slot: 3 * slots + slot).astype(BF16)
+    time_f = step[...].astype(F32)
+    time_sig = jax.nn.sigmoid(time_f)
+    d_time = jnp.zeros((slots, dim), F32)
+    mine = own[...].astype(F32)
+    for part in range(3):
+        mods = pick(lambda slot: 3 * slot + part)
+        lanes = slice(part * dim, (part + 1) * dim)
+        grad_ada[:, lanes] = dot_tn(times, mods.astype(BF16))
+        grad_ada_bias[:, lanes] = jnp.sum(mods, axis=0, keepdims=True)
+        picked = jnp.concatenate([mine[3 * i + part : 3 * i + part + 1] for i in range(slots)], axis=0)
+        d_time = d_time + dot_nt(picked.astype(BF16), ada[:, lanes])
+    grad_time[...] = d_time * time_sig * (1.0 + time_f * (1.0 - time_sig))
 
 
 def params(**more):
@@ -334,20 +747,9 @@
     proj_rows = wide_rank + 2 * states
     blocks = toks // BLK
     runs = lax.axis_size("seq")
-    place = lax.axis_index("seq")
-    live = (jnp.arange(slots) < counts[0]).astype(F32)
-    valid = (token_mask.astype(F32) * live[:, None])[:, :, None]
-    time_f = timestep.astype(F32)
-    time_sig = jax.nn.sigmoid(time_f)
-    time_low = (time_f * time_sig).astype(BF16)
-    modulate = (dot(time_low, ada_weight) + ada_bias)[:, None, :]
-
-    rim = jnp.concatenate([tokens, jnp.broadcast_to(valid, (slots, toks, 128)).astype(BF16)], axis=2)
-    up = [(i, i + 1) for i in range(runs - 1)]
-    down = [(i + 1, i) for i in range(runs - 1)]
-    from_prev = lax.ppermute(rim[:, toks - HALO :], "seq", up)
-    from_next = lax.ppermute(rim[:, :HALO], "seq", down)
-
+    groups = lax.axis_size("dp")
+    counts2 = counts[:, None]
+    step3 = timestep[:, None, :]
     xwt = jnp.swapaxes(x_weight, 1, 2)
     xwt = jnp.concatenate(
         [xwt[:, :rank], jnp.zeros((2, wide_rank - rank, inner), BF16), xwt[:, rank:]], axis=1
@@ -364,23 +766,32 @@
     def whole(*block):
         return spec(block, lambda *_: (0,) * len(block))
 
-    xe, dy, z_gate, hid = pl.pallas_call(
-        enter_kernel,
+    xe, dy, z_gate, hid, modulate = pl.pallas_call(
+        functools.partial(enter_kernel, runs),
         grid=(slots,),
         in_specs=[
-            item(toks, dim), item(HALO, dim + 128), item(HALO, dim + 128), item(toks, dim), item(1, 3 * dim), item(toks, 1),
-            whole(dim, 2 * inner), whole(inner, dim),
-        ],
-        out_specs=[item(2, HALO + toks, inner), item(2, toks, inner), item(toks, inner), item(toks, dim)],
+            whole(slots, toks, dim), item(toks, dim), whole(slots, toks), whole(1, 1), item(1, dim), whole(dim, 3 * dim),
+            whole(1, 3 * dim), whole(dim, 2 * inner), whole(inner, dim),
+        ],
+        out_specs=[
+            item(2, HALO + toks, inner), item(2, toks, inner), item(toks, inner), item(toks, dim), item(1, 3 * dim),
+        ],
         out_shape=[
             jax.ShapeDtypeStruct((slots, 2, HALO + toks, inner), BF16),
             jax.ShapeDtypeStruct((slots, 2, toks, inner), F32),
             jax.ShapeDtypeStruct((slots, toks, inner), F32),
             jax.ShapeDtypeStruct((slots, toks, dim), BF16),
-        ],
-        compiler_params=params(),
+            jax.ShapeDtypeStruct((slots, 1, 3 * dim), F32),
+        ],
+        scratch_shapes=[
+            pltpu.VMEM((slots, HALO, dim), BF16), pltpu.VMEM((slots, HALO, dim), BF16), pltpu.VMEM((slots, toks), jnp.int32),
+            pltpu.VMEM((slots, toks), jnp.int32), pltpu.SemaphoreType.DMA((4,)), pltpu.SemaphoreType.DMA((4,)),
+        ],
+        compiler_params=params(collective_id=1, has_side_effects=True),
         name="enter",
-    )(tokens, from_prev, from_next, cotangent, modulate, valid, input_weight, output_weight)
+    )(
+        tokens, cotangent, token_mask, counts2, step3, ada_weight, ada_bias[None, :], input_weight, output_weight,
+    )
 
     def unit(*block):
         return spec((None, None) + block, lambda b, i: (i, b) + (0,) * len(block))
@@ -416,33 +827,47 @@
         name="first",
     )(xe, dy, conv_weight, vec(conv_bias), xwt, dtw, vec(dt_bias), rate2)
 
-    ends, backs, totals = (lax.all_gather(a, "seq") for a in (end, back, total))
-
-    def gathered(*block):
-        return spec((runs, None, None) + block, lambda b, i: (0, i, b) + (0,) * len(block))
-
-    y, dxe, rate_grad, skip_grad, dtb_grad, dtp_grad, xp_grad, tap_grad, tapb_grad = pl.pallas_call(
+    pairs = int(math.log2(runs))
+    units = 2 * slots
+    vmem = pl.BlockSpec(memory_space=pltpu.VMEM)
+    s_in, lam_in = pl.pallas_call(
+        functools.partial(exchange_kernel, runs),
+        in_specs=[vmem] * 4,
+        out_specs=[vmem] * 2,
+        out_shape=[unit_shape(states, inner), unit_shape(states, inner)],
+        scratch_shapes=[
+            pltpu.VMEM((2, units, states, inner), F32), pltpu.VMEM((2, units, 8, inner), F32),
+            pltpu.VMEM((2, units, states, inner), F32), pltpu.VMEM((2, units, 8, inner), F32),
+            pltpu.VMEM((2 * pairs, units * (states + 16), inner), BF16),
+            pltpu.VMEM((2 * pairs, units * (states + 16), inner), BF16),
+            pltpu.SemaphoreType.DMA((2 * pairs,)), pltpu.SemaphoreType.DMA((2 * pairs,)),
+        ],
+        compiler_params=params(collective_id=2, has_side_effects=True),
+        name="exchange",
+    )(end, back, total, rate2)
+
+    rim_spec = spec((None, None, 8, inner), lambda b, i: (b, i, 0, 0))
+    y, dx, rims, rate_grad, skip_grad, dtb_grad, dtp_grad, xp_grad, tap_grad, tapb_grad = pl.pallas_call(
         second_kernel,
         grid=(2, slots),
         in_specs=[
-            pl.BlockSpec(memory_space=pltpu.SMEM),
-            gathered(states, inner), gathered(states, inner), gathered(1, inner), unit(blocks, states, inner),
+            unit(states, inner), unit(states, inner), unit(blocks, states, inner),
             unit(blocks, 1, inner), branch(states, inner), branch(states, inner), unit(HALO + toks, inner), unit(toks, inner),
             unit(toks, inner), unit(toks, inner), unit(toks, inner), unit(toks, inner), unit(proj_rows, toks),
             branch(proj_rows, inner), branch(inner, BLK * states), branch(inner, BLK * states), branch(wide_rank, inner),
             branch(tap_count, inner), branch(1, inner),
         ],
         out_specs=[
-            unit(toks, inner), unit(HALO + toks, inner), branch(states, inner), branch(1, inner), branch(1, inner),
+            unit(toks, inner), unit(toks, inner), rim_spec, branch(states, inner), branch(1, inner), branch(1, inner),
             branch(wide_rank, inner), branch(proj_rows, inner), branch(tap_count, inner), branch(1, inner),
         ],
         out_shape=[
-            unit_shape(toks, inner), unit_shape(HALO + toks, inner),
+            unit_shape(toks, inner), unit_shape(toks, inner), jax.ShapeDtypeStruct((2, slots, 8, inner), F32),
         ] + [
             jax.ShapeDtypeStruct((2, rows, inner), F32) for rows in (states, 1, 1, wide_rank, proj_rows, tap_count, 1)
         ],
         scratch_shapes=[
-            pltpu.VMEM((states, inner), F32), pltpu.VMEM((states, inner), F32), pltpu.VMEM((toks, inner), F32),
+            pltpu.VMEM((states, inner), F32), pltpu.VMEM((toks, inner), F32),
             pltpu.VMEM((toks, BLK * states), BF16), pltpu.VMEM((toks, BLK * states), BF16),
             pltpu.VMEM((BLK, inner), F32), pltpu.VMEM((BLK, inner), F32), pltpu.VMEM((BLK, inner), F32),
             pltpu.VMEM((BLK, states, inner), F32), pltpu.VMEM(((BLK + 1) * states, inner), BF16),
@@ -454,49 +879,77 @@
         compiler_params=params(),
         name="second",
     )(
-        jnp.reshape(place, (1,)).astype(jnp.int32), ends, backs, totals, starts, sums, rate2, decay_rate, xe, act, dsilu, delta,
+        s_in, lam_in, starts, sums, rate2, decay_rate, xe, act, dsilu, delta,
         sig, dy, proj, xwt, bwide, cwide, dtw, conv_weight, vec(skip_gain),
     )
 
-    late = jnp.stack(
-        [
-            lax.ppermute(dxe[:, 0, HALO - 8 : HALO], "seq", down),
-            lax.ppermute(dxe[:, 1, HALO - 8 : HALO], "seq", up),
-        ],
-        axis=1,
-    )
-
     mixed, d_tokens, d_mod, out_grad, in_grad = pl.pallas_call(
-        third_kernel,
+        functools.partial(third_kernel, runs),
         grid=(slots,),
         in_specs=[
-            item(toks, dim), item(toks, dim), item(1, 3 * dim), item(toks, 1), item(toks, dim), item(toks, inner),
-            item(2, toks, inner), item(2, HALO + toks, inner), item(2, 8, inner), whole(dim, 2 * inner), whole(inner, dim),
-        ],
-        out_specs=[item(toks, dim), item(toks, dim), item(1, 3 * dim), whole(inner, dim), whole(dim, 2 * inner)],
+            item(toks, dim), item(toks, dim), item(1, 3 * dim), whole(slots, toks), whole(1, 1), item(toks, dim),
+            item(toks, inner), item(2, toks, inner), item(2, toks, inner), whole(2, slots, 8, inner), whole(dim, 2 * inner),
+            whole(inner, dim),
+        ],
+        out_specs=[item(toks, dim), item(toks, dim), item(3, dim), whole(inner, dim), whole(dim, 2 * inner)],
         out_shape=[
             jax.ShapeDtypeStruct((slots, toks, dim), BF16), jax.ShapeDtypeStruct((slots, toks, dim), F32),
-            jax.ShapeDtypeStruct((slots, 1, 3 * dim), F32), jax.ShapeDtypeStruct((inner, dim), F32),
+            jax.ShapeDtypeStruct((slots, 3, dim), F32), jax.ShapeDtypeStruct((inner, dim), F32),
             jax.ShapeDtypeStruct((dim, 2 * inner), F32),
         ],
+        scratch_shapes=[
+            pltpu.VMEM((slots, 8, inner), F32), pltpu.VMEM((slots, 8, inner), F32), pltpu.SemaphoreType.DMA((2,)),
+            pltpu.SemaphoreType.DMA((2,)),
+        ],
+        compiler_params=params(collective_id=3, has_side_effects=True),
+        name="third",
+    )(
+        tokens, cotangent, modulate, token_mask, counts2, hid, z_gate, y, dx, rims, input_weight, output_weight,
+    )
+
+    small = 2 * (proj_rows + wide_rank + states + tap_count) + 8
+    rows = reduce_rows(dim, inner, small)
+    stages = int(math.log2(runs)) + int(math.log2(groups))
+    result, factors = pl.pallas_call(
+        functools.partial(reduce_kernel, (runs, groups, rows)),
+        in_specs=[vmem] * 11,
+        out_specs=[vmem] * 2,
+        out_shape=[jax.ShapeDtypeStruct((rows, inner), BF16), jax.ShapeDtypeStruct((16 * groups, dim), BF16)],
+        scratch_shapes=[
+            pltpu.VMEM((rows, inner), F32), pltpu.VMEM((rows + PARTS * LAST_ROWS * stages, inner), BF16),
+            pltpu.VMEM((rows + PARTS * LAST_ROWS * stages, inner), BF16),
+            pltpu.VMEM((rows, inner), BF16), pltpu.VMEM((16, dim), F32),
+            pltpu.VMEM((max(int(math.log2(runs)), 1), 16, dim), F32), pltpu.VMEM((16 * groups, dim), BF16),
+            pltpu.SemaphoreType.DMA((PARTS, 2 * stages)), pltpu.SemaphoreType.DMA((PARTS, 2 * stages)),
+            pltpu.SemaphoreType.DMA((stages,)), pltpu.SemaphoreType.DMA((stages,)),
+        ],
+        compiler_params=params(collective_id=4, has_side_effects=True),
+        name="reduce",
+    )(
+        in_grad, out_grad, xp_grad, dtp_grad, rate_grad, tap_grad, tapb_grad, skip_grad, dtb_grad, d_mod, timestep,
+    )
+
+    own = lax.dynamic_slice_in_dim(factors, lax.axis_index("dp") * 16, 16, 0)
+    (
+        d_time, grad_ada, grad_ada_bias, in_grad, tap_grad, tapb_grad, xp_grad, dtp_grad, dtb_grad, rate_grad, skip_grad,
+        out_grad,
+    ) = pl.pallas_call(
+        functools.partial(finish_kernel, (rank, wide_rank)),
+        in_specs=[vmem] * 5,
+        out_specs=[vmem] * 12,
+        out_shape=[
+            jax.ShapeDtypeStruct(shape, F32)
+            for shape in (
+                (slots, dim), (dim, 3 * dim), (1, 3 * dim), (dim, 2 * inner), (2, tap_count, inner), (2, inner),
+                (2, inner, rank + 2 * states), (2, rank, inner), (2, inner), (2, states, inner), (2, inner), (inner, dim),
+            )
+        ],
         compiler_params=params(),
-        name="third",
-    )(tokens, cotangent, modulate, valid, hid, z_gate, y, dxe, late, input_weight, output_weight)
-
-    d_mod_low = lax.psum(d_mod[:, 0], "seq").astype(BF16)
-    d_time = dot_nt(d_mod_low, ada_weight) * time_sig * (1.0 + time_f * (1.0 - time_sig))
-    factors = lax.all_gather(jnp.concatenate([time_low, d_mod_low], axis=1), "dp", tiled=True)
-    all_time, all_mod = factors[:, :dim], factors[:, dim:]
-    grad_ada = dot_tn(all_time, all_mod)
-    grad_ada_bias = jnp.sum(all_mod.astype(F32), axis=0)
-    summed = lax.psum(
-        (in_grad, out_grad, rate_grad, skip_grad, dtb_grad, dtp_grad, xp_grad, tap_grad, tapb_grad), ("dp", "seq")
-    )
-    in_grad, out_grad, rate_grad, skip_grad, dtb_grad, dtp_grad, xp_grad, tap_grad, tapb_grad = summed
-    xp_grad = jnp.swapaxes(jnp.concatenate([xp_grad[:, :rank], xp_grad[:, wide_rank:]], axis=1), 1, 2)
+        name="finish",
+    )(result, factors, own, timestep, ada_weight)
     return (
-        mixed, d_tokens, d_time, grad_ada, grad_ada_bias, in_grad, tap_grad, tapb_grad[:, 0], xp_grad, dtp_grad[:, :rank],
-        dtb_grad[:, 0], rate_grad, skip_grad[:, 0], out_grad,
+        mixed, d_tokens, d_time, grad_ada, grad_ada_bias[0], in_grad, tap_grad, tapb_grad, xp_grad, dtp_grad, dtb_grad,
+        rate_grad, skip_grad, out_grad,
     )
 
 

time: 406 us -> 265 us (0.65)
  blocking collectives: 92.8 us -> 0 us
  waiting for transfers between devices: 90.1 us -> 0 us
  Pallas kernels: 172 us -> 248 us
  between operations: 14.8 us -> 1.48 us
  local copies, waits for them, and re-layouts: 20.6 us -> 12.9 us
  starting transfers between devices: 7.2 us -> 0 us
    pallas_call x3 -> x6, Pallas kernels: 126 us -> 202 us  [the longest x1 103 us: per_device(): pl.pallas_call(second_kernel, grid=(2, slots), in_specs=[unit(states, inn...]
    psum x1 -> x0, waiting for transfers between devices: 59 us -> none  [per_device(): lax.psum((in_grad, out_grad, rate_grad, skip_grad, dtb_grad, dtp_grad, xp...]
    psum x2 -> x0, blocking collectives: 54.1 us -> none  [the longest x1 43.3 us: per_device(): lax.psum((in_grad, out_grad, rate_grad, skip_grad, dtb_grad, dtp_grad, xp...]
    all_gather x2 -> x0, blocking collectives: 38.6 us -> none  [the longest x1 30.6 us: per_device(): lax.all_gather(jnp.concatenate([time_low, d_mod_low], axis=1), 'dp', tile...]
    all_gather x2 -> x0, waiting for transfers between devices: 28.5 us -> none  [per_device(): ends, backs, totals = (lax.all_gather(a, 'seq') for a in (end, back, total))]
    ppermute x4 -> x0, starting transfers between devices: 7.08 us -> none  [the longest x1 2.36 us: per_device(): from_prev = lax.ppermute(rim[:, toks - HALO:], 'seq', up)]
  transfers between devices with their start and end apart: 7 -> 0, of which waited for: 4 -> 0; matrix products, arithmetic and copies ran while one was open for 4% -> 0% of each run, Pallas kernels for 0% -> 0%
where the time goes in v1:
time: 265 us
  Pallas kernels  248 us (94%)
  local copies, waits for them, and re-layouts  12.9 us (5%)
  other arithmetic  2.73 us (1%)
    pallas_call x1, Pallas kernels, per_device(): pl.pallas_call(second_kernel, grid=(2, slots), in_specs=[unit(states, inn...  103 us
    pallas_call x1, Pallas kernels, per_device(): pl.pallas_call(functools.partial(reduce_kernel, (runs, groups, rows)), in...  52.7 us
    pallas_call x1, Pallas kernels, per_device(): pl.pallas_call(first_kernel, grid=(2, slots), in_specs=[unit(HALO + toks,...  45.8 us
    pallas_call x1, Pallas kernels, per_device(): pl.pallas_call(functools.partial(exchange_kernel, runs), in_specs=[vmem]...  14.7 us
    pallas_call x1, Pallas kernels, per_device(): pl.pallas_call(functools.partial(third_kernel, runs), grid=(slots,), in_s...  13.9 us
    pallas_call x1, Pallas kernels, per_device(): pl.pallas_call(functools.partial(enter_kernel, runs), grid=(slots,), in_s...  11.9 us
    pallas_call x1, Pallas kernels, per_device(): pl.pallas_call(functools.partial(finish_kernel, (rank, wide_rank)), in_sp...  5.89 us

profile of v1, /device:TPU:0, one launch (start us, length us, event | category | flops | bytes accessed | tf_op | source)
XLA Modules:
  0.0 265.0 jit_solution(8492859518542965997)
XLA Ops:
  0.6 0.0 copy-start.5
  0.7 0.0 copy-start.2
  0.7 0.0 copy-start.4
  1.4 1.3 copy.33.step
  2.6 1.3 broadcast_in_dim.20.ada_bias
  3.9 0.0 copy-start.6
  3.9 0.0 copy-start.3
  3.9 11.9 %enter.1 = (bf16[3,2,272,768]{3,2,1,0:T(8,128)(2,1)}, f32[3,2,256,768]{3,2,1,0:T(8,128)}, f32[3,256,768]{2,1,0:T(8,128)}, bf16[3,256,384]{2,1,0:T(8,128)(2,1)}, f32[3,1,1152]{2,1,0:T(1,128)}) custom-call(bf16[3,256,384]{2,1,0:T(8,128)(2,1)} %tok.3, bf16[3,256,384]{2,1,0:T(8,128)(2,1)} %cot.3, s32[3,256]{1,0:T(4,128)} %mask.3, s32[1,1]{1,0:T(1,128)} %bitcast.5.counts, ...), custom_call_target="tpu_custom_call" | custom-call | tf_op jit(solution)/shard_map/enter/pallas_call | solution.py:769
  15.8 0.0 copy-done.5
  15.9 0.6 broadcast_in_dim.21.tap_bias
  16.5 0.0 copy-done.2
  16.5 0.1 pad.2.clone
  16.6 0.8 pad_maximum_fusion.xwt
  17.4 0.0 copy-done.4
  17.4 0.6 concatenate.7.dtw
  18.0 0.0 copy-done.6
  18.0 0.6 broadcast_in_dim.22.dt_bias
  18.6 0.0 copy-done.3
  18.6 0.6 broadcast_multiply_fusion.rate2
  19.3 45.8 %first.1 = (bf16[3,2,256,768]{3,2,1,0:T(8,128)(2,1)}, f32[3,2,256,768]{3,2,1,0:T(8,128)}, f32[3,2,256,768]{3,2,1,0:T(8,128)}, f32[3,2,256,768]{3,2,1,0:T(8,128)}...) custom-call(bf16[3,2,272,768]{3,2,1,0:T(8,128)(2,1)} %get-tuple-elem, ...), custom_call_target="tpu_custom_call" | custom-call | tf_op jit(solution)/shard_map/first/pallas_call | solution.py:805
  65.0 14.7 %exchange.1 = (f32[3,2,16,768]{3,2,1,0:T(8,128)}, f32[3,2,16,768]{3,2,1,0:T(8,128)}) custom-call(f32[3,2,16,768]{3,2,1,0:T(8,128)} %get-tuple-element.65.end, f32[3,2,16,768]{3,2,1,0:T(8,128)} %get-tuple-element.66.back, f32[3,2,1,768]{3,2,1,0:T(1,128)} %get-tuple-element.67.total, f32[2,16,768]{2,1,0:T(8,128)} %broadcast_multiply_fusion.rate2), custom_call_target="tpu_custom_call" | custom-call | tf_op jit(solution)/shard_map/exchange/pallas_call | solution.py:833
  79.7 0.0 copy-start.7
  79.7 0.1 tile.8
  79.8 1.2 copy.34.bwide
  80.9 0.1 tile.20
  81.0 1.2 copy.35.cwide
  82.1 0.0 copy-done.7
  82.1 0.6 broadcast_in_dim.23.skip
  82.7 103.2 %second.1 = (f32[3,2,256,768]{3,2,1,0:T(8,128)}, f32[3,2,256,768]{3,2,1,0:T(8,128)}, f32[2,3,8,768]{3,2,1,0:T(8,128)}, f32[2,16,768]{2,1,0:T(8,128)}, f32[2,1,76...) custom-call(f32[3,2,16,768]{3,2,1,0:T(8,128)} %get-tuple-element.68., ...), custom_call_target="tpu_custom_call" | custom-call | tf_op jit(solution)/shard_map/second/pallas_call | solution.py:850
  186.0 13.9 %third.1 = (bf16[3,256,384]{2,1,0:T(8,128)(2,1)}, f32[3,256,384]{2,1,0:T(8,128)}, f32[3,3,384]{2,1,0:T(4,128)}, f32[768,384]{1,0:T(8,128)}, f32[384,1536]{1,0:T(8,128)}) custom-call(bf16[3,256,384]{2,1,0:T(8,128)(2,1)} %tok.3, bf16[3,256,384]{2,1,0:T(8,128)(2,1)} %cot.3, f32[3,1,1152]{2,1,0:T(1,128)} %get-tuple-element.60.mod, s32[3,256]{1,0:T(4,128)} %mask.3, ...), custom_call_target="tpu_custom_call" | custom-call | tf_op jit(solution)/shard_map/third/pallas_call | solution.py:886
  199.8 52.7 %reduce.2 = (bf16[1536,768]{1,0:T(8,128)(2,1)}, bf16[128,384]{1,0:T(8,128)(2,1)}) custom-call(f32[384,1536]{1,0:T(8,128)} %get-tuple-element.82.in_grad, f32[768,384]{1,0:T(8,128)} %get-tuple-element.83.out_grad, f32[2,64,768]{2,1,0:T(8,128)} %get-tuple-element.84.xp_grad, f32[2,32,768]{2,1,0:T(8,128)} %get-tuple-element.85.dtp_grad, ...), custom_call_target="tpu_custom_call" | custom-call | tf_op jit(solution)/shard_map/reduce/pallas_call | solution.py:913
  252.5 0.0 copy-start.1
  252.5 1.4 constant_dynamic-slice_fusion.own
  253.9 0.0 copy-start
  253.9 5.9 %finish.1 = (f32[3,384]{1,0:T(4,128)}, f32[384,1152]{1,0:T(8,128)}, f32[1,1152]{1,0:T(1,128)}, f32[384,1536]{1,0:T(8,128)}, f32[2,4,768]{2,1,0:T(4,128)}, /*inde...) custom-call(bf16[1536,768]{1,0:T(8,128)(2,1)} %get-tuple-element.92., ...), custom_call_target="tpu_custom_call" | custom-call | tf_op jit(solution)/shard_map/finish/pallas_call | solution.py:936
  259.8 1.3 reduce.1
  261.1 2.1 copy.36
  263.2 0.0 copy-done.1
  263.2 0.8 copy.40
  264.0 0.0 copy-done
  264.0 1.0 copy.41
  (4 shorter events, 0.0 us)
Async XLA Ops:
  0.6 15.2 %copy-start.5 = (f32[2,768]{1,0:T(2,128)S(1)}, f32[2,768]{1,0:T(2,128)}, u32[]{:S(2)}) copy-start(f32[2,768]{1,0:T(2,128)} %param.24) | copy-start | bytes 18436
  0.7 15.8 %copy-start.2 = (bf16[2,768,56]{1,2,0:T(8,128)(2,1)S(1)}, bf16[2,768,56]{1,2,0:T(8,128)(2,1)}, u32[]{:S(2)}) copy-start(bf16[2,768,56]{1,2,0:T(8,128)(2,1)} %param.25) | copy-start | bytes 516100
  0.7 16.7 %copy-start.4 = (bf16[2,24,768]{2,1,0:T(8,128)(2,1)S(1)}, bf16[2,24,768]{2,1,0:T(8,128)(2,1)}, u32[]{:S(2)}) copy-start(bf16[2,24,768]{2,1,0:T(8,128)(2,1)} %param.26) | copy-start | bytes 221188
  3.9 14.1 %copy-start.6 = (f32[2,768]{1,0:T(2,128)S(1)}, f32[2,768]{1,0:T(2,128)}, u32[]{:S(2)}) copy-start(f32[2,768]{1,0:T(2,128)} %param.27) | copy-start | bytes 18436
  3.9 14.7 %copy-start.3 = (f32[2,16,768]{2,1,0:T(8,128)S(1)}, f32[2,16,768]{2,1,0:T(8,128)}, u32[]{:S(2)}) copy-start(f32[2,16,768]{2,1,0:T(8,128)} %rate.1) | copy-start | bytes 294916
  79.7 2.4 copy-start.7
  252.5 10.7 %copy-start.1 = (bf16[3,256,384]{2,1,0:T(8,128)(2,1)S(1)}, bf16[3,256,384]{2,1,0:T(8,128)(2,1)}, u32[]{:S(2)}) copy-start(bf16[3,256,384]{2,1,0:T(8,128)(2,1)} %get-tuple-element.150) | copy-start | bytes 1769476
  253.9 10.1 %copy-start = (f32[3,256,384]{2,1,0:T(8,128)S(1)}, f32[3,256,384]{2,1,0:T(8,128)}, u32[]{:S(2)}) copy-start(f32[3,256,384]{2,1,0:T(8,128)} %get-tuple-element.151) | copy-start | bytes 3538948

commit v2 on v1

--- a/solution.py
+++ b/solution.py
@@ -196,73 +196,86 @@
     return twice(ref[pl.ds(index, 8, stride=0), :])
 
 
-def columns(ref, block, first, count):
-    lane = pl.multiple_of((block // 8) * 128, 128)
-    return pltpu.roll(ref[first : first + count, pl.ds(lane, 128)], (128 - (block % 8) * BLK) % 128, 1)
+def lay_out(tiles, rows):
+    for t in range(rows.shape[1]):
+        tiles[t] = jnp.broadcast_to(rows[:, t : t + 1], (rows.shape[0], 128))
+
+
+def across_lanes(tile, inner):
+    return jnp.concatenate([tile] * (inner // 128), axis=1)
+
+
+def softplus_parts(pre):
+    e = jnp.exp2(-LOG2E * jnp.abs(pre))
+    more = jnp.where(e < 1e-3, e - 0.5 * e * e, jnp.log(1.0 + e))
+    return jnp.maximum(pre, 0.0) + more, jax.nn.sigmoid(pre)
 
 
 def first_kernel(
     xe, dy, taps, tap_bias, xwt, dtw, dt_bias, rate2,
-    act_out, dsilu_out, delta_out, sig_out, proj_out, end_out, back_out, total_out, starts_out, sums_out,
-    xf, dl, dx, drow, xrow, yrow, decay, through,
+    act_out, dsilu_out, delta_out, sig_out, proj_out, end_out, back_out, total_out, starts_out, sums_out, tiles,
+    dx, decay, through,
 ):
     toks, inner = dy.shape
     states = rate2.shape[0]
     blocks = toks // BLK
     rank = dtw.shape[0]
     tap_count = taps.shape[0]
-    xf[...] = xe[...].astype(F32)
-    conv = tap_bias[...] + jnp.zeros((toks, inner), F32)
-    for k in range(tap_count):
-        conv = conv + taps[k : k + 1, :] * xf[HALO - tap_count + 1 + k : HALO - tap_count + 1 + k + toks, :]
+    shifted = xe[...].astype(F32)
+    conv = tap_bias[...] + taps[tap_count - 1 : tap_count, :] * shifted[HALO:]
+    for k in reversed(range(tap_count - 1)):
+        shifted = pltpu.roll(shifted, 1, 0)
+        conv = conv + taps[k : k + 1, :] * shifted[HALO:]
     sig = jax.nn.sigmoid(conv)
-    act = (conv * sig).astype(BF16)
-    dsilu_out[...] = sig * (1.0 + conv * (1.0 - sig))
+    act_f = conv * sig
+    act = act_f.astype(BF16)
+    dsilu_out[...] = sig + act_f * (1.0 - sig)
     act_out[...] = act
     proj = dot_nt(xwt[...], act)
     proj_out[...] = proj
+    lay_out(tiles, proj[rank:, :])
     pre = dot_tn(proj[:rank, :].astype(BF16), dtw[...]) + dt_bias[...]
-    delta = jnp.maximum(pre, 0.0) + jnp.log1p(jnp.exp(-jnp.abs(pre)))
+    delta, slope = softplus_parts(pre)
     delta_out[...] = delta
-    sig_out[...] = jax.nn.sigmoid(pre)
-    dl[...] = delta
+    sig_out[...] = slope
     dx[...] = delta * act.astype(F32)
     end_out[...] = jnp.zeros((states, inner), F32)
     back_out[...] = jnp.zeros((states, inner), F32)
     through[...] = jnp.zeros((8, inner), F32)
 
-    def block_step(j, _):
+    def one_block(j, slot):
         t0 = pl.multiple_of(j * BLK, BLK)
-        drow[...] = dl[pl.ds(t0, BLK), :]
-        xrow[...] = dx[pl.ds(t0, BLK), :]
-        yrow[...] = dy[pl.ds(t0, BLK), :]
-        bt = columns(proj_out, j, rank, states)
-        ct = columns(proj_out, j, rank + states, states)
+        dr, xr, yr = (ref.at[pl.ds(t0, BLK), :] for ref in (delta_out, dx, dy))
+        tile = tiles.at[pl.ds(t0, BLK)]
         rate = rate2[...]
         s = end_out[...]
         starts_out[j] = s
         before = through[...]
         sums_out[j] = before[:1, :]
         for i in range(BLK):
-            a = jnp.exp2(spread(drow, i) * rate)
-            decay[i] = a
-            s = a * s + spread(xrow, i) * jnp.broadcast_to(bt[:, i : i + 1], (states, inner))
+            a = jnp.exp2(spread(dr, i) * rate)
+            decay[slot, i] = a
+            s = a * s + spread(xr, i) * across_lanes(tile[i, :states], inner)
         end_out[...] = s
         m = jnp.zeros((states, inner), F32)
         for i in reversed(range(BLK)):
-            m = decay[i] * (m + spread(yrow, i) * jnp.broadcast_to(ct[:, i : i + 1], (states, inner)))
+            m = decay[slot, i] * (m + spread(yr, i) * across_lanes(tile[i, states:], inner))
         back_out[...] = back_out[...] + m * jnp.exp2(twice(before) * rate)
-        through[...] = before + jnp.sum(drow[...], axis=0, keepdims=True)
+        through[...] = before + jnp.sum(dr[...], axis=0, keepdims=True)
+
+    def block_step(k, _):
+        one_block(2 * k, 0)
+        one_block(2 * k + 1, 1)
         return 0
 
-    lax.fori_loop(0, blocks, block_step, 0)
+    lax.fori_loop(0, blocks // 2, block_step, 0)
     total_out[...] = through[:1, :]
 
 
 def second_kernel(
-    s_in, lam_in, starts, sums, rate2, rate, xe, act, dsilu, delta, sig, dy, proj, xwt, bwide, cwide, dtw, taps, skip,
+    s_in, lam_in, starts, sums, tiles, rate2, rate, xe, act, dsilu, delta, sig, dy, proj, xwt, dtw, taps, skip,
     y_out, dx_out, rim_out, rate_grad, skip_grad, dtb_grad, dtp_grad, xp_grad, tap_grad, tapb_grad,
-    carry, dxs, bdiag, cdiag, drow, xrow, yrow, decay, states_low, lam_low, rq_low, racc, gsum, hsum, db, dc, pads, xf,
+    carry, dxs, bdiag, cdiag, decay, states_low, lam_low, rq_low, qd_low, dots, racc, gsum, hsum, db, dc,
 ):
     toks, inner = dy.shape
     states = rate2.shape[0]
@@ -270,92 +283,114 @@
     rank = dtw.shape[0]
     tap_count = taps.shape[0]
     item = pl.program_id(1)
-    carry[...] = lam_in[...]
-    act_low = act[...]
-    act_f = act_low.astype(F32)
-    dxs[...] = delta[...] * act_f
-    width = bwide.shape[1]
-    own = lax.broadcasted_iota(jnp.int32, (toks, width), 0) % BLK == lax.broadcasted_iota(jnp.int32, (toks, width), 1) // states
-    bdiag[...] = jnp.where(own, dot(act_low, bwide[...]), 0.0).astype(BF16)
-    cdiag[...] = jnp.where(own, dot(act_low, cwide[...]), 0.0).astype(BF16)
-    racc[...] = jnp.zeros((states, inner), F32)
-
-    def block_step(step, _):
-        j = blocks - 1 - step
-        t0 = pl.multiple_of(j * BLK, BLK)
-        drow[...] = delta[pl.ds(t0, BLK), :]
-        xrow[...] = dxs[pl.ds(t0, BLK), :]
-        yrow[...] = dy[pl.ds(t0, BLK), :]
-        bt = columns(proj, j, rank, states)
-        ct = columns(proj, j, rank + states, states)
-        r2 = rate2[...]
-        rr = rate[...]
-        s = starts[j] + s_in[...] * jnp.exp2(twice(jnp.broadcast_to(sums[j], (8, inner))) * r2)
-        states_low[:states, :] = s.astype(BF16)
-        for i in range(BLK):
-            a = jnp.exp2(spread(drow, i) * r2)
-            decay[i] = a
-            s = a * s + spread(xrow, i) * jnp.broadcast_to(bt[:, i : i + 1], (states, inner))
-            states_low[(i + 1) * states : (i + 2) * states, :] = s.astype(BF16)
-        cr = carry[...]
-        ra = racc[...]
-        for i in reversed(range(BLK)):
-            lam = cr + spread(yrow, i) * jnp.broadcast_to(ct[:, i : i + 1], (states, inner))
-            lam_low[i * states : (i + 1) * states, :] = lam.astype(BF16)
-            cr = decay[i] * lam
-            q = cr * states_low[i * states : (i + 1) * states, :].astype(F32)
-            rq_low[i * states : (i + 1) * states, :] = (q * rr).astype(BF16)
-            ra = ra + q * spread(drow, i)
-        carry[...] = cr
-        racc[...] = ra
-        after = states_low[states:, :]
-        lam_all = lam_low[...]
-        y_out[pl.ds(t0, BLK), :] = dot(cdiag[pl.ds(t0, BLK), :], after)
-        gsum[pl.ds(t0, BLK), :] = dot(bdiag[pl.ds(t0, BLK), :], lam_all)
-        ones = (
-            lax.broadcasted_iota(jnp.int32, (BLK, BLK * states), 1) // states
-            == lax.broadcasted_iota(jnp.int32, (BLK, BLK * states), 0)
-        )
-        hsum[pl.ds(t0, BLK), :] = dot(ones.astype(BF16), rq_low[...])
-        dc[pl.ds(t0, BLK), :] = jnp.where(ones, dot_nt(yrow[...].astype(BF16), after), 0.0).astype(BF16)
-        db[pl.ds(t0, BLK), :] = jnp.where(ones, dot_nt(xrow[...].astype(BF16), lam_all), 0.0).astype(BF16)
-        return 0
-
-    lax.fori_loop(0, blocks, block_step, 0)
+    width = BLK * states
 
     @pl.when(item == 0)
     def _():
         for ref in (rate_grad, skip_grad, dtb_grad, dtp_grad, xp_grad, tap_grad, tapb_grad):
             ref[...] = jnp.zeros(ref.shape, ref.dtype)
 
+    carry[...] = lam_in[...]
+    act_low = act[...]
+    dxs[:toks, :] = delta[...] * act_low.astype(F32)
+    fold = (
+        lax.broadcasted_iota(jnp.int32, (states, width), 1) % states == lax.broadcasted_iota(jnp.int32, (states, width), 0)
+    ).astype(BF16)
+    own = lax.broadcasted_iota(jnp.int32, (toks, width), 0) % BLK == lax.broadcasted_iota(jnp.int32, (toks, width), 1) // states
+    bdiag[:toks, :] = jnp.where(own, dot_tn(proj[rank : rank + states, :].astype(BF16), fold), 0.0).astype(BF16)
+    cdiag[...] = jnp.where(own, dot_tn(proj[rank + states :, :].astype(BF16), fold), 0.0).astype(BF16)
+    mine = own[:BLK]
+    picks = mine.astype(BF16)
+    sides = (
+        lax.broadcasted_iota(jnp.int32, (2 * BLK, 256), 0) // BLK == lax.broadcasted_iota(jnp.int32, (2 * BLK, 256), 1) // 128
+    ).astype(BF16)
+    racc[...] = jnp.zeros((states, inner), F32)
+    qd_low[1] = jnp.zeros(qd_low.shape[1:], BF16)
+
+    def lane_sum(wide):
+        part = [wide[:, at : at + 128] for at in range(0, inner, 128)]
+        while len(part) > 1:
+            part = [sum(part[at : at + 2]) for at in range(0, len(part), 2)]
+        return part[0]
+
+    def products(slot, j):
+        t0 = pl.multiple_of(j * BLK, BLK)
+        gsum[pl.ds(t0, BLK), :] = dot(bdiag[pl.ds(t0, BLK), :], lam_low[slot])
+        hsum[pl.ds(t0, BLK), :] = dot(picks, rq_low[slot])
+        racc[...] += dot(fold[:, : BLK // 4 * states], qd_low[slot])
+        both = dot_nt(sides, dots[slot])
+        dc[pl.ds(t0, BLK), :] = jnp.where(mine, both[:BLK], 0.0).astype(BF16)
+        db[pl.ds(t0, BLK), :] = jnp.where(mine, both[BLK:], 0.0).astype(BF16)
+
+    def one_block(slot, j):
+        t0 = pl.multiple_of(j * BLK, BLK)
+        dr, xr, yr = (ref.at[pl.ds(t0, BLK), :] for ref in (delta, dxs, dy))
+        tile = tiles.at[pl.ds(t0, BLK)]
+        r2 = rate2[...]
+        r_low = rate[...].astype(BF16)
+        s = starts[j] + s_in[...] * jnp.exp2(twice(jnp.broadcast_to(sums[j], (8, inner))) * r2)
+        states_low[slot, :states, :] = s.astype(BF16)
+        for i in range(BLK):
+            a = jnp.exp2(spread(dr, i) * r2)
+            decay[slot, i] = a
+            s = a * s + spread(xr, i) * across_lanes(tile[i, :states], inner)
+            s_low = s.astype(BF16)
+            states_low[slot, (i + 1) * states : (i + 2) * states, :] = s_low
+            dots[slot, i * states : (i + 1) * states, :128] = lane_sum(s_low * spread(yr, i).astype(BF16))
+        y_out[pl.ds(t0, BLK), :] = dot(cdiag[pl.ds(t0, BLK), :], states_low[slot, states:, :])
+        cr = carry[...]
+        qds = []
+        for i in reversed(range(BLK)):
+            lam = cr + spread(yr, i) * across_lanes(tile[i, states:], inner)
+            l_low = lam.astype(BF16)
+            lam_low[slot, i * states : (i + 1) * states, :] = l_low
+            dots[slot, i * states : (i + 1) * states, 128:] = lane_sum(l_low * spread(xr, i).astype(BF16))
+            cr = decay[slot, i] * lam
+            q = cr.astype(BF16) * states_low[slot, i * states : (i + 1) * states, :]
+            rq_low[slot, i * states : (i + 1) * states, :] = q * r_low
+            qds.append(q * spread(dr, i).astype(BF16))
+            if i % 4 == 0:
+                qd_low[slot, i // 4 * states : (i // 4 + 1) * states, :] = (qds[0] + qds[1]) + (qds[2] + qds[3])
+                qds = []
+        carry[...] = cr
+
+    def block_step(k, _):
+        j = blocks - 1 - 2 * k
+        products(1, jnp.where(k == 0, blocks, j + 1))
+        one_block(0, j)
+        products(0, j)
+        one_block(1, j - 1)
+        return 0
+
+    lax.fori_loop(0, blocks // 2, block_step, 0)
+    products(1, 0)
+
     rate_grad[...] += -racc[...]
+    act_f = act_low.astype(F32)
     d_summed = dy[...]
-    g = gsum[...]
+    g = gsum[:toks, :]
     skip_grad[...] += jnp.sum(d_summed * act_f, axis=0, keepdims=True)
     y_out[...] += skip[...] * act_f
-    d_pre = (act_f * g - hsum[...]) * sig[...]
+    d_pre = (act_f * g - hsum[:toks, :]) * sig[...]
     dtb_grad[...] += jnp.sum(d_pre, axis=0, keepdims=True)
     d_pre_low = d_pre.astype(BF16)
     dtp_grad[...] += dot(proj[:rank, :].astype(BF16), d_pre_low)
-    fold = (
-        lax.broadcasted_iota(jnp.int32, (states, width), 1) % states == lax.broadcasted_iota(jnp.int32, (states, width), 0)
-    ).astype(BF16)
     d_proj = jnp.concatenate(
-        [dot_nt(dtw[...], d_pre_low), dot_nt(fold, db[...]), dot_nt(fold, dc[...])], axis=0
+        [dot_nt(dtw[...], d_pre_low), dot_nt(fold, db[:toks, :]), dot_nt(fold, dc[:toks, :])], axis=0
     ).astype(BF16)
     xp_grad[...] += dot(d_proj, act_low)
     d_act = delta[...] * g + skip[...] * d_summed + dot_tn(d_proj, xwt[...])
     d_conv = d_act * dsilu[...]
     tapb_grad[...] += jnp.sum(d_conv, axis=0, keepdims=True)
-    xf[...] = xe[...].astype(F32)
-    pads[:HALO, :] = jnp.zeros((HALO, inner), F32)
-    pads[HALO : HALO + toks, :] = d_conv
-    pads[HALO + toks :, :] = jnp.zeros((HALO, inner), F32)
-    d_window = jnp.zeros((HALO + toks, inner), F32)
-    first = HALO - tap_count + 1
-    for k in range(tap_count):
-        tap_grad[k : k + 1, :] += jnp.sum(d_conv * xf[first + k : first + k + toks, :], axis=0, keepdims=True)
-        d_window = d_window + taps[k : k + 1, :] * pads[tap_count - 1 - k : tap_count - 1 - k + HALO + toks, :]
+    x_f = xe[...].astype(F32)
+    moved = jnp.concatenate([jnp.zeros((HALO, inner), F32), d_conv], axis=0)
+    window = HALO + toks
+    d_window = taps[tap_count - 1 : tap_count, :] * moved
+    tap_grad[tap_count - 1 : tap_count, :] += jnp.sum(moved * x_f, axis=0, keepdims=True)
+    for k in reversed(range(tap_count - 1)):
+        moved = pltpu.roll(moved, window - 1, 0)
+        tap_grad[k : k + 1, :] += jnp.sum(moved * x_f, axis=0, keepdims=True)
+        d_window = d_window + taps[k : k + 1, :] * moved
     rim_out[...] = d_window[HALO - 8 : HALO]
     dx_out[...] = d_window[HALO:]
 
@@ -755,8 +790,6 @@
         [xwt[:, :rank], jnp.zeros((2, wide_rank - rank, inner), BF16), xwt[:, rank:]], axis=1
     )
     dtw = jnp.concatenate([dt_weight, jnp.zeros((2, wide_rank - rank, inner), BF16)], axis=1)
-    bwide = jnp.tile(x_weight[:, :, rank : rank + states], (1, 1, BLK))
-    cwide = jnp.tile(x_weight[:, :, rank + states :], (1, 1, BLK))
     rate2 = -LOG2E * decay_rate
     vec = lambda a: a[:, None, :]
 
@@ -802,7 +835,7 @@
     def unit_shape(*block, kind=F32):
         return jax.ShapeDtypeStruct((slots, 2) + block, kind)
 
-    act, dsilu, delta, sig, proj, end, back, total, starts, sums = pl.pallas_call(
+    act, dsilu, delta, sig, proj, end, back, total, starts, sums, tiles = pl.pallas_call(
         first_kernel,
         grid=(2, slots),
         in_specs=[
@@ -812,16 +845,15 @@
         out_specs=[
             unit(toks, inner), unit(toks, inner), unit(toks, inner), unit(toks, inner), unit(proj_rows, toks),
             unit(states, inner), unit(states, inner), unit(1, inner), unit(blocks, states, inner), unit(blocks, 1, inner),
+            unit(toks, 2 * states, 128),
         ],
         out_shape=[
             unit_shape(toks, inner, kind=BF16), unit_shape(toks, inner), unit_shape(toks, inner), unit_shape(toks, inner),
             unit_shape(proj_rows, toks), unit_shape(states, inner), unit_shape(states, inner), unit_shape(1, inner),
-            unit_shape(blocks, states, inner), unit_shape(blocks, 1, inner),
+            unit_shape(blocks, states, inner), unit_shape(blocks, 1, inner), unit_shape(toks, 2 * states, 128),
         ],
         scratch_shapes=[
-            pltpu.VMEM((HALO + toks, inner), F32), pltpu.VMEM((toks, inner), F32), pltpu.VMEM((toks, inner), F32),
-            pltpu.VMEM((BLK, inner), F32), pltpu.VMEM((BLK, inner), F32), pltpu.VMEM((BLK, inner), F32),
-            pltpu.VMEM((BLK, states, inner), F32), pltpu.VMEM((8, inner), F32),
+            pltpu.VMEM((toks, inner), F32), pltpu.VMEM((2, BLK, states, inner), F32), pltpu.VMEM((8, inner), F32),
         ],
         compiler_params=params(),
         name="first",
@@ -852,9 +884,9 @@
         grid=(2, slots),
         in_specs=[
             unit(states, inner), unit(states, inner), unit(blocks, states, inner),
-            unit(blocks, 1, inner), branch(states, inner), branch(states, inner), unit(HALO + toks, inner), unit(toks, inner),
+            unit(blocks, 1, inner), unit(toks, 2 * states, 128), branch(states, inner), branch(states, inner), unit(HALO + toks, inner), unit(toks, inner),
             unit(toks, inner), unit(toks, inner), unit(toks, inner), unit(toks, inner), unit(proj_rows, toks),
-            branch(proj_rows, inner), branch(inner, BLK * states), branch(inner, BLK * states), branch(wide_rank, inner),
+            branch(proj_rows, inner), branch(wide_rank, inner),
             branch(tap_count, inner), branch(1, inner),
         ],
         out_specs=[
@@ -867,20 +899,20 @@
             jax.ShapeDtypeStruct((2, rows, inner), F32) for rows in (states, 1, 1, wide_rank, proj_rows, tap_count, 1)
         ],
         scratch_shapes=[
-            pltpu.VMEM((states, inner), F32), pltpu.VMEM((toks, inner), F32),
-            pltpu.VMEM((toks, BLK * states), BF16), pltpu.VMEM((toks, BLK * states), BF16),
-            pltpu.VMEM((BLK, inner), F32), pltpu.VMEM((BLK, inner), F32), pltpu.VMEM((BLK, inner), F32),
-            pltpu.VMEM((BLK, states, inner), F32), pltpu.VMEM(((BLK + 1) * states, inner), BF16),
-            pltpu.VMEM((BLK * states, inner), BF16), pltpu.VMEM((BLK * states, inner), BF16),
-            pltpu.VMEM((states, inner), F32), pltpu.VMEM((toks, inner), F32), pltpu.VMEM((toks, inner), F32),
-            pltpu.VMEM((toks, BLK * states), BF16), pltpu.VMEM((toks, BLK * states), BF16),
-            pltpu.VMEM((toks + 2 * HALO, inner), F32), pltpu.VMEM((toks + HALO, inner), F32),
+            pltpu.VMEM((states, inner), F32), pltpu.VMEM((toks + BLK, inner), F32), pltpu.VMEM((toks + BLK, BLK * states), BF16),
+            pltpu.VMEM((toks, BLK * states), BF16),
+            pltpu.VMEM((2, BLK, states, inner), F32),
+            pltpu.VMEM((2, (BLK + 1) * states, inner), BF16), pltpu.VMEM((2, BLK * states, inner), BF16),
+            pltpu.VMEM((2, BLK * states, inner), BF16), pltpu.VMEM((2, BLK // 4 * states, inner), BF16),
+            pltpu.VMEM((2, BLK * states, 256), BF16), pltpu.VMEM((states, inner), F32),
+            pltpu.VMEM((toks + BLK, inner), F32), pltpu.VMEM((toks + BLK, inner), F32),
+            pltpu.VMEM((toks + BLK, BLK * states), BF16), pltpu.VMEM((toks + BLK, BLK * states), BF16),
         ],
         compiler_params=params(),
         name="second",
     )(
-        s_in, lam_in, starts, sums, rate2, decay_rate, xe, act, dsilu, delta,
-        sig, dy, proj, xwt, bwide, cwide, dtw, conv_weight, vec(skip_gain),
+        s_in, lam_in, starts, sums, tiles, rate2, decay_rate, xe, act, dsilu, delta,
+        sig, dy, proj, xwt, dtw, conv_weight, vec(skip_gain),
     )
 
     mixed, d_tokens, d_mod, out_grad, in_grad = pl.pallas_call(

time: 265 us -> 240 us (0.906)
  Pallas kernels: 248 us -> 225 us
    pallas_call x1, Pallas kernels: 103 us -> 83.2 us  [per_device(): pl.pallas_call(second_kernel, grid=(2, slots), in_specs=[unit(states, inn...]
where the time goes in v2:
time: 240 us
  Pallas kernels  225 us (94%)
  local copies, waits for them, and re-layouts  10.5 us (4%)
  other arithmetic  2.72 us (1%)
    pallas_call x1, Pallas kernels, per_device(): pl.pallas_call(second_kernel, grid=(2, slots), in_specs=[unit(states, inn...  83.2 us
    pallas_call x1, Pallas kernels, per_device(): pl.pallas_call(functools.partial(reduce_kernel, (runs, groups, rows)), in...  52.6 us
    pallas_call x1, Pallas kernels, per_device(): pl.pallas_call(first_kernel, grid=(2, slots), in_specs=[unit(HALO + toks,...  43.3 us
    pallas_call x1, Pallas kernels, per_device(): pl.pallas_call(functools.partial(exchange_kernel, runs), in_specs=[vmem]...  14.7 us
    pallas_call x1, Pallas kernels, per_device(): pl.pallas_call(functools.partial(third_kernel, runs), grid=(slots,), in_s...  13.9 us
    pallas_call x1, Pallas kernels, per_device(): pl.pallas_call(functools.partial(enter_kernel, runs), grid=(slots,), in_s...  11.8 us
    pallas_call x1, Pallas kernels, per_device(): pl.pallas_call(functools.partial(finish_kernel, (rank, wide_rank)), in_sp...  5.89 us

profile of v2, /device:TPU:0, one launch (start us, length us, event | category | flops | bytes accessed | tf_op | source)
XLA Modules:
  0.0 240.1 jit_solution(1867577840451824967)
XLA Ops:
  0.6 0.0 copy-start.5
  0.7 0.0 copy-start.3
  0.7 0.0 copy-start.4
  1.4 1.3 copy.31.step
  2.6 1.3 broadcast_in_dim.20.ada_bias
  3.9 0.0 copy-start.6
  3.9 0.0 copy-start.2
  3.9 11.8 %enter.1 = (bf16[3,2,272,768]{3,2,1,0:T(8,128)(2,1)}, f32[3,2,256,768]{3,2,1,0:T(8,128)}, f32[3,256,768]{2,1,0:T(8,128)}, bf16[3,256,384]{2,1,0:T(8,128)(2,1)}, f32[3,1,1152]{2,1,0:T(1,128)}) custom-call(bf16[3,256,384]{2,1,0:T(8,128)(2,1)} %tok.3, bf16[3,256,384]{2,1,0:T(8,128)(2,1)} %cot.3, s32[3,256]{1,0:T(4,128)} %mask.3, s32[1,1]{1,0:T(1,128)} %bitcast.3.counts, ...), custom_call_target="tpu_custom_call" | custom-call | tf_op jit(solution)/shard_map/enter/pallas_call | solution.py:802
  15.8 0.0 copy-done.5
  15.8 0.6 broadcast_in_dim.21.tap_bias
  16.4 0.0 copy-done.3
  16.4 0.1 pad.2.clone
  16.5 0.8 pad_maximum_fusion.xwt
  17.3 0.0 copy-done.4
  17.3 0.6 concatenate.7.dtw
  17.9 0.0 copy-done.6
  17.9 0.6 broadcast_in_dim.22.dt_bias
  18.5 0.0 copy-done.2
  18.5 0.6 broadcast_multiply_fusion.rate2
  19.2 0.0 copy-start.7
  19.2 43.3 %first.1 = (bf16[3,2,256,768]{3,2,1,0:T(8,128)(2,1)}, f32[3,2,256,768]{3,2,1,0:T(8,128)}, f32[3,2,256,768]{3,2,1,0:T(8,128)}, f32[3,2,256,768]{3,2,1,0:T(8,128)}...) custom-call(bf16[3,2,272,768]{3,2,1,0:T(8,128)(2,1)} %get-tuple-elem, ...), custom_call_target="tpu_custom_call" | custom-call | tf_op jit(solution)/shard_map/first/pallas_call | solution.py:838
  62.5 14.7 %exchange.1 = (f32[3,2,16,768]{3,2,1,0:T(8,128)}, f32[3,2,16,768]{3,2,1,0:T(8,128)}) custom-call(f32[3,2,16,768]{3,2,1,0:T(8,128)} %get-tuple-element.66.end, f32[3,2,16,768]{3,2,1,0:T(8,128)} %get-tuple-element.67.back, f32[3,2,1,768]{3,2,1,0:T(1,128)} %get-tuple-element.68.total, f32[2,16,768]{2,1,0:T(8,128)} %broadcast_multiply_fusion.rate2), custom_call_target="tpu_custom_call" | custom-call | tf_op jit(solution)/shard_map/exchange/pallas_call | solution.py:865
  77.2 0.0 copy-done.7
  77.2 0.6 broadcast_in_dim.23.skip
  77.8 83.2 %second.1 = (f32[3,2,256,768]{3,2,1,0:T(8,128)}, f32[3,2,256,768]{3,2,1,0:T(8,128)}, f32[2,3,8,768]{3,2,1,0:T(8,128)}, f32[2,16,768]{2,1,0:T(8,128)}, f32[2,1,76...) custom-call(f32[3,2,16,768]{3,2,1,0:T(8,128)} %get-tuple-element.69., ...), custom_call_target="tpu_custom_call" | custom-call | tf_op jit(solution)/shard_map/second/pallas_call | solution.py:882
  161.0 13.9 %third.1 = (bf16[3,256,384]{2,1,0:T(8,128)(2,1)}, f32[3,256,384]{2,1,0:T(8,128)}, f32[3,3,384]{2,1,0:T(4,128)}, f32[768,384]{1,0:T(8,128)}, f32[384,1536]{1,0:T(8,128)}) custom-call(bf16[3,256,384]{2,1,0:T(8,128)(2,1)} %tok.3, bf16[3,256,384]{2,1,0:T(8,128)(2,1)} %cot.3, f32[3,1,1152]{2,1,0:T(1,128)} %get-tuple-element.61.mod, s32[3,256]{1,0:T(4,128)} %mask.3, ...), custom_call_target="tpu_custom_call" | custom-call | tf_op jit(solution)/shard_map/third/pallas_call | solution.py:918
  174.9 52.6 %reduce.2 = (bf16[1536,768]{1,0:T(8,128)(2,1)}, bf16[128,384]{1,0:T(8,128)(2,1)}) custom-call(f32[384,1536]{1,0:T(8,128)} %get-tuple-element.84.in_grad, f32[768,384]{1,0:T(8,128)} %get-tuple-element.85.out_grad, f32[2,64,768]{2,1,0:T(8,128)} %get-tuple-element.86.xp_grad, f32[2,32,768]{2,1,0:T(8,128)} %get-tuple-element.87.dtp_grad, ...), custom_call_target="tpu_custom_call" | custom-call | tf_op jit(solution)/shard_map/reduce/pallas_call | solution.py:945
  227.6 0.0 copy-start.1
  227.6 1.4 constant_dynamic-slice_fusion.own
  228.9 0.0 copy-start
  228.9 5.9 %finish.1 = (f32[3,384]{1,0:T(4,128)}, f32[384,1152]{1,0:T(8,128)}, f32[1,1152]{1,0:T(1,128)}, f32[384,1536]{1,0:T(8,128)}, f32[2,4,768]{2,1,0:T(4,128)}, /*inde...) custom-call(bf16[1536,768]{1,0:T(8,128)(2,1)} %get-tuple-element.94., ...), custom_call_target="tpu_custom_call" | custom-call | tf_op jit(solution)/shard_map/finish/pallas_call | solution.py:968
  234.8 1.3 reduce.1
  236.1 2.1 copy.32
  238.3 0.0 copy-done.1
  238.3 0.8 copy.36
  239.1 0.0 copy-done
  239.1 1.0 copy.37
  (3 shorter events, 0.0 us)
Async XLA Ops:
  0.6 15.1 %copy-start.5 = (f32[2,768]{1,0:T(2,128)S(1)}, f32[2,768]{1,0:T(2,128)}, u32[]{:S(2)}) copy-start(f32[2,768]{1,0:T(2,128)} %param.24) | copy-start | bytes 18436
  0.7 15.7 %copy-start.3 = (bf16[2,768,56]{1,2,0:T(8,128)(2,1)S(1)}, bf16[2,768,56]{1,2,0:T(8,128)(2,1)}, u32[]{:S(2)}) copy-start(bf16[2,768,56]{1,2,0:T(8,128)(2,1)} %param.25) | copy-start | bytes 516100
  0.7 16.6 %copy-start.4 = (bf16[2,24,768]{2,1,0:T(8,128)(2,1)S(1)}, bf16[2,24,768]{2,1,0:T(8,128)(2,1)}, u32[]{:S(2)}) copy-start(bf16[2,24,768]{2,1,0:T(8,128)(2,1)} %param.26) | copy-start | bytes 221188
  3.9 14.0 %copy-start.6 = (f32[2,768]{1,0:T(2,128)S(1)}, f32[2,768]{1,0:T(2,128)}, u32[]{:S(2)}) copy-start(f32[2,768]{1,0:T(2,128)} %param.27) | copy-start | bytes 18436
  3.9 14.6 %copy-start.2 = (f32[2,16,768]{2,1,0:T(8,128)S(1)}, f32[2,16,768]{2,1,0:T(8,128)}, u32[]{:S(2)}) copy-start(f32[2,16,768]{2,1,0:T(8,128)} %rate.1) | copy-start | bytes 294916
  19.2 58.0 %copy-start.7 = (f32[2,768]{1,0:T(2,128)S(1)}, f32[2,768]{1,0:T(2,128)}, u32[]{:S(2)}) copy-start(f32[2,768]{1,0:T(2,128)} %param.29) | copy-start | bytes 18436
  227.6 10.7 %copy-start.1 = (bf16[3,256,384]{2,1,0:T(8,128)(2,1)S(1)}, bf16[3,256,384]{2,1,0:T(8,128)(2,1)}, u32[]{:S(2)}) copy-start(bf16[3,256,384]{2,1,0:T(8,128)(2,1)} %get-tuple-element.150) | copy-start | bytes 1769476
  228.9 10.1 %copy-start = (f32[3,256,384]{2,1,0:T(8,128)S(1)}, f32[3,256,384]{2,1,0:T(8,128)}, u32[]{:S(2)}) copy-start(f32[3,256,384]{2,1,0:T(8,128)} %get-tuple-element.151) | copy-start | bytes 3538948

commit v3 on v2

--- a/solution.py
+++ b/solution.py
@@ -152,9 +152,11 @@
             next_mask[...] = jnp.zeros(next_mask.shape, jnp.int32)
 
     live = (counts[...] > i).astype(F32)
-    time_f = step[...].astype(F32)
+    steps = step[...].astype(F32)
+    here = lax.broadcasted_iota(jnp.int32, steps.shape, 0) == i
+    time_f = jnp.sum(jnp.where(here, steps, 0.0), axis=0, keepdims=True)
     time_low = (time_f * jax.nn.sigmoid(time_f)).astype(BF16)
-    mod = dot(time_low, ada[...]) + ada_bias[...]
+    mod = dot(time_low, ada[...]) + ada_bias[...].reshape(1, 3 * dim)
     mod_out[...] = mod
     shift, scale, gate = mod[:, :dim], mod[:, dim : 2 * dim], mod[:, 2 * dim :]
 
@@ -196,9 +198,21 @@
     return twice(ref[pl.ds(index, 8, stride=0), :])
 
 
-def lay_out(tiles, rows):
-    for t in range(rows.shape[1]):
-        tiles[t] = jnp.broadcast_to(rows[:, t : t + 1], (rows.shape[0], 128))
+def lay_out(wide, rows, picks):
+    count, toks = rows.shape
+    high = rows.astype(BF16).astype(F32)
+    halves = jnp.concatenate([high, rows - high], axis=0).T.astype(BF16)
+    for n in range(0, count, 2):
+        pair = dot(halves, picks[:, n * 128 : (n + 2) * 128])
+        for t in range(0, toks, 8):
+            for k in range(2):
+                at = 8 * (count * (t // 8) + n + k)
+                wide[at : at + 8, :] = pair[t : t + 8, k * 128 : (k + 1) * 128]
+
+
+def wide_tile(wide, i, count):
+    at = 8 * count * (i // 8) + i % 8
+    return jnp.concatenate([wide[pl.ds(at + 64 * n, 8, stride=8), :] for n in range(count // 8)], axis=0)
 
 
 def across_lanes(tile, inner):
@@ -212,17 +226,32 @@
 
 
 def first_kernel(
-    xe, dy, taps, tap_bias, xwt, dtw, dt_bias, rate2,
-    act_out, dsilu_out, delta_out, sig_out, proj_out, end_out, back_out, total_out, starts_out, sums_out, tiles,
-    dx, decay, through,
+    xe, dy, taps, tap_bias, x_rows, dt_rows, dt_bias, rate,
+    act_out, dsilu_out, delta_out, sig_out, proj_out, end_out, back_out, total_out, starts_out, sums_out, tiles, xwt, dtw,
+    dx, decay, through, rate2, wide, picks,
 ):
     toks, inner = dy.shape
-    states = rate2.shape[0]
+    states = rate.shape[0]
     blocks = toks // BLK
     rank = dtw.shape[0]
     tap_count = taps.shape[0]
+    branch = pl.program_id(0)
+
+    @pl.when(pl.program_id(1) == 0)
+    def _():
+        rate2[...] = rate[...] * -LOG2E
+        picks[...] = (
+            lax.broadcasted_iota(jnp.int32, picks.shape, 0) % (2 * states)
+            == lax.broadcasted_iota(jnp.int32, picks.shape, 1) // 128
+        ).astype(BF16)
+        held = dt_rows.shape[0]
+        rows = x_rows[...].astype(F32)
+        gap = jnp.zeros((rank - held, inner), F32)
+        xwt[...] = jnp.concatenate([rows[:held], gap, rows[held:]], axis=0).astype(BF16)
+        dtw[...] = jnp.concatenate([dt_rows[...].astype(F32), gap], axis=0).astype(BF16)
+
     shifted = xe[...].astype(F32)
-    conv = tap_bias[...] + taps[tap_count - 1 : tap_count, :] * shifted[HALO:]
+    conv = tap_bias[pl.ds(branch, 1), :] + taps[tap_count - 1 : tap_count, :] * shifted[HALO:]
     for k in reversed(range(tap_count - 1)):
         shifted = pltpu.roll(shifted, 1, 0)
         conv = conv + taps[k : k + 1, :] * shifted[HALO:]
@@ -233,12 +262,12 @@
     act_out[...] = act
     proj = dot_nt(xwt[...], act)
     proj_out[...] = proj
-    lay_out(tiles, proj[rank:, :])
-    pre = dot_tn(proj[:rank, :].astype(BF16), dtw[...]) + dt_bias[...]
+    pre = dot_tn(proj[:rank, :].astype(BF16), dtw[...]) + dt_bias[pl.ds(branch, 1), :]
     delta, slope = softplus_parts(pre)
     delta_out[...] = delta
     sig_out[...] = slope
     dx[...] = delta * act.astype(F32)
+    lay_out(wide, proj[rank:, :], picks)
     end_out[...] = jnp.zeros((states, inner), F32)
     back_out[...] = jnp.zeros((states, inner), F32)
     through[...] = jnp.zeros((8, inner), F32)
@@ -246,21 +275,24 @@
     def one_block(j, slot):
         t0 = pl.multiple_of(j * BLK, BLK)
         dr, xr, yr = (ref.at[pl.ds(t0, BLK), :] for ref in (delta_out, dx, dy))
-        tile = tiles.at[pl.ds(t0, BLK)]
-        rate = rate2[...]
+        count = 2 * states
+        wide_rows = wide.at[pl.ds(pl.multiple_of(j * (BLK * count), BLK * count), BLK * count), :]
         s = end_out[...]
         starts_out[j] = s
         before = through[...]
         sums_out[j] = before[:1, :]
+        rates = rate2[...]
         for i in range(BLK):
-            a = jnp.exp2(spread(dr, i) * rate)
+            a = jnp.exp2(spread(dr, i) * rates)
             decay[slot, i] = a
-            s = a * s + spread(xr, i) * across_lanes(tile[i, :states], inner)
+            tile = wide_tile(wide_rows, i, count)
+            tiles[t0 + i] = tile
+            s = a * s + spread(xr, i) * across_lanes(tile[:states], inner)
         end_out[...] = s
         m = jnp.zeros((states, inner), F32)
         for i in reversed(range(BLK)):
-            m = decay[slot, i] * (m + spread(yr, i) * across_lanes(tile[i, states:], inner))
-        back_out[...] = back_out[...] + m * jnp.exp2(twice(before) * rate)
+            m = decay[slot, i] * (m + spread(yr, i) * across_lanes(tiles[t0 + i, states:], inner))
+        back_out[...] = back_out[...] + m * jnp.exp2(twice(before) * rates)
         through[...] = before + jnp.sum(dr[...], axis=0, keepdims=True)
 
     def block_step(k, _):
@@ -273,16 +305,18 @@
 
 
 def second_kernel(
-    s_in, lam_in, starts, sums, tiles, rate2, rate, xe, act, dsilu, delta, sig, dy, proj, xwt, dtw, taps, skip,
+    s_in, lam_in, starts, sums, tiles, rate, xe, act, dsilu, delta, sig, dy, proj, xwt, dtw, taps, skip,
     y_out, dx_out, rim_out, rate_grad, skip_grad, dtb_grad, dtp_grad, xp_grad, tap_grad, tapb_grad,
-    carry, dxs, bdiag, cdiag, decay, states_low, lam_low, rq_low, qd_low, dots, racc, gsum, hsum, db, dc,
+    rate2, carry, dxs, bdiag, cdiag, decay, states_low, lam_low, rq_low, qd_low, dots, racc, gsum, hsum, db, dc,
 ):
     toks, inner = dy.shape
-    states = rate2.shape[0]
+    states = rate.shape[0]
     blocks = toks // BLK
     rank = dtw.shape[0]
     tap_count = taps.shape[0]
     item = pl.program_id(1)
+    gain = skip[pl.ds(pl.program_id(0), 1), :]
+    rate2[...] = rate[...] * -LOG2E
     width = BLK * states
 
     @pl.when(item == 0)
@@ -370,7 +404,7 @@
     d_summed = dy[...]
     g = gsum[:toks, :]
     skip_grad[...] += jnp.sum(d_summed * act_f, axis=0, keepdims=True)
-    y_out[...] += skip[...] * act_f
+    y_out[...] += gain * act_f
     d_pre = (act_f * g - hsum[:toks, :]) * sig[...]
     dtb_grad[...] += jnp.sum(d_pre, axis=0, keepdims=True)
     d_pre_low = d_pre.astype(BF16)
@@ -379,7 +413,7 @@
         [dot_nt(dtw[...], d_pre_low), dot_nt(fold, db[:toks, :]), dot_nt(fold, dc[:toks, :])], axis=0
     ).astype(BF16)
     xp_grad[...] += dot(d_proj, act_low)
-    d_act = delta[...] * g + skip[...] * d_summed + dot_tn(d_proj, xwt[...])
+    d_act = delta[...] * g + gain * d_summed + dot_tn(d_proj, xwt[...])
     d_conv = d_act * dsilu[...]
     tapb_grad[...] += jnp.sum(d_conv, axis=0, keepdims=True)
     x_f = xe[...].astype(F32)
@@ -473,7 +507,7 @@
     return mine, {axis: me + (1 - 2 * mine) * (1 << bit)}
 
 
-def exchange_kernel(runs, end, back, total, rate2, s_in, lam_in, group, span, pre, pre_span, sends, arrivals, send_sem, recv_sem):
+def exchange_kernel(runs, end, back, total, rates, s_in, lam_in, group, span, pre, pre_span, sends, arrivals, send_sem, recv_sem):
     slots, _, states, inner = end.shape
     bits = int(math.log2(runs))
     links = [across("seq", bit) for bit in range(bits)]
@@ -483,38 +517,40 @@
     rows = units * states
     pre[...] = jnp.zeros(pre.shape, F32)
     pre_span[...] = jnp.zeros(pre_span.shape, F32)
+    span[...] = jnp.zeros(span.shape, F32)
     for flow in range(2):
         for kind, (array, branch) in enumerate(flows[flow]):
             for i in range(slots):
-                group[flow, kind * slots + i] = array[i, branch]
-                span[flow, kind * slots + i] = jnp.broadcast_to(total[i, branch], (8, inner))
+                unit = kind * slots + i
+                group[flow, unit] = array[i, branch]
+                span[flow, unit : unit + 1, :] = total[i, branch]
 
     def load(flow, slot):
         for unit in range(units):
             sends[slot, unit * states : (unit + 1) * states, :] = group[flow, unit].astype(BF16)
-            high = span[flow, unit].astype(BF16)
-            low = (span[flow, unit] - high.astype(F32)).astype(BF16)
-            at = rows + unit * 16
-            sends[slot, at : at + 16, :] = jnp.concatenate([high.astype(F32), low.astype(F32)], axis=0).astype(BF16)
+        high = span[flow].astype(BF16).astype(F32)
+        sends[slot, rows:, :] = jnp.concatenate([high, span[flow] - high], axis=0).astype(BF16)
 
     def join(flow, slot, earlier, last):
+        both = arrivals[slot, rows:, :].astype(F32)
+        length = both[: both.shape[0] // 2] + both[both.shape[0] // 2 :]
+        own_span = span[flow]
+        mine_span = pre_span[flow]
+        second_span = jnp.where(earlier, own_span, length)
         for unit in range(units):
-            rate = rate2[flows[flow][unit // slots][1]]
+            rate = rates[flows[flow][unit // slots][1]] * -LOG2E
             state = arrivals[slot, unit * states : (unit + 1) * states, :].astype(F32)
-            at = rows + unit * 16
-            both = arrivals[slot, at : at + 16, :].astype(F32)
-            length = both[:8] + both[8:]
-            mine, mine_span = pre[flow, unit], pre_span[flow, unit]
-            joined = state * jnp.exp2(rate * twice(mine_span)) + mine
+            mine = pre[flow, unit]
+            joined = state * jnp.exp2(rate * mine_span[unit : unit + 1]) + mine
             pre[flow, unit] = jnp.where(earlier, joined, mine)
-            pre_span[flow, unit] = jnp.where(earlier, length + mine_span, mine_span)
             if not last:
-                own, own_span = group[flow, unit], span[flow, unit]
+                own = group[flow, unit]
                 first = jnp.where(earlier, state, own)
                 second = jnp.where(earlier, own, state)
-                second_span = jnp.where(earlier, own_span, length)
-                group[flow, unit] = first * jnp.exp2(rate * twice(second_span)) + second
-                span[flow, unit] = own_span + length
+                group[flow, unit] = first * jnp.exp2(rate * second_span[unit : unit + 1]) + second
+        pre_span[flow] = jnp.where(earlier, length + mine_span, mine_span)
+        if not last:
+            span[flow] = own_span + length
 
     for stage, (mine, target) in enumerate(links):
         last = stage == bits - 1
@@ -561,19 +597,19 @@
                 result[i, branch] = pre[flow, kind * slots + i]
 
 
-PARTS = 3
+PARTS = 6
 LAST_ROWS = 16
 
 
 def reduce_rows(dim, inner, small):
-    rows = 3 * dim + small
+    rows = inner + (2 * dim + small) * (inner // dim)
     unit = PARTS * LAST_ROWS * 32
     return -(-rows // unit) * unit
 
 
 def reduce_kernel(
     plan, in_grad, out_grad, xp_grad, dtp_grad, rate_grad, tap_grad, tapb_grad, skip_grad, dtb_grad, d_mod, step,
-    result, factors,
+    result, factors, own_rows,
     acc, sends, arrivals, gathered, mod_sum, mod_in, table, send_sem, recv_sem, small_send, small_recv,
 ):
     runs, groups, total_rows = plan
@@ -583,18 +619,12 @@
     seq_bits = [("seq", bit) for bit in range(int(math.log2(runs)))]
     dp_bits = [("dp", bit) for bit in range(int(math.log2(groups)))]
     all_bits = seq_bits + dp_bits
+    count = len(all_bits)
     links = {key: across(*key) for key in all_bits}
-    greet([links[key][1] for key in all_bits])
     middle = all_bits[1:-1]
-    orders = [
-        all_bits[:1] + middle[part % max(len(middle), 1) :] + middle[: part % max(len(middle), 1)] + all_bits[1:][-1:]
-        for part in range(PARTS)
-    ]
+    turn = [part % max(len(middle), 1) for part in range(PARTS)]
+    orders = [all_bits[:1] + middle[at:] + middle[:at] + all_bits[1:][-1:] for at in turn]
     part_rows = total_rows // PARTS
-
-    mod_sum[...] = jnp.zeros(mod_sum.shape, F32)
-    for i in range(slots):
-        mod_sum[3 * i : 3 * i + 3, :] = d_mod[i]
 
     def small_copy(stage):
         axis, bit = all_bits[stage]
@@ -611,87 +641,126 @@
         time_low = time_f * jax.nn.sigmoid(time_f)
         at = pl.multiple_of(lax.axis_index("dp") * 16, 16)
         own = jnp.concatenate([mod_sum[: 3 * slots, :], time_low, mod_sum[4 * slots :, :]], axis=0)
+        own_rows[...] = own.astype(BF16)
         table[pl.ds(at, 16), :] = own.astype(BF16)
 
-    half = dim
-    acc[0:dim, :] = in_grad[:, :inner]
-    acc[dim : 2 * dim, :] = in_grad[:, inner:]
-    acc[2 * dim : 3 * dim, :] = jnp.concatenate([out_grad[:half, :], out_grad[half:, :]], axis=1)
-    at = 3 * dim
+    def start_small(stage):
+        if stage == len(seq_bits):
+            fill_table()
+        if stage < count:
+            small_copy(stage).start()
+
+    def end_small(stage):
+        small_copy(stage).wait()
+        if all_bits[stage][0] == "seq":
+            mod_sum[...] += mod_in[stage]
+
+    segments = [(lambda at, size: out_grad[at : at + size, :], inner)]
+    for lane in range(0, 2 * inner, dim):
+        segments.append((lambda at, size, lane=lane: in_grad[at : at + size, lane : lane + dim], dim))
+    small = []
     for ref in (xp_grad, dtp_grad, rate_grad, tap_grad):
-        for branch in range(2):
-            size = ref.shape[1]
-            acc[at : at + size, :] = ref[branch]
+        small += [(lambda ref=ref, branch=branch: ref[branch], ref.shape[1]) for branch in range(2)]
+
+    def tail():
+        rows = [ref[branch] for ref in (tapb_grad, skip_grad, dtb_grad) for branch in range(2)]
+        return jnp.concatenate(rows + [jnp.zeros((2, inner), F32)], axis=0)
+
+    small.append((tail, 8))
+    for lane in range(0, inner, dim):
+        for get, size in small:
+            segments.append((lambda at, size, get=get, lane=lane: get()[at : at + size, lane : lane + dim], size))
+    total = sum(size for _, size in segments)
+    segments.append((lambda at, size: jnp.zeros((size, dim), F32), total_rows - total))
+
+    def assemble(part):
+        low, high = part * part_rows, (part + 1) * part_rows
+        at = 0
+        for get, size in segments:
+            first, last = max(at, low), min(at + size, high)
+            if first < last:
+                acc[first:last, :] = get(first - at, last - first)
             at += size
-    tail = [ref[branch] for ref in (tapb_grad, skip_grad, dtb_grad) for branch in range(2)]
-    acc[at : at + 8, :] = jnp.concatenate(tail + [jnp.zeros((2, inner), F32)], axis=0)
-    at += 8
-    acc[at:, :] = jnp.zeros((total_rows - at, inner), F32)
 
     starts = [part * part_rows for part in range(PARTS)]
     sizes = [part_rows] * PARTS
     history = [[] for _ in range(PARTS)]
-    offsets = [part * part_rows for part in range(PARTS)]
-    count = len(all_bits)
-    for stage in range(count):
-        copies = []
+    offsets = [part * (part_rows + LAST_ROWS * count) for part in range(PARTS)]
+    flying = [None] * PARTS
+
+    def scatter(part, stage):
+        mine, target = links[orders[part][stage]]
+        start, size = starts[part], sizes[part]
+        split = size >= 2 * LAST_ROWS
+        moved = size // 2 if split else size
+        away = keep = start
+        if split:
+            away = pl.multiple_of(start + (1 - mine) * moved, LAST_ROWS)
+            keep = pl.multiple_of(start + mine * moved, LAST_ROWS)
+        history[part].append((start, size, split))
+        at = offsets[part]
+        offsets[part] += moved
+        sends[at : at + moved, :] = acc[pl.ds(away, moved), :].astype(BF16)
+        copy = remote(
+            sends.at[pl.ds(at, moved), :], arrivals.at[pl.ds(at, moved), :], send_sem.at[part, stage],
+            recv_sem.at[part, stage], target,
+        )
+        copy.start()
+        starts[part], sizes[part] = keep, moved
+        flying[part] = (copy, keep, moved, at, split)
+
+    def settle(part):
+        copy, keep, moved, at, split = flying[part]
+        copy.wait()
+        held = acc[pl.ds(keep, moved), :]
+        if not split:
+            held = held.astype(BF16).astype(F32)
+        acc[pl.ds(keep, moved), :] = held + arrivals[at : at + moved, :].astype(F32)
+
+    def gather(part, stage):
+        start, size, split = history[part][stage]
+        flying[part] = None
+        if split:
+            here = gathered.at[pl.ds(starts[part], sizes[part]), :]
+            target = links[orders[part][stage]][1]
+            flying[part] = remote(
+                here, here, send_sem.at[part, count + stage], recv_sem.at[part, count + stage], target
+            )
+            flying[part].start()
+            starts[part], sizes[part] = start, size
+
+    mod_sum[...] = jnp.zeros(mod_sum.shape, F32)
+    for i in range(slots):
+        mod_sum[3 * i : 3 * i + 3, :] = d_mod[i]
+    greet([links[key][1] for key in all_bits])
+    start_small(0)
+    for part in range(PARTS):
+        assemble(part)
+        scatter(part, 0)
+    for stage in range(1, count):
+        end_small(stage - 1)
+        start_small(stage)
         for part in range(PARTS):
-            mine, target = links[orders[part][stage]]
-            start, size = starts[part], sizes[part]
-            split = size >= 2 * LAST_ROWS
-            moved = size // 2 if split else size
-            if split:
-                away = pl.multiple_of(start + (1 - mine) * moved, LAST_ROWS)
-                keep = pl.multiple_of(start + mine * moved, LAST_ROWS)
-            else:
-                away = keep = start
-            history[part].append((start, size, split))
-            at = offsets[part]
-            offsets[part] += moved
-            here = sends.at[pl.ds(at, moved), :]
-            sends[at : at + moved, :] = acc[pl.ds(away, moved), :].astype(BF16)
-            copy = remote(
-                here, arrivals.at[pl.ds(at, moved), :], send_sem.at[part, stage], recv_sem.at[part, stage], target
-            )
-            copy.start()
-            copies.append((copy, part, keep, moved, at, split))
-            starts[part], sizes[part] = keep, moved
-        if stage == len(seq_bits):
-            fill_table()
-        small = small_copy(stage)
-        small.start()
-        for copy, part, keep, moved, at, split in copies:
-            copy.wait()
-            held = acc[pl.ds(keep, moved), :]
-            if not split:
-                held = held.astype(BF16).astype(F32)
-            acc[pl.ds(keep, moved), :] = held + arrivals[at : at + moved, :].astype(F32)
-        small.wait()
-        if all_bits[stage][0] == "seq":
-            mod_sum[...] += mod_in[stage]
+            settle(part)
+            scatter(part, stage)
+    end_small(count - 1)
     if not dp_bits:
         fill_table()
-    factors[...] = table[...]
     for part in range(PARTS):
+        settle(part)
         where = pl.ds(starts[part], sizes[part])
         gathered[where, :] = acc[where, :].astype(BF16)
-    for stage in reversed(range(count)):
-        copies = []
+        gather(part, count - 1)
+    for stage in reversed(range(count - 1)):
         for part in range(PARTS):
-            start, size, split = history[part][stage]
-            if not split:
-                continue
-            target = links[orders[part][stage]][1]
-            here = gathered.at[pl.ds(starts[part], sizes[part]), :]
-            copy = remote(
-                here, here, send_sem.at[part, count + stage], recv_sem.at[part, count + stage], target
-            )
-            copy.start()
-            copies.append(copy)
-            starts[part], sizes[part] = start, size
-        for copy in copies:
-            copy.wait()
-    result[...] = gathered[...]
+            if flying[part] is not None:
+                flying[part].wait()
+            gather(part, stage)
+    for part in range(PARTS):
+        if flying[part] is not None:
+            flying[part].wait()
+        result[part * part_rows : (part + 1) * part_rows, :] = gathered[part * part_rows : (part + 1) * part_rows, :]
+    factors[...] = table[...]
 
 
 def finish_kernel(
@@ -708,31 +777,31 @@
     def rows(at, size):
         return result[at : at + size, :].astype(F32)
 
-    in_grad[:, :inner] = rows(0, dim)
-    in_grad[:, inner:] = rows(dim, dim)
-    both = rows(2 * dim, dim)
-    out_grad[:dim, :] = both[:, :dim]
-    out_grad[dim:, :] = both[:, dim:]
-    at = 3 * dim
+    out_grad[...] = rows(0, inner)
+    at = inner
+    for lane in range(0, 2 * inner, dim):
+        in_grad[:, lane : lane + dim] = rows(at, dim)
+        at += dim
     wide = wide_rank + 2 * states
-    for branch in range(2):
-        part = rows(at, wide)
-        part = jnp.concatenate([part[:rank], part[wide_rank:], part[rank:wide_rank]], axis=0)
-        part = jnp.concatenate([part, jnp.zeros((128 - wide, inner), F32)], axis=0)
-        xp_grad[branch] = part.T[:, : rank + 2 * states]
-        at += wide
-    for branch in range(2):
-        dtp_grad[branch] = rows(at, wide_rank)[:rank]
-        at += wide_rank
-    for branch in range(2):
-        rate_grad[branch] = rows(at, states)
-        at += states
-    tail = rows(at, 16)
-    for branch in range(2):
-        tap_grad[branch] = tail[branch * taps : (branch + 1) * taps]
-    tapb_grad[...] = tail[2 * taps : 2 * taps + 2]
-    skip_grad[...] = tail[2 * taps + 2 : 2 * taps + 4]
-    dtb_grad[...] = tail[2 * taps + 4 : 2 * taps + 6]
+    for first in range(0, inner, dim):
+        lanes = slice(first, first + dim)
+        for branch in range(2):
+            part = rows(at, wide)
+            xp_grad[branch, :, lanes] = jnp.concatenate([part[:rank], part[wide_rank:]], axis=0)
+            at += wide
+        for branch in range(2):
+            dtp_grad[branch, :, lanes] = rows(at, wide_rank)[:rank]
+            at += wide_rank
+        for branch in range(2):
+            rate_grad[branch, :, lanes] = rows(at, states)
+            at += states
+        tail = rows(at, 16)
+        for branch in range(2):
+            tap_grad[branch, :, lanes] = tail[branch * taps : (branch + 1) * taps]
+        tapb_grad[:, lanes] = tail[2 * taps : 2 * taps + 2]
+        skip_grad[:, lanes] = tail[2 * taps + 2 : 2 * taps + 4]
+        dtb_grad[:, lanes] = tail[2 * taps + 4 : 2 * taps + 6]
+        at += 16
 
     table = factors[...]
     length = table.shape[0]
@@ -755,7 +824,7 @@
         mods = pick(lambda slot: 3 * slot + part)
         lanes = slice(part * dim, (part + 1) * dim)
         grad_ada[:, lanes] = dot_tn(times, mods.astype(BF16))
-        grad_ada_bias[:, lanes] = jnp.sum(mods, axis=0, keepdims=True)
+        grad_ada_bias[lanes] = jnp.sum(mods, axis=0)
         picked = jnp.concatenate([mine[3 * i + part : 3 * i + part + 1] for i in range(slots)], axis=0)
         d_time = d_time + dot_nt(picked.astype(BF16), ada[:, lanes])
     grad_time[...] = d_time * time_sig * (1.0 + time_f * (1.0 - time_sig))
@@ -784,14 +853,7 @@
     runs = lax.axis_size("seq")
     groups = lax.axis_size("dp")
     counts2 = counts[:, None]
-    step3 = timestep[:, None, :]
-    xwt = jnp.swapaxes(x_weight, 1, 2)
-    xwt = jnp.concatenate(
-        [xwt[:, :rank], jnp.zeros((2, wide_rank - rank, inner), BF16), xwt[:, rank:]], axis=1
-    )
-    dtw = jnp.concatenate([dt_weight, jnp.zeros((2, wide_rank - rank, inner), BF16)], axis=1)
-    rate2 = -LOG2E * decay_rate
-    vec = lambda a: a[:, None, :]
+    x_rows = jnp.swapaxes(x_weight, 1, 2)
 
     def item(*block):
         return spec((None,) + block, lambda i: (i,) + (0,) * len(block))
@@ -803,8 +865,8 @@
         functools.partial(enter_kernel, runs),
         grid=(slots,),
         in_specs=[
-            whole(slots, toks, dim), item(toks, dim), whole(slots, toks), whole(1, 1), item(1, dim), whole(dim, 3 * dim),
-            whole(1, 3 * dim), whole(dim, 2 * inner), whole(inner, dim),
+            whole(slots, toks, dim), item(toks, dim), whole(slots, toks), whole(1, 1), whole(slots, dim), whole(dim, 3 * dim),
+            whole(3 * dim), whole(dim, 2 * inner), whole(inner, dim),
         ],
         out_specs=[
             item(2, HALO + toks, inner), item(2, toks, inner), item(toks, inner), item(toks, dim), item(1, 3 * dim),
@@ -823,7 +885,7 @@
         compiler_params=params(collective_id=1, has_side_effects=True),
         name="enter",
     )(
-        tokens, cotangent, token_mask, counts2, step3, ada_weight, ada_bias[None, :], input_weight, output_weight,
+        tokens, cotangent, token_mask, counts2, timestep, ada_weight, ada_bias, input_weight, output_weight,
     )
 
     def unit(*block):
@@ -835,32 +897,36 @@
     def unit_shape(*block, kind=F32):
         return jax.ShapeDtypeStruct((slots, 2) + block, kind)
 
-    act, dsilu, delta, sig, proj, end, back, total, starts, sums, tiles = pl.pallas_call(
+    act, dsilu, delta, sig, proj, end, back, total, starts, sums, tiles, xwt, dtw = pl.pallas_call(
         first_kernel,
         grid=(2, slots),
         in_specs=[
-            unit(HALO + toks, inner), unit(toks, inner), branch(tap_count, inner), branch(1, inner), branch(proj_rows, inner),
-            branch(wide_rank, inner), branch(1, inner), branch(states, inner),
+            unit(HALO + toks, inner), unit(toks, inner), branch(tap_count, inner), whole(2, inner),
+            branch(rank + 2 * states, inner), branch(rank, inner), whole(2, inner), branch(states, inner),
         ],
         out_specs=[
             unit(toks, inner), unit(toks, inner), unit(toks, inner), unit(toks, inner), unit(proj_rows, toks),
             unit(states, inner), unit(states, inner), unit(1, inner), unit(blocks, states, inner), unit(blocks, 1, inner),
-            unit(toks, 2 * states, 128),
+            unit(toks, 2 * states, 128), branch(proj_rows, inner), branch(wide_rank, inner),
         ],
         out_shape=[
             unit_shape(toks, inner, kind=BF16), unit_shape(toks, inner), unit_shape(toks, inner), unit_shape(toks, inner),
             unit_shape(proj_rows, toks), unit_shape(states, inner), unit_shape(states, inner), unit_shape(1, inner),
             unit_shape(blocks, states, inner), unit_shape(blocks, 1, inner), unit_shape(toks, 2 * states, 128),
+            jax.ShapeDtypeStruct((2, proj_rows, inner), BF16), jax.ShapeDtypeStruct((2, wide_rank, inner), BF16),
         ],
         scratch_shapes=[
             pltpu.VMEM((toks, inner), F32), pltpu.VMEM((2, BLK, states, inner), F32), pltpu.VMEM((8, inner), F32),
+            pltpu.VMEM((states, inner), F32), pltpu.VMEM((2 * states * toks, 128), F32),
+            pltpu.VMEM((4 * states, 2 * states * 128), BF16),
         ],
         compiler_params=params(),
         name="first",
-    )(xe, dy, conv_weight, vec(conv_bias), xwt, dtw, vec(dt_bias), rate2)
+    )(xe, dy, conv_weight, conv_bias, x_rows, dt_weight, dt_bias, decay_rate)
 
     pairs = int(math.log2(runs))
     units = 2 * slots
+    span_rows = -(-units // 8) * 8
     vmem = pl.BlockSpec(memory_space=pltpu.VMEM)
     s_in, lam_in = pl.pallas_call(
         functools.partial(exchange_kernel, runs),
@@ -868,15 +934,15 @@
         out_specs=[vmem] * 2,
         out_shape=[unit_shape(states, inner), unit_shape(states, inner)],
         scratch_shapes=[
-            pltpu.VMEM((2, units, states, inner), F32), pltpu.VMEM((2, units, 8, inner), F32),
-            pltpu.VMEM((2, units, states, inner), F32), pltpu.VMEM((2, units, 8, inner), F32),
-            pltpu.VMEM((2 * pairs, units * (states + 16), inner), BF16),
-            pltpu.VMEM((2 * pairs, units * (states + 16), inner), BF16),
+            pltpu.VMEM((2, units, states, inner), F32), pltpu.VMEM((2, span_rows, inner), F32),
+            pltpu.VMEM((2, units, states, inner), F32), pltpu.VMEM((2, span_rows, inner), F32),
+            pltpu.VMEM((2 * pairs, units * states + 2 * span_rows, inner), BF16),
+            pltpu.VMEM((2 * pairs, units * states + 2 * span_rows, inner), BF16),
             pltpu.SemaphoreType.DMA((2 * pairs,)), pltpu.SemaphoreType.DMA((2 * pairs,)),
         ],
         compiler_params=params(collective_id=2, has_side_effects=True),
         name="exchange",
-    )(end, back, total, rate2)
+    )(end, back, total, decay_rate)
 
     rim_spec = spec((None, None, 8, inner), lambda b, i: (b, i, 0, 0))
     y, dx, rims, rate_grad, skip_grad, dtb_grad, dtp_grad, xp_grad, tap_grad, tapb_grad = pl.pallas_call(
@@ -884,10 +950,10 @@
         grid=(2, slots),
         in_specs=[
             unit(states, inner), unit(states, inner), unit(blocks, states, inner),
-            unit(blocks, 1, inner), unit(toks, 2 * states, 128), branch(states, inner), branch(states, inner), unit(HALO + toks, inner), unit(toks, inner),
+            unit(blocks, 1, inner), unit(toks, 2 * states, 128), branch(states, inner), unit(HALO + toks, inner), unit(toks, inner),
             unit(toks, inner), unit(toks, inner), unit(toks, inner), unit(toks, inner), unit(proj_rows, toks),
             branch(proj_rows, inner), branch(wide_rank, inner),
-            branch(tap_count, inner), branch(1, inner),
+            branch(tap_count, inner), whole(2, inner),
         ],
         out_specs=[
             unit(toks, inner), unit(toks, inner), rim_spec, branch(states, inner), branch(1, inner), branch(1, inner),
@@ -899,7 +965,7 @@
             jax.ShapeDtypeStruct((2, rows, inner), F32) for rows in (states, 1, 1, wide_rank, proj_rows, tap_count, 1)
         ],
         scratch_shapes=[
-            pltpu.VMEM((states, inner), F32), pltpu.VMEM((toks + BLK, inner), F32), pltpu.VMEM((toks + BLK, BLK * states), BF16),
+            pltpu.VMEM((states, inner), F32), pltpu.VMEM((states, inner), F32), pltpu.VMEM((toks + BLK, inner), F32), pltpu.VMEM((toks + BLK, BLK * states), BF16),
             pltpu.VMEM((toks, BLK * states), BF16),
             pltpu.VMEM((2, BLK, states, inner), F32),
             pltpu.VMEM((2, (BLK + 1) * states, inner), BF16), pltpu.VMEM((2, BLK * states, inner), BF16),
@@ -911,8 +977,8 @@
         compiler_params=params(),
         name="second",
     )(
-        s_in, lam_in, starts, sums, tiles, rate2, decay_rate, xe, act, dsilu, delta,
-        sig, dy, proj, xwt, dtw, conv_weight, vec(skip_gain),
+        s_in, lam_in, starts, sums, tiles, decay_rate, xe, act, dsilu, delta,
+        sig, dy, proj, xwt, dtw, conv_weight, skip_gain,
     )
 
     mixed, d_tokens, d_mod, out_grad, in_grad = pl.pallas_call(
@@ -942,15 +1008,18 @@
     small = 2 * (proj_rows + wide_rank + states + tap_count) + 8
     rows = reduce_rows(dim, inner, small)
     stages = int(math.log2(runs)) + int(math.log2(groups))
-    result, factors = pl.pallas_call(
+    result, factors, own = pl.pallas_call(
         functools.partial(reduce_kernel, (runs, groups, rows)),
         in_specs=[vmem] * 11,
-        out_specs=[vmem] * 2,
-        out_shape=[jax.ShapeDtypeStruct((rows, inner), BF16), jax.ShapeDtypeStruct((16 * groups, dim), BF16)],
+        out_specs=[vmem] * 3,
+        out_shape=[
+            jax.ShapeDtypeStruct((rows, dim), BF16), jax.ShapeDtypeStruct((16 * groups, dim), BF16),
+            jax.ShapeDtypeStruct((16, dim), BF16),
+        ],
         scratch_shapes=[
-            pltpu.VMEM((rows, inner), F32), pltpu.VMEM((rows + PARTS * LAST_ROWS * stages, inner), BF16),
-            pltpu.VMEM((rows + PARTS * LAST_ROWS * stages, inner), BF16),
-            pltpu.VMEM((rows, inner), BF16), pltpu.VMEM((16, dim), F32),
+            pltpu.VMEM((rows, dim), F32), pltpu.VMEM((rows + PARTS * LAST_ROWS * stages, dim), BF16),
+            pltpu.VMEM((rows + PARTS * LAST_ROWS * stages, dim), BF16),
+            pltpu.VMEM((rows, dim), BF16), pltpu.VMEM((16, dim), F32),
             pltpu.VMEM((max(int(math.log2(runs)), 1), 16, dim), F32), pltpu.VMEM((16 * groups, dim), BF16),
             pltpu.SemaphoreType.DMA((PARTS, 2 * stages)), pltpu.SemaphoreType.DMA((PARTS, 2 * stages)),
             pltpu.SemaphoreType.DMA((stages,)), pltpu.SemaphoreType.DMA((stages,)),
@@ -961,7 +1030,6 @@
         in_grad, out_grad, xp_grad, dtp_grad, rate_grad, tap_grad, tapb_grad, skip_grad, dtb_grad, d_mod, timestep,
     )
 
-    own = lax.dynamic_slice_in_dim(factors, lax.axis_index("dp") * 16, 16, 0)
     (
         d_time, grad_ada, grad_ada_bias, in_grad, tap_grad, tapb_grad, xp_grad, dtp_grad, dtb_grad, rate_grad, skip_grad,
         out_grad,
@@ -972,15 +1040,15 @@
         out_shape=[
             jax.ShapeDtypeStruct(shape, F32)
             for shape in (
-                (slots, dim), (dim, 3 * dim), (1, 3 * dim), (dim, 2 * inner), (2, tap_count, inner), (2, inner),
-                (2, inner, rank + 2 * states), (2, rank, inner), (2, inner), (2, states, inner), (2, inner), (inner, dim),
+                (slots, dim), (dim, 3 * dim), (3 * dim,), (dim, 2 * inner), (2, tap_count, inner), (2, inner),
+                (2, rank + 2 * states, inner), (2, rank, inner), (2, inner), (2, states, inner), (2, inner), (inner, dim),
             )
         ],
         compiler_params=params(),
         name="finish",
     )(result, factors, own, timestep, ada_weight)
     return (
-        mixed, d_tokens, d_time, grad_ada, grad_ada_bias[0], in_grad, tap_grad, tapb_grad, xp_grad, dtp_grad, dtb_grad,
+        mixed, d_tokens, d_time, grad_ada, grad_ada_bias, in_grad, tap_grad, tapb_grad, jnp.swapaxes(xp_grad, 1, 2), dtp_grad, dtb_grad,
         rate_grad, skip_grad, out_grad,
     )
 

time: 240 us -> 217 us (0.904)
  Pallas kernels: 225 us -> 214 us
  local copies, waits for them, and re-layouts: 10.5 us -> 1.84 us
  other arithmetic: 2.72 us -> 0 us
    pallas_call x1, Pallas kernels: 52.6 us -> 44.3 us  [per_device(): pl.pallas_call(functools.partial(reduce_kernel, (runs, groups, rows)), in...]
    broadcast_in_dim x5 -> x0, local copies, waits for them, and re-layouts: 4.37 us -> none  [the longest x3 1.79 us: per_device(): vec = lambda a: a[:, None, :]]
    pallas_call x1, Pallas kernels: 14.7 us -> 11.6 us  [per_device(): pl.pallas_call(functools.partial(exchange_kernel, runs), in_specs=[vmem]...]
where the time goes in v3:
time: 217 us
  Pallas kernels  214 us (99%)
    pallas_call x1, Pallas kernels, per_device(): pl.pallas_call(second_kernel, grid=(2, slots), in_specs=[unit(states, inn...  84.3 us
    pallas_call x1, Pallas kernels, per_device(): pl.pallas_call(functools.partial(reduce_kernel, (runs, groups, rows)), in...  44.3 us
    pallas_call x1, Pallas kernels, per_device(): pl.pallas_call(first_kernel, grid=(2, slots), in_specs=[unit(HALO + toks,...  42.4 us
    pallas_call x1, Pallas kernels, per_device(): pl.pallas_call(functools.partial(third_kernel, runs), grid=(slots,), in_s...  13.9 us
    pallas_call x1, Pallas kernels, per_device(): pl.pallas_call(functools.partial(enter_kernel, runs), grid=(slots,), in_s...  11.8 us
    pallas_call x1, Pallas kernels, per_device(): pl.pallas_call(functools.partial(exchange_kernel, runs), in_specs=[vmem]...  11.6 us
    pallas_call x1, Pallas kernels, per_device(): pl.pallas_call(functools.partial(finish_kernel, (rank, wide_rank)), in_sp...  5.76 us

profile of v3, /device:TPU:0, one launch (start us, length us, event | category | flops | bytes accessed | tf_op | source)
XLA Modules:
  0.0 217.2 jit_solution(6234058255106922247)
XLA Ops:
  1.3 11.8 %enter.1 = (bf16[3,2,272,768]{3,2,1,0:T(8,128)(2,1)}, f32[3,2,256,768]{3,2,1,0:T(8,128)}, f32[3,256,768]{2,1,0:T(8,128)}, bf16[3,256,384]{2,1,0:T(8,128)(2,1)}, f32[3,1,1152]{2,1,0:T(1,128)}) custom-call(bf16[3,256,384]{2,1,0:T(8,128)(2,1)} %tok.3, bf16[3,256,384]{2,1,0:T(8,128)(2,1)} %cot.3, s32[3,256]{1,0:T(4,128)} %mask.3, s32[1,1]{1,0:T(1,128)} %bitcast.3.counts, ...), custom_call_target="tpu_custom_call" | custom-call | tf_op jit(solution)/shard_map/enter/pallas_call | solution.py:864
  13.1 42.4 %first.1 = (bf16[3,2,256,768]{3,2,1,0:T(8,128)(2,1)}, f32[3,2,256,768]{3,2,1,0:T(8,128)}, f32[3,2,256,768]{3,2,1,0:T(8,128)}, f32[3,2,256,768]{3,2,1,0:T(8,128)}...) custom-call(bf16[3,2,272,768]{3,2,1,0:T(8,128)(2,1)} %get-tuple-elem, ...), custom_call_target="tpu_custom_call" | custom-call | tf_op jit(solution)/shard_map/first/pallas_call | solution.py:900
  55.5 11.6 %exchange.1 = (f32[3,2,16,768]{3,2,1,0:T(8,128)}, f32[3,2,16,768]{3,2,1,0:T(8,128)}) custom-call(f32[3,2,16,768]{3,2,1,0:T(8,128)} %get-tuple-element.69.end, f32[3,2,16,768]{3,2,1,0:T(8,128)} %get-tuple-element.70.back, f32[3,2,1,768]{3,2,1,0:T(1,128)} %get-tuple-element.71.total, f32[2,16,768]{2,1,0:T(8,128)} %rate.3), custom_call_target="tpu_custom_call" | custom-call | tf_op jit(solution)/shard_map/exchange/pallas_call | solution.py:931
  67.1 84.3 %second.1 = (f32[3,2,256,768]{3,2,1,0:T(8,128)}, f32[3,2,256,768]{3,2,1,0:T(8,128)}, f32[2,3,8,768]{3,2,1,0:T(8,128)}, f32[2,16,768]{2,1,0:T(8,128)}, f32[2,1,76...) custom-call(f32[3,2,16,768]{3,2,1,0:T(8,128)} %get-tuple-element.72., ...), custom_call_target="tpu_custom_call" | custom-call | tf_op jit(solution)/shard_map/second/pallas_call | solution.py:948
  151.4 13.9 %third.1 = (bf16[3,256,384]{2,1,0:T(8,128)(2,1)}, f32[3,256,384]{2,1,0:T(8,128)}, f32[3,3,384]{2,1,0:T(4,128)}, f32[768,384]{1,0:T(8,128)}, f32[384,1536]{1,0:T(8,128)}) custom-call(bf16[3,256,384]{2,1,0:T(8,128)(2,1)} %tok.3, bf16[3,256,384]{2,1,0:T(8,128)(2,1)} %cot.3, f32[3,1,1152]{2,1,0:T(1,128)} %get-tuple-element.64.mod, s32[3,256]{1,0:T(4,128)} %mask.3, ...), custom_call_target="tpu_custom_call" | custom-call | tf_op jit(solution)/shard_map/third/pallas_call | solution.py:984
  165.3 44.3 %reduce.1 = (bf16[3072,384]{1,0:T(8,128)(2,1)}, bf16[128,384]{1,0:T(8,128)(2,1)}, bf16[16,384]{1,0:T(8,128)(2,1)}) custom-call(f32[384,1536]{1,0:T(8,128)} %get-tuple-element.89.in_grad, f32[768,384]{1,0:T(8,128)} %get-tuple-element.90.out_grad, f32[2,64,768]{2,1,0:T(8,128)} %get-tuple-element.91.xp_grad, f32[2,32,768]{2,1,0:T(8,128)} %get-tuple-element.92.dtp_grad, ...), custom_call_target="tpu_custom_call" | custom-call | tf_op jit(solution)/shard_map/reduce/pallas_call | solution.py:1011
  209.6 0.0 copy-start.1
  209.6 0.0 copy-start
  209.7 5.8 %finish.1 = (f32[3,384]{1,0:T(4,128)}, f32[384,1152]{1,0:T(8,128)}, f32[1152]{0:T(1024)}, f32[384,1536]{1,0:T(8,128)}, f32[2,4,768]{2,1,0:T(4,128)}, /*index=5*/...) custom-call(bf16[3072,384]{1,0:T(8,128)(2,1)} %get-tuple-element.99., ...), custom_call_target="tpu_custom_call" | custom-call | tf_op jit(solution)/shard_map/finish/pallas_call | solution.py:1036
  215.4 0.0 copy-done.1
  215.4 0.8 copy.33
  216.2 0.0 copy-done
  216.2 1.0 copy.34
Async XLA Ops:
  209.6 5.8 %copy-start.1 = (bf16[3,256,384]{2,1,0:T(8,128)(2,1)S(1)}, bf16[3,256,384]{2,1,0:T(8,128)(2,1)}, u32[]{:S(2)}) copy-start(bf16[3,256,384]{2,1,0:T(8,128)(2,1)} %get-tuple-element.128) | copy-start | bytes 1769476
  209.6 6.6 %copy-start = (f32[3,256,384]{2,1,0:T(8,128)S(1)}, f32[3,256,384]{2,1,0:T(8,128)}, u32[]{:S(2)}) copy-start(f32[3,256,384]{2,1,0:T(8,128)} %get-tuple-element.129) | copy-start | bytes 3538948

commit v4 on v3

--- a/solution.py
+++ b/solution.py
@@ -305,9 +305,10 @@
 
 
 def second_kernel(
-    s_in, lam_in, starts, sums, tiles, rate, xe, act, dsilu, delta, sig, dy, proj, xwt, dtw, taps, skip,
-    y_out, dx_out, rim_out, rate_grad, skip_grad, dtb_grad, dtp_grad, xp_grad, tap_grad, tapb_grad,
+    runs, s_in, lam_in, starts, sums, tiles, rate, xe, act, dsilu, delta, sig, dy, proj, xwt, dtw, taps, skip,
+    y_out, dx_out, late_out, rate_grad, skip_grad, dtb_grad, dtp_grad, xp_grad, tap_grad, tapb_grad,
     rate2, carry, dxs, bdiag, cdiag, decay, states_low, lam_low, rq_low, qd_low, dots, racc, gsum, hsum, db, dc,
+    rims, late, send_sem, recv_sem,
 ):
     toks, inner = dy.shape
     states = rate.shape[0]
@@ -315,6 +316,15 @@
     rank = dtw.shape[0]
     tap_count = taps.shape[0]
     item = pl.program_id(1)
+    last_item = item == pl.num_programs(1) - 1
+    me = lax.axis_index("seq")
+    downs = [(rims.at[0], late.at[0], send_sem.at[0], recv_sem.at[0])]
+    ups = [(rims.at[1], late.at[1], send_sem.at[1], recv_sem.at[1])]
+
+    @pl.when((item == 0) & (pl.program_id(0) == 0))
+    def _():
+        greet_line(me, runs)
+
     gain = skip[pl.ds(pl.program_id(0), 1), :]
     rate2[...] = rate[...] * -LOG2E
     width = BLK * states
@@ -425,35 +435,39 @@
         moved = pltpu.roll(moved, window - 1, 0)
         tap_grad[k : k + 1, :] += jnp.sum(moved * x_f, axis=0, keepdims=True)
         d_window = d_window + taps[k : k + 1, :] * moved
-    rim_out[...] = d_window[HALO - 8 : HALO]
+    rims[pl.program_id(0), item] = d_window[HALO - 8 : HALO]
     dx_out[...] = d_window[HALO:]
 
+    @pl.when(last_item & (pl.program_id(0) == 0))
+    def _():
+        swap_along_line(me, runs, [], downs, True)
+
+    @pl.when(last_item & (pl.program_id(0) == 1))
+    def _():
+        swap_along_line(me, runs, ups, [], True)
+        swap_along_line(me, runs, ups, downs, False)
+
+        @pl.when(me == 0)
+        def _():
+            late[1] = jnp.zeros(late.shape[1:], F32)
+
+        @pl.when(me == runs - 1)
+        def _():
+            late[0] = jnp.zeros(late.shape[1:], F32)
+
+        late_out[...] = late[...]
+
 
 def third_kernel(
-    runs, tok, cot, mod, mask, counts, hid, z_in, y, dx, rims, win, wout,
+    tok, cot, mod, mask, counts, hid, z_in, y, dx, late, win, wout,
     mixed, d_tokens, d_mod, out_grad, in_grad,
-    late_up, late_down, send_sem, recv_sem,
 ):
     dim = tok.shape[-1]
     toks, inner = z_in.shape
-    me = lax.axis_index("seq")
     i = pl.program_id(0)
-    ups = [(rims.at[1], late_up, send_sem.at[0], recv_sem.at[0])]
-    downs = [(rims.at[0], late_down, send_sem.at[1], recv_sem.at[1])]
 
     @pl.when(i == 0)
     def _():
-        greet_line(me, runs)
-        swap_along_line(me, runs, ups, downs, True)
-
-        @pl.when(me == 0)
-        def _():
-            late_up[...] = jnp.zeros(late_up.shape, F32)
-
-        @pl.when(me == runs - 1)
-        def _():
-            late_down[...] = jnp.zeros(late_down.shape, F32)
-
         out_grad[...] = jnp.zeros(out_grad.shape, F32)
         in_grad[...] = jnp.zeros(in_grad.shape, F32)
 
@@ -473,16 +487,12 @@
     d_zgate = d_gated * summed * z_sig * (1.0 + z * (1.0 - z_sig))
     out_grad[...] += dot_tn(gated, d_branch)
 
-    @pl.when(i == 0)
-    def _():
-        swap_along_line(me, runs, ups, downs, False)
-
-    edge = late_up.shape[1]
+    edge = late.shape[2]
 
     def with_late(part, extra):
         return jnp.concatenate([part[: toks - edge], part[toks - edge :] + extra], axis=0)
 
-    d_x = with_late(dx[0], late_down[i]) + flip_full(with_late(dx[1], late_up[i]))
+    d_x = with_late(dx[0], late[0, i]) + flip_full(with_late(dx[1], late[1, i]))
     d_xz = (jnp.concatenate([d_x, d_zgate], axis=1) * valid).astype(BF16)
     d_hidden = dot_nt(d_xz, win[...])
     in_grad[...] += dot_tn(hid[...], d_xz)
@@ -944,9 +954,8 @@
         name="exchange",
     )(end, back, total, decay_rate)
 
-    rim_spec = spec((None, None, 8, inner), lambda b, i: (b, i, 0, 0))
-    y, dx, rims, rate_grad, skip_grad, dtb_grad, dtp_grad, xp_grad, tap_grad, tapb_grad = pl.pallas_call(
-        second_kernel,
+    y, dx, late, rate_grad, skip_grad, dtb_grad, dtp_grad, xp_grad, tap_grad, tapb_grad = pl.pallas_call(
+        functools.partial(second_kernel, runs),
         grid=(2, slots),
         in_specs=[
             unit(states, inner), unit(states, inner), unit(blocks, states, inner),
@@ -956,7 +965,7 @@
             branch(tap_count, inner), whole(2, inner),
         ],
         out_specs=[
-            unit(toks, inner), unit(toks, inner), rim_spec, branch(states, inner), branch(1, inner), branch(1, inner),
+            unit(toks, inner), unit(toks, inner), whole(2, slots, 8, inner), branch(states, inner), branch(1, inner), branch(1, inner),
             branch(wide_rank, inner), branch(proj_rows, inner), branch(tap_count, inner), branch(1, inner),
         ],
         out_shape=[
@@ -973,8 +982,10 @@
             pltpu.VMEM((2, BLK * states, 256), BF16), pltpu.VMEM((states, inner), F32),
             pltpu.VMEM((toks + BLK, inner), F32), pltpu.VMEM((toks + BLK, inner), F32),
             pltpu.VMEM((toks + BLK, BLK * states), BF16), pltpu.VMEM((toks + BLK, BLK * states), BF16),
-        ],
-        compiler_params=params(),
+            pltpu.VMEM((2, slots, 8, inner), F32), pltpu.VMEM((2, slots, 8, inner), F32),
+            pltpu.SemaphoreType.DMA((2,)), pltpu.SemaphoreType.DMA((2,)),
+        ],
+        compiler_params=params(collective_id=3, has_side_effects=True),
         name="second",
     )(
         s_in, lam_in, starts, sums, tiles, decay_rate, xe, act, dsilu, delta,
@@ -982,7 +993,7 @@
     )
 
     mixed, d_tokens, d_mod, out_grad, in_grad = pl.pallas_call(
-        functools.partial(third_kernel, runs),
+        third_kernel,
         grid=(slots,),
         in_specs=[
             item(toks, dim), item(toks, dim), item(1, 3 * dim), whole(slots, toks), whole(1, 1), item(toks, dim),
@@ -995,14 +1006,10 @@
             jax.ShapeDtypeStruct((slots, 3, dim), F32), jax.ShapeDtypeStruct((inner, dim), F32),
             jax.ShapeDtypeStruct((dim, 2 * inner), F32),
         ],
-        scratch_shapes=[
-            pltpu.VMEM((slots, 8, inner), F32), pltpu.VMEM((slots, 8, inner), F32), pltpu.SemaphoreType.DMA((2,)),
-            pltpu.SemaphoreType.DMA((2,)),
-        ],
-        compiler_params=params(collective_id=3, has_side_effects=True),
+        compiler_params=params(),
         name="third",
     )(
-        tokens, cotangent, modulate, token_mask, counts2, hid, z_gate, y, dx, rims, input_weight, output_weight,
+        tokens, cotangent, modulate, token_mask, counts2, hid, z_gate, y, dx, late, input_weight, output_weight,
     )
 
     small = 2 * (proj_rows + wide_rank + states + tap_count) + 8

time: 217 us -> 218 us (level)
  no operation moved by 1% of the time
where the time goes in v4:
time: 218 us; the launch traced here: 217 us
  Pallas kernels  216 us (99%)
    pallas_call x1, Pallas kernels, per_device(): pl.pallas_call(functools.partial(second_kernel, runs), grid=(2, slots), i...  86 us
    pallas_call x1, Pallas kernels, per_device(): pl.pallas_call(functools.partial(reduce_kernel, (runs, groups, rows)), in...  46.1 us
    pallas_call x1, Pallas kernels, per_device(): pl.pallas_call(first_kernel, grid=(2, slots), in_specs=[unit(HALO + toks,...  42.5 us
    pallas_call x1, Pallas kernels, per_device(): pl.pallas_call(third_kernel, grid=(slots,), in_specs=[item(toks, dim), it...  12.4 us
    pallas_call x1, Pallas kernels, per_device(): pl.pallas_call(functools.partial(enter_kernel, runs), grid=(slots,), in_s...  11.8 us
    pallas_call x1, Pallas kernels, per_device(): pl.pallas_call(functools.partial(exchange_kernel, runs), in_specs=[vmem]...  11.6 us
    pallas_call x1, Pallas kernels, per_device(): pl.pallas_call(functools.partial(finish_kernel, (rank, wide_rank)), in_sp...  5.65 us

profile of v4, /device:TPU:0, one launch (start us, length us, event | category | flops | bytes accessed | tf_op | source)
XLA Modules:
  0.0 217.3 jit_solution(7732407124709735477)
XLA Ops:
  1.3 11.8 %enter.1 = (bf16[3,2,272,768]{3,2,1,0:T(8,128)(2,1)}, f32[3,2,256,768]{3,2,1,0:T(8,128)}, f32[3,256,768]{2,1,0:T(8,128)}, bf16[3,256,384]{2,1,0:T(8,128)(2,1)}, f32[3,1,1152]{2,1,0:T(1,128)}) custom-call(bf16[3,256,384]{2,1,0:T(8,128)(2,1)} %tok.3, bf16[3,256,384]{2,1,0:T(8,128)(2,1)} %cot.3, s32[3,256]{1,0:T(4,128)} %mask.3, s32[1,1]{1,0:T(1,128)} %bitcast.3.counts, ...), custom_call_target="tpu_custom_call" | custom-call | tf_op jit(solution)/shard_map/enter/pallas_call | solution.py:874
  13.1 42.5 %first.1 = (bf16[3,2,256,768]{3,2,1,0:T(8,128)(2,1)}, f32[3,2,256,768]{3,2,1,0:T(8,128)}, f32[3,2,256,768]{3,2,1,0:T(8,128)}, f32[3,2,256,768]{3,2,1,0:T(8,128)}...) custom-call(bf16[3,2,272,768]{3,2,1,0:T(8,128)(2,1)} %get-tuple-elem, ...), custom_call_target="tpu_custom_call" | custom-call | tf_op jit(solution)/shard_map/first/pallas_call | solution.py:910
  55.6 11.6 %exchange.1 = (f32[3,2,16,768]{3,2,1,0:T(8,128)}, f32[3,2,16,768]{3,2,1,0:T(8,128)}) custom-call(f32[3,2,16,768]{3,2,1,0:T(8,128)} %get-tuple-element.69.end, f32[3,2,16,768]{3,2,1,0:T(8,128)} %get-tuple-element.70.back, f32[3,2,1,768]{3,2,1,0:T(1,128)} %get-tuple-element.71.total, f32[2,16,768]{2,1,0:T(8,128)} %rate.3), custom_call_target="tpu_custom_call" | custom-call | tf_op jit(solution)/shard_map/exchange/pallas_call | solution.py:941
  67.2 86.0 %second.1 = (f32[3,2,256,768]{3,2,1,0:T(8,128)}, f32[3,2,256,768]{3,2,1,0:T(8,128)}, f32[2,3,8,768]{3,2,1,0:T(8,128)}, f32[2,16,768]{2,1,0:T(8,128)}, f32[2,1,76...) custom-call(f32[3,2,16,768]{3,2,1,0:T(8,128)} %get-tuple-element.72., ...), custom_call_target="tpu_custom_call" | custom-call | tf_op jit(solution)/shard_map/second/pallas_call | solution.py:957
  153.2 12.4 %third.1 = (bf16[3,256,384]{2,1,0:T(8,128)(2,1)}, f32[3,256,384]{2,1,0:T(8,128)}, f32[3,3,384]{2,1,0:T(4,128)}, f32[768,384]{1,0:T(8,128)}, f32[384,1536]{1,0:T(8,128)}) custom-call(bf16[3,256,384]{2,1,0:T(8,128)(2,1)} %tok.3, bf16[3,256,384]{2,1,0:T(8,128)(2,1)} %cot.3, f32[3,1,1152]{2,1,0:T(1,128)} %get-tuple-element.64.mod, s32[3,256]{1,0:T(4,128)} %mask.3, ...), custom_call_target="tpu_custom_call" | custom-call | tf_op jit(solution)/shard_map/third/pallas_call | solution.py:995
  165.6 46.1 %reduce.1 = (bf16[3072,384]{1,0:T(8,128)(2,1)}, bf16[128,384]{1,0:T(8,128)(2,1)}, bf16[16,384]{1,0:T(8,128)(2,1)}) custom-call(f32[384,1536]{1,0:T(8,128)} %get-tuple-element.89.in_grad, f32[768,384]{1,0:T(8,128)} %get-tuple-element.90.out_grad, f32[2,64,768]{2,1,0:T(8,128)} %get-tuple-element.91.xp_grad, f32[2,32,768]{2,1,0:T(8,128)} %get-tuple-element.92.dtp_grad, ...), custom_call_target="tpu_custom_call" | custom-call | tf_op jit(solution)/shard_map/reduce/pallas_call | solution.py:1018
  211.7 5.6 %finish.1 = (f32[3,384]{1,0:T(4,128)}, f32[384,1152]{1,0:T(8,128)}, f32[1152]{0:T(1024)}, f32[384,1536]{1,0:T(8,128)}, f32[2,4,768]{2,1,0:T(4,128)}, /*index=5*/...) custom-call(bf16[3072,384]{1,0:T(8,128)(2,1)} %get-tuple-element.99., ...), custom_call_target="tpu_custom_call" | custom-call | tf_op jit(solution)/shard_map/finish/pallas_call | solution.py:1043

commit v5 on v4

--- a/solution.py
+++ b/solution.py
@@ -76,8 +76,10 @@
     pl.semaphore_wait(barrier, len(targets))
 
 
-def greet_line(me, runs):
+def greet_line(me, runs, others=()):
     barrier = pltpu.get_barrier_semaphore()
+    for target in others:
+        pl.semaphore_signal(barrier, inc=1, device_id=target, device_id_type=MESH)
 
     @pl.when(me > 0)
     def _():
@@ -88,7 +90,7 @@
         pl.semaphore_signal(barrier, inc=1, device_id={"seq": me + 1}, device_id_type=MESH)
 
     neighbours = (me + runs - 1) // runs + (2 * runs - 2 - me) // runs
-    pl.semaphore_wait(barrier, neighbours)
+    pl.semaphore_wait(barrier, neighbours + len(others))
 
 
 def swap_along_line(me, runs, ups, downs, start):
@@ -225,19 +227,140 @@
     return jnp.maximum(pre, 0.0) + more, jax.nn.sigmoid(pre)
 
 
+def bit_of(index, bit):
+    return (index // (1 << bit)) % 2
+
+
+def across(axis, bit):
+    me = lax.axis_index(axis)
+    mine = bit_of(me, bit)
+    return mine, {axis: me + (1 - 2 * mine) * (1 << bit)}
+
+
+class Exchange:
+    def __init__(self, runs, branch, ends, backs, totals, rate, results, group, span, pre, pre_span, sends, arrivals, sems):
+        self.branch, self.rate = branch, rate
+        self.sources, self.totals, self.results = (ends, backs), totals, results
+        self.group, self.span, self.pre, self.pre_span = group, span, pre, pre_span
+        self.sends, self.arrivals, self.sems = sends, arrivals, sems
+        self.links = [across("seq", bit) for bit in range(int(math.log2(runs)))]
+        self.slots, self.states, self.inner = ends.shape
+
+    def flow(self, kind):
+        return kind if self.branch == 0 else 1 - kind
+
+    def targets(self):
+        return [target for _, target in self.links]
+
+    def copy(self, stage, kind):
+        at = 2 * stage + kind
+        return remote(
+            self.sends.at[at], self.arrivals.at[at], self.sems.at[0, at], self.sems.at[1, at], self.links[stage][1]
+        )
+
+    def send(self, stage, kind):
+        rows = self.slots * self.states
+        at = 2 * stage + kind
+        for i in range(self.slots):
+            self.sends[at, i * self.states : (i + 1) * self.states, :] = self.group[kind, i].astype(BF16)
+        high = self.span[kind].astype(BF16).astype(F32)
+        self.sends[at, rows:, :] = jnp.concatenate([high, self.span[kind] - high], axis=0).astype(BF16)
+        self.copy(stage, kind).start()
+
+    def join(self, stage, kind, last):
+        mine = self.links[stage][0]
+        self.copy(stage, kind).wait()
+        at = 2 * stage + kind
+        earlier = (mine == 1) if self.flow(kind) == 0 else (mine == 0)
+        both = self.arrivals[at, self.slots * self.states :, :].astype(F32)
+        length = both[: both.shape[0] // 2] + both[both.shape[0] // 2 :]
+        own_span, pre_span = self.span[kind], self.pre_span[kind]
+        second_span = jnp.where(earlier, own_span, length)
+        rate = self.rate[...] * -LOG2E
+        for i in range(self.slots):
+            state = self.arrivals[at, i * self.states : (i + 1) * self.states, :].astype(F32)
+            before = self.pre[kind, i]
+            self.pre[kind, i] = jnp.where(earlier, state * jnp.exp2(rate * pre_span[i : i + 1]) + before, before)
+            if not last:
+                own = self.group[kind, i]
+                first, second = jnp.where(earlier, state, own), jnp.where(earlier, own, state)
+                self.group[kind, i] = first * jnp.exp2(rate * second_span[i : i + 1]) + second
+        self.pre_span[kind] = jnp.where(earlier, length + pre_span, pre_span)
+        if not last:
+            self.span[kind] = own_span + length
+
+    def points(self):
+        count = len(self.links)
+
+        def begin():
+            self.pre[...] = jnp.zeros(self.pre.shape, F32)
+            self.pre_span[...] = jnp.zeros(self.pre_span.shape, F32)
+            self.span[...] = jnp.zeros(self.span.shape, F32)
+            for kind in range(2):
+                for i in range(self.slots):
+                    self.group[kind, i] = self.sources[kind][i]
+                    self.span[kind, i : i + 1, :] = self.totals[i]
+                if count:
+                    self.send(0, kind)
+
+        def step(stage):
+            last = stage == count - 1
+            for kind in range(2):
+                self.join(stage, kind, last)
+                if not last:
+                    self.send(stage + 1, kind)
+
+        def end():
+            for kind in range(2):
+                for i in range(self.slots):
+                    self.results[kind][i] = self.pre[kind, i]
+
+        return [begin] + [functools.partial(step, stage) for stage in range(count)] + [end]
+
+
+def exchange_shapes(runs, slots, states, inner):
+    pairs = max(int(math.log2(runs)), 1)
+    span_rows = -(-slots // 8) * 8
+    return [
+        pltpu.VMEM((2, slots, states, inner), F32), pltpu.VMEM((2, span_rows, inner), F32),
+        pltpu.VMEM((2, slots, states, inner), F32), pltpu.VMEM((2, span_rows, inner), F32),
+        pltpu.VMEM((2 * pairs, slots * states + 2 * span_rows, inner), BF16),
+        pltpu.VMEM((2 * pairs, slots * states + 2 * span_rows, inner), BF16),
+        pltpu.SemaphoreType.DMA((2, 2 * pairs)),
+    ]
+
+
+def beside(points, step, first, count):
+    for at in range(min(len(points), count)):
+        todo = points[at:] if at == count - 1 else points[at : at + 1]
+
+        @pl.when(step == first + at)
+        def _():
+            for point in todo:
+                point()
+
+
 def first_kernel(
-    xe, dy, taps, tap_bias, x_rows, dt_rows, dt_bias, rate,
-    act_out, dsilu_out, delta_out, sig_out, proj_out, end_out, back_out, total_out, starts_out, sums_out, tiles, xwt, dtw,
-    dx, decay, through, rate2, wide, picks,
+    runs, slots, xe, dy, taps, tap_bias, x_rows, dt_rows, dt_bias, rate,
+    act_out, dsilu_out, delta_out, sig_out, proj_out, end_out, back_out, total_out, starts_out, sums_out, tiles, xwt, dtw, s_in, lam_in,
+    dx, decay, through, rate2, wide, picks, ends, backs, totals, first_rate, *exchange_scratch,
 ):
     toks, inner = dy.shape
     states = rate.shape[0]
     blocks = toks // BLK
     rank = dtw.shape[0]
     tap_count = taps.shape[0]
-    branch = pl.program_id(0)
-
-    @pl.when(pl.program_id(1) == 0)
+    branch, item = pl.program_id(0), pl.program_id(1)
+    exchange = Exchange(runs, 0, ends, backs, totals, first_rate, (s_in, lam_in), *exchange_scratch)
+
+    @pl.when((branch == 0) & (item == 0))
+    def _():
+        greet(exchange.targets())
+        first_rate[...] = rate[...]
+
+    beside(exchange.points(), branch * slots + item, slots, slots)
+
+    @pl.when(item == 0)
     def _():
         rate2[...] = rate[...] * -LOG2E
         picks[...] = (
@@ -303,12 +426,18 @@
     lax.fori_loop(0, blocks // 2, block_step, 0)
     total_out[...] = through[:1, :]
 
+    @pl.when(branch == 0)
+    def _():
+        ends[item] = end_out[...]
+        backs[item] = back_out[...]
+        totals[item] = through[:1, :]
+
 
 def second_kernel(
-    runs, s_in, lam_in, starts, sums, tiles, rate, xe, act, dsilu, delta, sig, dy, proj, xwt, dtw, taps, skip,
+    runs, s_first, lam_first, ends, backs, totals, last_rate, starts, sums, tiles, rate, xe, act, dsilu, delta, sig, dy, proj, xwt, dtw, taps, skip,
     y_out, dx_out, late_out, rate_grad, skip_grad, dtb_grad, dtp_grad, xp_grad, tap_grad, tapb_grad,
     rate2, carry, dxs, bdiag, cdiag, decay, states_low, lam_low, rq_low, qd_low, dots, racc, gsum, hsum, db, dc,
-    rims, late, send_sem, recv_sem,
+    rims, late, send_sem, recv_sem, s_in, s_last, lam_last, *exchange_scratch,
 ):
     toks, inner = dy.shape
     states = rate.shape[0]
@@ -321,9 +450,25 @@
     downs = [(rims.at[0], late.at[0], send_sem.at[0], recv_sem.at[0])]
     ups = [(rims.at[1], late.at[1], send_sem.at[1], recv_sem.at[1])]
 
-    @pl.when((item == 0) & (pl.program_id(0) == 0))
-    def _():
-        greet_line(me, runs)
+    branch = pl.program_id(0)
+    slots = ends.shape[0]
+    exchange = Exchange(runs, 1, ends, backs, totals, last_rate, (s_last, lam_last), *exchange_scratch)
+
+    @pl.when((item == 0) & (branch == 0))
+    def _():
+        greet_line(me, runs, exchange.targets())
+
+    beside(exchange.points(), branch * slots + item, 0, slots)
+
+    @pl.when(branch == 0)
+    def _():
+        s_in[...] = s_first[item]
+        carry[...] = lam_first[item]
+
+    @pl.when(branch == 1)
+    def _():
+        s_in[...] = s_last[item]
+        carry[...] = lam_last[item]
 
     gain = skip[pl.ds(pl.program_id(0), 1), :]
     rate2[...] = rate[...] * -LOG2E
@@ -334,7 +479,6 @@
         for ref in (rate_grad, skip_grad, dtb_grad, dtp_grad, xp_grad, tap_grad, tapb_grad):
             ref[...] = jnp.zeros(ref.shape, ref.dtype)
 
-    carry[...] = lam_in[...]
     act_low = act[...]
     dxs[:toks, :] = delta[...] * act_low.astype(F32)
     fold = (
@@ -505,106 +649,6 @@
         - jnp.mean(d_normed, axis=-1, keepdims=True)
         - normed * jnp.mean(d_normed * normed, axis=-1, keepdims=True)
     )
-
-
-def bit_of(index, bit):
-    return (index // (1 << bit)) % 2
-
-
-def across(axis, bit):
-    me = lax.axis_index(axis)
-    mine = bit_of(me, bit)
-    return mine, {axis: me + (1 - 2 * mine) * (1 << bit)}
-
-
-def exchange_kernel(runs, end, back, total, rates, s_in, lam_in, group, span, pre, pre_span, sends, arrivals, send_sem, recv_sem):
-    slots, _, states, inner = end.shape
-    bits = int(math.log2(runs))
-    links = [across("seq", bit) for bit in range(bits)]
-    greet([target for _, target in links])
-    flows = (((end, 0), (back, 1)), ((end, 1), (back, 0)))
-    units = 2 * slots
-    rows = units * states
-    pre[...] = jnp.zeros(pre.shape, F32)
-    pre_span[...] = jnp.zeros(pre_span.shape, F32)
-    span[...] = jnp.zeros(span.shape, F32)
-    for flow in range(2):
-        for kind, (array, branch) in enumerate(flows[flow]):
-            for i in range(slots):
-                unit = kind * slots + i
-                group[flow, unit] = array[i, branch]
-                span[flow, unit : unit + 1, :] = total[i, branch]
-
-    def load(flow, slot):
-        for unit in range(units):
-            sends[slot, unit * states : (unit + 1) * states, :] = group[flow, unit].astype(BF16)
-        high = span[flow].astype(BF16).astype(F32)
-        sends[slot, rows:, :] = jnp.concatenate([high, span[flow] - high], axis=0).astype(BF16)
-
-    def join(flow, slot, earlier, last):
-        both = arrivals[slot, rows:, :].astype(F32)
-        length = both[: both.shape[0] // 2] + both[both.shape[0] // 2 :]
-        own_span = span[flow]
-        mine_span = pre_span[flow]
-        second_span = jnp.where(earlier, own_span, length)
-        for unit in range(units):
-            rate = rates[flows[flow][unit // slots][1]] * -LOG2E
-            state = arrivals[slot, unit * states : (unit + 1) * states, :].astype(F32)
-            mine = pre[flow, unit]
-            joined = state * jnp.exp2(rate * mine_span[unit : unit + 1]) + mine
-            pre[flow, unit] = jnp.where(earlier, joined, mine)
-            if not last:
-                own = group[flow, unit]
-                first = jnp.where(earlier, state, own)
-                second = jnp.where(earlier, own, state)
-                group[flow, unit] = first * jnp.exp2(rate * second_span[unit : unit + 1]) + second
-        pre_span[flow] = jnp.where(earlier, length + mine_span, mine_span)
-        if not last:
-            span[flow] = own_span + length
-
-    for stage, (mine, target) in enumerate(links):
-        last = stage == bits - 1
-        if last:
-            slot = 2 * stage
-
-            @pl.when(mine == 0)
-            def _():
-                load(0, slot)
-
-            @pl.when(mine == 1)
-            def _():
-                load(1, slot)
-
-            copies = [remote(sends.at[slot], arrivals.at[slot], send_sem.at[slot], recv_sem.at[slot], target)]
-        else:
-            copies = []
-            for flow in range(2):
-                slot = 2 * stage + flow
-                load(flow, slot)
-                copies.append(
-                    remote(sends.at[slot], arrivals.at[slot], send_sem.at[slot], recv_sem.at[slot], target)
-                )
-        for copy in copies:
-            copy.start()
-        for copy in copies:
-            copy.wait()
-        if last:
-
-            @pl.when(mine == 1)
-            def _():
-                join(0, 2 * stage, True, True)
-
-            @pl.when(mine == 0)
-            def _():
-                join(1, 2 * stage, True, True)
-        else:
-            join(0, 2 * stage, mine == 1, False)
-            join(1, 2 * stage + 1, mine == 0, False)
-    for flow in range(2):
-        for kind, (_, branch) in enumerate(flows[flow]):
-            result = (s_in, lam_in)[kind]
-            for i in range(slots):
-                result[i, branch] = pre[flow, kind * slots + i]
 
 
 PARTS = 6
@@ -907,8 +951,8 @@
     def unit_shape(*block, kind=F32):
         return jax.ShapeDtypeStruct((slots, 2) + block, kind)
 
-    act, dsilu, delta, sig, proj, end, back, total, starts, sums, tiles, xwt, dtw = pl.pallas_call(
-        first_kernel,
+    act, dsilu, delta, sig, proj, end, back, total, starts, sums, tiles, xwt, dtw, s_first, lam_first = pl.pallas_call(
+        functools.partial(first_kernel, runs, slots),
         grid=(2, slots),
         in_specs=[
             unit(HALO + toks, inner), unit(toks, inner), branch(tap_count, inner), whole(2, inner),
@@ -918,48 +962,37 @@
             unit(toks, inner), unit(toks, inner), unit(toks, inner), unit(toks, inner), unit(proj_rows, toks),
             unit(states, inner), unit(states, inner), unit(1, inner), unit(blocks, states, inner), unit(blocks, 1, inner),
             unit(toks, 2 * states, 128), branch(proj_rows, inner), branch(wide_rank, inner),
+            whole(slots, states, inner), whole(slots, states, inner),
         ],
         out_shape=[
             unit_shape(toks, inner, kind=BF16), unit_shape(toks, inner), unit_shape(toks, inner), unit_shape(toks, inner),
             unit_shape(proj_rows, toks), unit_shape(states, inner), unit_shape(states, inner), unit_shape(1, inner),
             unit_shape(blocks, states, inner), unit_shape(blocks, 1, inner), unit_shape(toks, 2 * states, 128),
             jax.ShapeDtypeStruct((2, proj_rows, inner), BF16), jax.ShapeDtypeStruct((2, wide_rank, inner), BF16),
+            jax.ShapeDtypeStruct((slots, states, inner), F32), jax.ShapeDtypeStruct((slots, states, inner), F32),
         ],
         scratch_shapes=[
             pltpu.VMEM((toks, inner), F32), pltpu.VMEM((2, BLK, states, inner), F32), pltpu.VMEM((8, inner), F32),
             pltpu.VMEM((states, inner), F32), pltpu.VMEM((2 * states * toks, 128), F32),
-            pltpu.VMEM((4 * states, 2 * states * 128), BF16),
-        ],
-        compiler_params=params(),
+            pltpu.VMEM((4 * states, 2 * states * 128), BF16), pltpu.VMEM((slots, states, inner), F32),
+            pltpu.VMEM((slots, states, inner), F32), pltpu.VMEM((slots, 1, inner), F32), pltpu.VMEM((states, inner), F32),
+            *exchange_shapes(runs, slots, states, inner),
+        ],
+        compiler_params=params(collective_id=2, has_side_effects=True),
         name="first",
     )(xe, dy, conv_weight, conv_bias, x_rows, dt_weight, dt_bias, decay_rate)
 
-    pairs = int(math.log2(runs))
-    units = 2 * slots
-    span_rows = -(-units // 8) * 8
     vmem = pl.BlockSpec(memory_space=pltpu.VMEM)
-    s_in, lam_in = pl.pallas_call(
-        functools.partial(exchange_kernel, runs),
-        in_specs=[vmem] * 4,
-        out_specs=[vmem] * 2,
-        out_shape=[unit_shape(states, inner), unit_shape(states, inner)],
-        scratch_shapes=[
-            pltpu.VMEM((2, units, states, inner), F32), pltpu.VMEM((2, span_rows, inner), F32),
-            pltpu.VMEM((2, units, states, inner), F32), pltpu.VMEM((2, span_rows, inner), F32),
-            pltpu.VMEM((2 * pairs, units * states + 2 * span_rows, inner), BF16),
-            pltpu.VMEM((2 * pairs, units * states + 2 * span_rows, inner), BF16),
-            pltpu.SemaphoreType.DMA((2 * pairs,)), pltpu.SemaphoreType.DMA((2 * pairs,)),
-        ],
-        compiler_params=params(collective_id=2, has_side_effects=True),
-        name="exchange",
-    )(end, back, total, decay_rate)
+    last = spec((slots, None, states, inner), lambda b, i: (0, 1, 0, 0))
+    last_total = spec((slots, None, 1, inner), lambda b, i: (0, 1, 0, 0))
+    last_branch = spec((None, states, inner), lambda b, i: (1, 0, 0))
 
     y, dx, late, rate_grad, skip_grad, dtb_grad, dtp_grad, xp_grad, tap_grad, tapb_grad = pl.pallas_call(
         functools.partial(second_kernel, runs),
         grid=(2, slots),
         in_specs=[
-            unit(states, inner), unit(states, inner), unit(blocks, states, inner),
-            unit(blocks, 1, inner), unit(toks, 2 * states, 128), branch(states, inner), unit(HALO + toks, inner), unit(toks, inner),
+            whole(slots, states, inner), whole(slots, states, inner), last, last, last_total, last_branch,
+            unit(blocks, states, inner), unit(blocks, 1, inner), unit(toks, 2 * states, 128), branch(states, inner), unit(HALO + toks, inner), unit(toks, inner),
             unit(toks, inner), unit(toks, inner), unit(toks, inner), unit(toks, inner), unit(proj_rows, toks),
             branch(proj_rows, inner), branch(wide_rank, inner),
             branch(tap_count, inner), whole(2, inner),
@@ -983,12 +1016,14 @@
             pltpu.VMEM((toks + BLK, inner), F32), pltpu.VMEM((toks + BLK, inner), F32),
             pltpu.VMEM((toks + BLK, BLK * states), BF16), pltpu.VMEM((toks + BLK, BLK * states), BF16),
             pltpu.VMEM((2, slots, 8, inner), F32), pltpu.VMEM((2, slots, 8, inner), F32),
-            pltpu.SemaphoreType.DMA((2,)), pltpu.SemaphoreType.DMA((2,)),
+            pltpu.SemaphoreType.DMA((2,)), pltpu.SemaphoreType.DMA((2,)), pltpu.VMEM((states, inner), F32),
+            pltpu.VMEM((slots, states, inner), F32), pltpu.VMEM((slots, states, inner), F32),
+            *exchange_shapes(runs, slots, states, inner),
         ],
         compiler_params=params(collective_id=3, has_side_effects=True),
         name="second",
     )(
-        s_in, lam_in, starts, sums, tiles, decay_rate, xe, act, dsilu, delta,
+        s_first, lam_first, end, back, total, decay_rate, starts, sums, tiles, decay_rate, xe, act, dsilu, delta,
         sig, dy, proj, xwt, dtw, conv_weight, skip_gain,
     )
 

time: 218 us -> 204 us (0.936)
  Pallas kernels: 216 us -> 202 us
    pallas_call x2 -> x1, Pallas kernels: 54.1 us -> 45.2 us  [per_device(): pl.pallas_call(functools.partial(first_kernel, runs, slots), grid=(2, slo...]
    pallas_call x1, Pallas kernels: 86 us -> 82.7 us  [per_device(): pl.pallas_call(functools.partial(second_kernel, runs), grid=(2, slots), i...]
where the time goes in v5:
time: 204 us
  Pallas kernels  202 us (99%)
    pallas_call x1, Pallas kernels, per_device(): pl.pallas_call(functools.partial(second_kernel, runs), grid=(2, slots), i...  82.7 us
    pallas_call x1, Pallas kernels, per_device(): pl.pallas_call(functools.partial(first_kernel, runs, slots), grid=(2, slo...  45.2 us
    pallas_call x1, Pallas kernels, per_device(): pl.pallas_call(functools.partial(reduce_kernel, (runs, groups, rows)), in...  44.6 us
    pallas_call x1, Pallas kernels, per_device(): pl.pallas_call(third_kernel, grid=(slots,), in_specs=[item(toks, dim), it...  12.4 us
    pallas_call x1, Pallas kernels, per_device(): pl.pallas_call(functools.partial(enter_kernel, runs), grid=(slots,), in_s...  11.9 us
    pallas_call x1, Pallas kernels, per_device(): pl.pallas_call(functools.partial(finish_kernel, (rank, wide_rank)), in_sp...  5.65 us

profile of v5, /device:TPU:0, one launch (start us, length us, event | category | flops | bytes accessed | tf_op | source)
XLA Modules:
  0.0 203.7 jit_solution(12031411919706754603)
XLA Ops:
  1.3 11.9 %enter.1 = (bf16[3,2,272,768]{3,2,1,0:T(8,128)(2,1)}, f32[3,2,256,768]{3,2,1,0:T(8,128)}, f32[3,256,768]{2,1,0:T(8,128)}, bf16[3,256,384]{2,1,0:T(8,128)(2,1)}, f32[3,1,1152]{2,1,0:T(1,128)}) custom-call(bf16[3,256,384]{2,1,0:T(8,128)(2,1)} %tok.3, bf16[3,256,384]{2,1,0:T(8,128)(2,1)} %cot.3, s32[3,256]{1,0:T(4,128)} %mask.3, s32[1,1]{1,0:T(1,128)} %bitcast.3.counts, ...), custom_call_target="tpu_custom_call" | custom-call | tf_op jit(solution)/shard_map/enter/pallas_call | solution.py:918
  13.2 45.2 %first.1 = (bf16[3,2,256,768]{3,2,1,0:T(8,128)(2,1)}, f32[3,2,256,768]{3,2,1,0:T(8,128)}, f32[3,2,256,768]{3,2,1,0:T(8,128)}, f32[3,2,256,768]{3,2,1,0:T(8,128)}...) custom-call(bf16[3,2,272,768]{3,2,1,0:T(8,128)(2,1)} %get-tuple-elem, ...), custom_call_target="tpu_custom_call" | custom-call | tf_op jit(solution)/shard_map/first/pallas_call | solution.py:954
  58.4 82.7 %second.1 = (f32[3,2,256,768]{3,2,1,0:T(8,128)}, f32[3,2,256,768]{3,2,1,0:T(8,128)}, f32[2,3,8,768]{3,2,1,0:T(8,128)}, f32[2,16,768]{2,1,0:T(8,128)}, f32[2,1,76...) custom-call(f32[3,16,768]{2,1,0:T(8,128)} %get-tuple-element.69.s_fi, ...), custom_call_target="tpu_custom_call" | custom-call | tf_op jit(solution)/shard_map/second/pallas_call | solution.py:990
  141.1 12.4 %third.1 = (bf16[3,256,384]{2,1,0:T(8,128)(2,1)}, f32[3,256,384]{2,1,0:T(8,128)}, f32[3,3,384]{2,1,0:T(4,128)}, f32[768,384]{1,0:T(8,128)}, f32[384,1536]{1,0:T(8,128)}) custom-call(bf16[3,256,384]{2,1,0:T(8,128)(2,1)} %tok.3, bf16[3,256,384]{2,1,0:T(8,128)(2,1)} %cot.3, f32[3,1,1152]{2,1,0:T(1,128)} %get-tuple-element.64.mod, s32[3,256]{1,0:T(4,128)} %mask.3, ...), custom_call_target="tpu_custom_call" | custom-call | tf_op jit(solution)/shard_map/third/pallas_call | solution.py:1030
  153.5 44.6 %reduce.1 = (bf16[3072,384]{1,0:T(8,128)(2,1)}, bf16[128,384]{1,0:T(8,128)(2,1)}, bf16[16,384]{1,0:T(8,128)(2,1)}) custom-call(f32[384,1536]{1,0:T(8,128)} %get-tuple-element.89.in_grad, f32[768,384]{1,0:T(8,128)} %get-tuple-element.90.out_grad, f32[2,64,768]{2,1,0:T(8,128)} %get-tuple-element.91.xp_grad, f32[2,32,768]{2,1,0:T(8,128)} %get-tuple-element.92.dtp_grad, ...), custom_call_target="tpu_custom_call" | custom-call | tf_op jit(solution)/shard_map/reduce/pallas_call | solution.py:1053
  198.1 5.6 %finish.1 = (f32[3,384]{1,0:T(4,128)}, f32[384,1152]{1,0:T(8,128)}, f32[1152]{0:T(1024)}, f32[384,1536]{1,0:T(8,128)}, f32[2,4,768]{2,1,0:T(4,128)}, /*index=5*/...) custom-call(bf16[3072,384]{1,0:T(8,128)(2,1)} %get-tuple-element.99., ...), custom_call_target="tpu_custom_call" | custom-call | tf_op jit(solution)/shard_map/finish/pallas_call | solution.py:1078

commit v6 on v5

--- a/solution.py
+++ b/solution.py
@@ -31,20 +31,14 @@
     return lax.dot_general(a, b, TN, preferred_element_type=F32)
 
 
-def reversal(size):
-    rows = lax.broadcasted_iota(jnp.int32, (size, size), 0)
-    cols = lax.broadcasted_iota(jnp.int32, (size, size), 1)
-    return (rows + cols == size - 1).astype(BF16)
+def flip_full(value):
+    turned = lax.broadcasted_iota(jnp.int32, (8, value.shape[1]), 0)
+    groups = [value[at : at + 8] for at in range(0, value.shape[0], 8)]
+    return jnp.concatenate([jnp.take_along_axis(group, 7 - turned, axis=0) for group in reversed(groups)], axis=0)
 
 
 def flip_low(value):
-    return dot(reversal(value.shape[0]), value).astype(BF16)
-
-
-def flip_full(value):
-    order = reversal(value.shape[0])
-    high = value.astype(BF16)
-    return dot(order, high) + dot(order, (value - high.astype(F32)).astype(BF16))
+    return flip_full(value.astype(F32)).astype(BF16)
 
 
 def normalise(tokens_f):
@@ -123,7 +117,7 @@
 def enter_kernel(
     runs, tok, cot, mask, counts, step, ada, ada_bias, win, wout,
     xe, dy, z_out, hid_out, mod_out,
-    prev_tok, next_tok, prev_mask, next_mask, send_sem, recv_sem,
+    mods, prev_tok, next_tok, prev_mask, next_mask, send_sem, recv_sem,
 ):
     slots, toks, dim = tok.shape
     inner = wout.shape[0]
@@ -154,11 +148,14 @@
             next_mask[...] = jnp.zeros(next_mask.shape, jnp.int32)
 
     live = (counts[...] > i).astype(F32)
-    steps = step[...].astype(F32)
-    here = lax.broadcasted_iota(jnp.int32, steps.shape, 0) == i
-    time_f = jnp.sum(jnp.where(here, steps, 0.0), axis=0, keepdims=True)
-    time_low = (time_f * jax.nn.sigmoid(time_f)).astype(BF16)
-    mod = dot(time_low, ada[...]) + ada_bias[...].reshape(1, 3 * dim)
+
+    @pl.when(i == 0)
+    def _():
+        time_f = step[...].astype(F32)
+        time_low = (time_f * jax.nn.sigmoid(time_f)).astype(BF16)
+        mods[...] = dot(time_low, ada[...]) + ada_bias[...].reshape(1, 3 * dim)
+
+    mod = mods[pl.ds(i, 1), :]
     mod_out[...] = mod
     shift, scale, gate = mod[:, :dim], mod[:, dim : 2 * dim], mod[:, 2 * dim :]
 
@@ -190,6 +187,10 @@
     rim_x = rim_x.astype(BF16)
     xe[0, :HALO, :] = rim_x[:HALO]
     xe[1, :HALO, :] = flip_low(rim_x[HALO:])
+
+
+def columns(inner, width=128):
+    return [slice(at, at + width) for at in range(0, inner, width)]
 
 
 def twice(row8):
@@ -373,23 +374,25 @@
         xwt[...] = jnp.concatenate([rows[:held], gap, rows[held:]], axis=0).astype(BF16)
         dtw[...] = jnp.concatenate([dt_rows[...].astype(F32), gap], axis=0).astype(BF16)
 
-    shifted = xe[...].astype(F32)
-    conv = tap_bias[pl.ds(branch, 1), :] + taps[tap_count - 1 : tap_count, :] * shifted[HALO:]
-    for k in reversed(range(tap_count - 1)):
-        shifted = pltpu.roll(shifted, 1, 0)
-        conv = conv + taps[k : k + 1, :] * shifted[HALO:]
-    sig = jax.nn.sigmoid(conv)
-    act_f = conv * sig
-    act = act_f.astype(BF16)
-    dsilu_out[...] = sig + act_f * (1.0 - sig)
-    act_out[...] = act
-    proj = dot_nt(xwt[...], act)
+    tap_row, dt_row = tap_bias[pl.ds(branch, 1), :], dt_bias[pl.ds(branch, 1), :]
+    for cols in columns(inner):
+        x_f = xe[:, cols].astype(F32)
+        conv = tap_row[:, cols] + taps[tap_count - 1 : tap_count, cols] * x_f[HALO:]
+        for k in range(tap_count - 1):
+            conv = conv + taps[k : k + 1, cols] * pltpu.roll(x_f, tap_count - 1 - k, 0)[HALO:]
+        open_part = jax.nn.sigmoid(conv)
+        act_f = conv * open_part
+        act_out[:, cols] = act_f.astype(BF16)
+        dsilu_out[:, cols] = open_part + act_f * (1.0 - open_part)
+    proj = dot_nt(xwt[...], act_out[...])
     proj_out[...] = proj
-    pre = dot_tn(proj[:rank, :].astype(BF16), dtw[...]) + dt_bias[pl.ds(branch, 1), :]
-    delta, slope = softplus_parts(pre)
-    delta_out[...] = delta
-    sig_out[...] = slope
-    dx[...] = delta * act.astype(F32)
+    dt_low = proj[:rank, :].astype(BF16)
+    for cols in columns(inner, 256):
+        pre = dot_tn(dt_low, dtw[:, cols]) + dt_row[:, cols]
+        delta, slope = softplus_parts(pre)
+        delta_out[:, cols] = delta
+        sig_out[:, cols] = slope
+        dx[:, cols] = delta * act_out[:, cols].astype(F32)
     lay_out(wide, proj[rank:, :], picks)
     end_out[...] = jnp.zeros((states, inner), F32)
     back_out[...] = jnp.zeros((states, inner), F32)
@@ -437,7 +440,7 @@
     runs, s_first, lam_first, ends, backs, totals, last_rate, starts, sums, tiles, rate, xe, act, dsilu, delta, sig, dy, proj, xwt, dtw, taps, skip,
     y_out, dx_out, late_out, rate_grad, skip_grad, dtb_grad, dtp_grad, xp_grad, tap_grad, tapb_grad,
     rate2, carry, dxs, bdiag, cdiag, decay, states_low, lam_low, rq_low, qd_low, dots, racc, gsum, hsum, db, dc,
-    rims, late, send_sem, recv_sem, s_in, s_last, lam_last, *exchange_scratch,
+    rims, late, send_sem, recv_sem, d_pre_low, s_in, s_last, lam_last, *exchange_scratch,
 ):
     toks, inner = dy.shape
     states = rate.shape[0]
@@ -479,8 +482,8 @@
         for ref in (rate_grad, skip_grad, dtb_grad, dtp_grad, xp_grad, tap_grad, tapb_grad):
             ref[...] = jnp.zeros(ref.shape, ref.dtype)
 
-    act_low = act[...]
-    dxs[:toks, :] = delta[...] * act_low.astype(F32)
+    for cols in columns(inner):
+        dxs[:toks, cols] = delta[:, cols] * act[:, cols].astype(F32)
     fold = (
         lax.broadcasted_iota(jnp.int32, (states, width), 1) % states == lax.broadcasted_iota(jnp.int32, (states, width), 0)
     ).astype(BF16)
@@ -554,33 +557,39 @@
     products(1, 0)
 
     rate_grad[...] += -racc[...]
-    act_f = act_low.astype(F32)
-    d_summed = dy[...]
-    g = gsum[:toks, :]
-    skip_grad[...] += jnp.sum(d_summed * act_f, axis=0, keepdims=True)
-    y_out[...] += gain * act_f
-    d_pre = (act_f * g - hsum[:toks, :]) * sig[...]
-    dtb_grad[...] += jnp.sum(d_pre, axis=0, keepdims=True)
-    d_pre_low = d_pre.astype(BF16)
-    dtp_grad[...] += dot(proj[:rank, :].astype(BF16), d_pre_low)
+    for cols in columns(inner):
+        act_f = act[:, cols].astype(F32)
+        skip_grad[:, cols] += jnp.sum(dy[:, cols] * act_f, axis=0, keepdims=True)
+        y_out[:, cols] += gain[:, cols] * act_f
+        d_pre = (act_f * gsum[:toks, cols] - hsum[:toks, cols]) * sig[:, cols]
+        dtb_grad[:, cols] += jnp.sum(d_pre, axis=0, keepdims=True)
+        d_pre_low[:, cols] = d_pre.astype(BF16)
+    held = dtp_grad.shape[0]
+    dtp_grad[...] += dot(proj[:rank, :].astype(BF16), d_pre_low[...])[:held]
     d_proj = jnp.concatenate(
-        [dot_nt(dtw[...], d_pre_low), dot_nt(fold, db[:toks, :]), dot_nt(fold, dc[:toks, :])], axis=0
+        [dot_nt(dtw[...], d_pre_low[...]), dot_nt(fold, db[:toks, :]), dot_nt(fold, dc[:toks, :])], axis=0
     ).astype(BF16)
-    xp_grad[...] += dot(d_proj, act_low)
-    d_act = delta[...] * g + gain * d_summed + dot_tn(d_proj, xwt[...])
-    d_conv = d_act * dsilu[...]
-    tapb_grad[...] += jnp.sum(d_conv, axis=0, keepdims=True)
-    x_f = xe[...].astype(F32)
-    moved = jnp.concatenate([jnp.zeros((HALO, inner), F32), d_conv], axis=0)
+    xp_new = dot(d_proj, act[...])
+    xp_grad[:held, :] += xp_new[:held]
+    xp_grad[held:, :] += xp_new[rank:]
     window = HALO + toks
-    d_window = taps[tap_count - 1 : tap_count, :] * moved
-    tap_grad[tap_count - 1 : tap_count, :] += jnp.sum(moved * x_f, axis=0, keepdims=True)
-    for k in reversed(range(tap_count - 1)):
-        moved = pltpu.roll(moved, window - 1, 0)
-        tap_grad[k : k + 1, :] += jnp.sum(moved * x_f, axis=0, keepdims=True)
-        d_window = d_window + taps[k : k + 1, :] * moved
-    rims[pl.program_id(0), item] = d_window[HALO - 8 : HALO]
-    dx_out[...] = d_window[HALO:]
+    for wide_cols in columns(inner, 256):
+        through = dot_tn(d_proj, xwt[:, wide_cols])
+        for at in columns(256):
+            cols = slice(wide_cols.start + at.start, wide_cols.start + at.stop)
+            d_act = delta[:, cols] * gsum[:toks, cols] + gain[:, cols] * dy[:, cols] + through[:, at]
+            d_conv = d_act * dsilu[:, cols]
+            tapb_grad[:, cols] += jnp.sum(d_conv, axis=0, keepdims=True)
+            x_f = xe[:, cols].astype(F32)
+            base = jnp.concatenate([jnp.zeros((HALO, 128), F32), d_conv], axis=0)
+            d_window = taps[tap_count - 1 : tap_count, cols] * base
+            tap_grad[tap_count - 1 : tap_count, cols] += jnp.sum(d_conv * x_f[HALO:], axis=0, keepdims=True)
+            for k in range(tap_count - 1):
+                moved = pltpu.roll(base, window - (tap_count - 1 - k), 0)
+                tap_grad[k : k + 1, cols] += jnp.sum(moved * x_f, axis=0, keepdims=True)
+                d_window = d_window + taps[k : k + 1, cols] * moved
+            rims[branch, item, :, cols] = d_window[HALO - 8 : HALO]
+            dx_out[:, cols] = d_window[HALO:]
 
     @pl.when(last_item & (pl.program_id(0) == 0))
     def _():
@@ -602,265 +611,373 @@
         late_out[...] = late[...]
 
 
-def third_kernel(
-    tok, cot, mod, mask, counts, hid, z_in, y, dx, late, win, wout,
-    mixed, d_tokens, d_mod, out_grad, in_grad,
+LAST_ROWS = 16
+PART_ROWS = 512
+
+
+class Ring:
+    def __init__(self, bits):
+        self.bits = bits
+        self.size = 1 << len(bits)
+        self.digits = [bit_of(lax.axis_index(axis), bit) for axis, bit in bits]
+        self.place = sum(digit * (1 << at) for at, digit in enumerate(self.digits))
+
+    def target(self, ahead):
+        place = (self.place + ahead) % self.size
+        where = {}
+        for at, (axis, bit) in enumerate(self.bits):
+            base = where.get(axis, lax.axis_index(axis))
+            where[axis] = base + (bit_of(place, at) - self.digits[at]) * (1 << bit)
+        return where, place
+
+    def targets(self):
+        return [self.target(ahead)[0] for ahead in range(1, self.size)]
+
+
+def stage_rings(runs, groups):
+    bits = [("seq", bit) for bit in range(int(math.log2(runs)))] + [("dp", bit) for bit in range(int(math.log2(groups)))]
+    return [Ring(bits[:1])] + [Ring(bits[at : at + 2]) for at in range(1, len(bits), 2)]
+
+
+def part_count(rows):
+    return -(-rows // PART_ROWS)
+
+
+def buffer_rows(runs, groups):
+    bits = int(math.log2(runs)) + int(math.log2(groups))
+    size, total = PART_ROWS, 0
+    for members in [2] + [1 << min(2, bits - at) for at in range(1, bits, 2)]:
+        moved = size // members if size >= members * LAST_ROWS else size
+        total += moved * (members - 1)
+        size = moved
+    return total
+
+
+def reduce_shapes(parts, dim, runs, groups):
+    bits = int(math.log2(runs)) + int(math.log2(groups))
+    stages = 1 + bits // 2
+    room = parts * buffer_rows(runs, groups)
+    sems = pltpu.SemaphoreType.DMA((parts, 2 * stages, 3))
+    return [
+        pltpu.VMEM((parts * PART_ROWS, dim), F32), pltpu.VMEM((room, dim), BF16), pltpu.VMEM((room, dim), BF16),
+        pltpu.VMEM((parts * PART_ROWS, dim), BF16), sems, sems,
+    ]
+
+
+class Reduction:
+    def __init__(self, rings, turns, segments, acc, sends, arrivals, gathered, send_sem, recv_sem):
+        self.rings = rings
+        self.count = len(rings)
+        self.parts = len(turns)
+        self.segments = segments
+        self.acc, self.sends, self.arrivals, self.gathered = acc, sends, arrivals, gathered
+        self.send_sem, self.recv_sem = send_sem, recv_sem
+        room = sends.shape[0] // self.parts
+        self.steps = []
+        for part, turn in enumerate(turns):
+            later = rings[1:]
+            turn = turn % max(len(later), 1)
+            order = rings[:1] + later[turn:] + later[:turn]
+            start, size, at = part * PART_ROWS, PART_ROWS, part * room
+            steps = []
+            for ring in order:
+                split = size >= ring.size * LAST_ROWS
+                moved = size // ring.size if split else size
+                keep = pl.multiple_of(start + ring.place * moved, LAST_ROWS) if split else start
+                steps.append((ring, start, split, moved, keep, at))
+                at += moved * (ring.size - 1)
+                start, size = keep, moved
+            self.steps.append(steps)
+
+    def assemble(self, part):
+        low, high = part * PART_ROWS, (part + 1) * PART_ROWS
+        at = 0
+        for get, size in self.segments:
+            first, last = max(at, low), min(at + size, high)
+            if first < last:
+                self.acc[first:last, :] = get(first - at, last - first)
+            at += size
+        if at < high:
+            first = max(at, low)
+            self.acc[first:high, :] = jnp.zeros((high - first, self.acc.shape[1]), F32)
+
+    def scatter_copy(self, part, stage, ahead):
+        ring, _, _, moved, _, at = self.steps[part][stage]
+        at += (ahead - 1) * moved
+        return remote(
+            self.sends.at[pl.ds(at, moved), :], self.arrivals.at[pl.ds(at, moved), :],
+            self.send_sem.at[part, stage, ahead - 1], self.recv_sem.at[part, stage, ahead - 1], ring.target(ahead)[0],
+        )
+
+    def scatter(self, part, stage):
+        ring, start, split, moved, _, at = self.steps[part][stage]
+        for ahead in range(1, ring.size):
+            place = ring.target(ahead)[1]
+            away = pl.multiple_of(start + place * moved, LAST_ROWS) if split else start
+            here = at + (ahead - 1) * moved
+            self.sends[here : here + moved, :] = self.acc[pl.ds(away, moved), :].astype(BF16)
+            self.scatter_copy(part, stage, ahead).start()
+
+    def settle(self, part, stage):
+        ring, _, split, moved, keep, at = self.steps[part][stage]
+        for ahead in range(1, ring.size):
+            self.scatter_copy(part, stage, ahead).wait()
+        held = self.acc[pl.ds(keep, moved), :]
+        came = [
+            self.arrivals[at + (ahead - 1) * moved : at + ahead * moved, :].astype(F32) for ahead in range(1, ring.size)
+        ]
+        if split:
+            held = held + sum(came)
+        else:
+            values = [held.astype(BF16).astype(F32)] + came
+            total = jnp.zeros_like(held)
+            for place in range(ring.size):
+                behind = (ring.place - place + ring.size) % ring.size
+                chosen = values[0]
+                for ahead in range(1, ring.size):
+                    chosen = jnp.where(behind == ahead, values[ahead], chosen)
+                total = total + chosen
+            held = total
+        self.acc[pl.ds(keep, moved), :] = held
+
+    def gather_copies(self, part, stage):
+        ring, _, split, moved, keep, _ = self.steps[part][stage]
+        here = self.gathered.at[pl.ds(keep, moved), :]
+        return [
+            remote(
+                here, here, self.send_sem.at[part, self.count + stage, ahead - 1],
+                self.recv_sem.at[part, self.count + stage, ahead - 1], ring.target(ahead)[0],
+            )
+            for ahead in range(1, ring.size)
+            if split
+        ]
+
+    def points(self):
+        def begin():
+            for part in range(self.parts):
+                self.assemble(part)
+                self.scatter(part, 0)
+
+        def split(stage):
+            for part in range(self.parts):
+                self.settle(part, stage - 1)
+                self.scatter(part, stage)
+
+        def turn():
+            for part in range(self.parts):
+                self.settle(part, self.count - 1)
+                _, _, _, moved, keep, _ = self.steps[part][-1]
+                self.gathered[pl.ds(keep, moved), :] = self.acc[pl.ds(keep, moved), :].astype(BF16)
+                for copy in self.gather_copies(part, self.count - 1):
+                    copy.start()
+
+        def join(stage):
+            for part in range(self.parts):
+                for copy in self.gather_copies(part, stage + 1):
+                    copy.wait()
+                if stage >= 0:
+                    for copy in self.gather_copies(part, stage):
+                        copy.start()
+
+        points = [begin]
+        points += [functools.partial(split, stage) for stage in range(1, self.count)]
+        points += [turn]
+        return points + [functools.partial(join, stage) for stage in reversed(range(-1, self.count - 1))]
+
+
+def big_segments(ref, dim):
+    return [
+        (lambda at, size, lane=lane: ref[at : at + size, lane : lane + dim], ref.shape[0])
+        for lane in range(0, ref.shape[1], dim)
+    ]
+
+
+def small_segments(refs, tails, dim):
+    inner = refs[0].shape[2]
+    blocks = [(lambda ref=ref, branch=branch: ref[branch], ref.shape[1]) for ref in refs for branch in range(2)]
+
+    def tail():
+        lines = [ref[branch] for ref in tails for branch in range(2)]
+        return jnp.concatenate(lines + [jnp.zeros((8 - len(lines), inner), F32)], axis=0)
+
+    blocks.append((tail, 8))
+    return [
+        (lambda at, size, get=get, lane=lane: get()[at : at + size, lane : lane + dim], size)
+        for lane in range(0, inner, dim)
+        for get, size in blocks
+    ]
+
+
+def tail_kernel(
+    plan, tok, cot, mod, mask, counts, hid, z_in, y, dx, late, win, wout, step,
+    xp_grad, dtp_grad, rate_grad, tap_grad, tapb_grad, skip_grad, dtb_grad,
+    mixed, d_tokens, result, x_result, factors, own_rows,
+    dz, out_grad, z_grad, x_grad, mod_sum, mod_in, table, small_send, small_recv, *reduce_scratch,
 ):
+    runs, groups, slots = plan
     dim = tok.shape[-1]
     toks, inner = z_in.shape
-    i = pl.program_id(0)
-
-    @pl.when(i == 0)
-    def _():
+    now = pl.program_id(0)
+    i = now % slots
+    rings = stage_rings(runs, groups)
+    seq_ring = Ring([("seq", bit) for bit in range(int(math.log2(runs)))])
+    dp_ring = Ring([("dp", bit) for bit in range(int(math.log2(groups)))])
+    half = len(reduce_scratch) // 2
+    smalls = small_segments((xp_grad, dtp_grad, rate_grad, tap_grad), (tapb_grad, skip_grad, dtb_grad), dim)
+    segments = big_segments(out_grad, dim) + big_segments(z_grad, dim) + smalls
+    main = Reduction(rings, [part % 3 // 2 for part in range(result.shape[0] // PART_ROWS)], segments, *reduce_scratch[:half])
+    rest = Reduction(rings, [part % 2 for part in range(x_result.shape[0] // PART_ROWS)], big_segments(x_grad, dim), *reduce_scratch[half:])
+    main_points, rest_points = main.points(), rest.points()
+
+    @pl.when(now == 0)
+    def _():
+        greet([target for ring in rings + [seq_ring, dp_ring] for target in ring.targets()])
         out_grad[...] = jnp.zeros(out_grad.shape, F32)
-        in_grad[...] = jnp.zeros(in_grad.shape, F32)
-
-    shift, scale, gate = mod[:, :dim], mod[:, dim : 2 * dim], mod[:, 2 * dim :]
+        z_grad[...] = jnp.zeros(z_grad.shape, F32)
+        x_grad[...] = jnp.zeros(x_grad.shape, F32)
+        mod_sum[...] = jnp.zeros(mod_sum.shape, F32)
+
+    scale, gate = mod[:, dim : 2 * dim], mod[:, 2 * dim :]
     valid = as_column(mask[pl.ds(i, 1), :]) * (counts[...] > i).astype(F32)
-    tok_f = tok[...].astype(F32)
-    normed, inv_std = normalise(tok_f)
-    cot_f = cot[...].astype(F32)
-    z = z_in[...]
-    z_sig = jax.nn.sigmoid(z)
-    summed = y[0] + flip_full(y[1])
-    gated = (summed * z * z_sig).astype(BF16)
-    branch_out = dot(gated, wout[...])
-    mixed[...] = (tok_f + gate * branch_out).astype(BF16)
-    d_branch = (cot_f * gate).astype(BF16)
-    d_gated = dot_nt(d_branch, wout[...])
-    d_zgate = d_gated * summed * z_sig * (1.0 + z * (1.0 - z_sig))
-    out_grad[...] += dot_tn(gated, d_branch)
-
-    edge = late.shape[2]
-
-    def with_late(part, extra):
-        return jnp.concatenate([part[: toks - edge], part[toks - edge :] + extra], axis=0)
-
-    d_x = with_late(dx[0], late[0, i]) + flip_full(with_late(dx[1], late[1, i]))
-    d_xz = (jnp.concatenate([d_x, d_zgate], axis=1) * valid).astype(BF16)
-    d_hidden = dot_nt(d_xz, win[...])
-    in_grad[...] += dot_tn(hid[...], d_xz)
-    d_mod[0:1, :] = jnp.sum(d_hidden, axis=0, keepdims=True)
-    d_mod[1:2, :] = jnp.sum(d_hidden * normed, axis=0, keepdims=True)
-    d_mod[2:3, :] = jnp.sum(cot_f * branch_out, axis=0, keepdims=True)
-    d_normed = d_hidden * (1.0 + scale)
-    d_tokens[...] = cot_f + inv_std * (
-        d_normed
-        - jnp.mean(d_normed, axis=-1, keepdims=True)
-        - normed * jnp.mean(d_normed * normed, axis=-1, keepdims=True)
-    )
-
-
-PARTS = 6
-LAST_ROWS = 16
-
-
-def reduce_rows(dim, inner, small):
-    rows = inner + (2 * dim + small) * (inner // dim)
-    unit = PARTS * LAST_ROWS * 32
-    return -(-rows // unit) * unit
-
-
-def reduce_kernel(
-    plan, in_grad, out_grad, xp_grad, dtp_grad, rate_grad, tap_grad, tapb_grad, skip_grad, dtb_grad, d_mod, step,
-    result, factors, own_rows,
-    acc, sends, arrivals, gathered, mod_sum, mod_in, table, send_sem, recv_sem, small_send, small_recv,
-):
-    runs, groups, total_rows = plan
-    dim = in_grad.shape[0]
-    inner = out_grad.shape[0]
-    slots = step.shape[0]
-    seq_bits = [("seq", bit) for bit in range(int(math.log2(runs)))]
-    dp_bits = [("dp", bit) for bit in range(int(math.log2(groups)))]
-    all_bits = seq_bits + dp_bits
-    count = len(all_bits)
-    links = {key: across(*key) for key in all_bits}
-    middle = all_bits[1:-1]
-    turn = [part % max(len(middle), 1) for part in range(PARTS)]
-    orders = [all_bits[:1] + middle[at:] + middle[:at] + all_bits[1:][-1:] for at in turn]
-    part_rows = total_rows // PARTS
-
-    def small_copy(stage):
-        axis, bit = all_bits[stage]
-        target = links[(axis, bit)][1]
-        if axis == "seq":
-            return remote(mod_sum, mod_in.at[stage], small_send.at[stage], small_recv.at[stage], target)
-        size = 16 << bit
-        at = pl.multiple_of(lax.axis_index("dp") // (1 << bit) * size, 16)
-        here = table.at[pl.ds(at, size), :]
-        return remote(here, here, small_send.at[stage], small_recv.at[stage], target)
-
-    def fill_table():
+    mod_rows = pl.ds(pl.multiple_of(8 * i, 8), 8)
+
+    @pl.when(now < slots)
+    def _():
+        cot_f = cot[...].astype(F32)
+        z = z_in[...]
+        z_sig = jax.nn.sigmoid(z)
+        z_silu = z * z_sig
+        summed = y[0] + flip_full(y[1])
+        gated = (summed * z_silu).astype(BF16)
+        branch_out = dot(gated, wout[...])
+        mixed[...] = (tok[...].astype(F32) + gate * branch_out).astype(BF16)
+        d_branch = (cot_f * gate).astype(BF16)
+        out_grad[...] += dot_tn(gated, d_branch)
+        d_zgate = dot_nt(d_branch, wout[...]) * summed * (z_sig + z_silu * (1.0 - z_sig))
+        d_low = (d_zgate * valid).astype(BF16)
+        dz[i] = d_low
+        z_grad[...] += dot_tn(hid[...], d_low)
+        d_gate = jnp.sum(cot_f * branch_out, axis=0, keepdims=True)
+        mod_sum[mod_rows, :] = jnp.concatenate([jnp.zeros((2, dim), F32), d_gate, jnp.zeros((5, dim), F32)], axis=0)
+
+    @pl.when(now == slots)
+    def _():
+        main_points[0]()
+
+    @pl.when(now >= slots)
+    def _():
+        edge = late.shape[2]
+
+        def with_late(part, extra):
+            return jnp.concatenate([part[: toks - edge], part[toks - edge :] + extra], axis=0)
+
+        d_x = with_late(dx[0], late[0, i]) + flip_full(with_late(dx[1], late[1, i]))
+        d_x = (d_x * valid).astype(BF16)
+        x_grad[...] += dot_tn(hid[...], d_x)
+        d_hidden = dot_nt(d_x, win[:, :inner]) + dot_nt(dz[i], win[:, inner:])
+        normed, inv_std = normalise(tok[...].astype(F32))
+        d_shift = jnp.sum(d_hidden, axis=0, keepdims=True)
+        d_scale = jnp.sum(d_hidden * normed, axis=0, keepdims=True)
+        mod_sum[mod_rows, :] += jnp.concatenate([d_shift, d_scale, jnp.zeros((6, dim), F32)], axis=0)
+        d_normed = d_hidden * (1.0 + scale)
+        d_tokens[...] = cot[...].astype(F32) + inv_std * (
+            d_normed
+            - jnp.mean(d_normed, axis=-1, keepdims=True)
+            - normed * jnp.mean(d_normed * normed, axis=-1, keepdims=True)
+        )
+
+    @pl.when(now == slots)
+    def _():
+        main_points[1]()
+
+    def sum_copies():
+        return [
+            remote(mod_sum, mod_in.at[ahead - 1], small_send.at[ahead - 1], small_recv.at[ahead - 1], seq_ring.target(ahead)[0])
+            for ahead in range(1, seq_ring.size)
+        ]
+
+    def table_copies():
+        at = pl.multiple_of(dp_ring.place * 16, 16)
+        here = table.at[pl.ds(at, 16), :]
+        base = seq_ring.size - 1
+        return [
+            remote(here, here, small_send.at[base + ahead - 1], small_recv.at[base + ahead - 1], dp_ring.target(ahead)[0])
+            for ahead in range(1, dp_ring.size)
+        ]
+
+    def start_small():
+        for copy in sum_copies():
+            copy.start()
+
+    def turn_small():
+        for copy in sum_copies():
+            copy.wait()
+        values = [mod_sum[...]] + [mod_in[ahead - 1] for ahead in range(1, seq_ring.size)]
+        total = jnp.zeros(mod_sum.shape, F32)
+        for place in range(seq_ring.size):
+            behind = (seq_ring.place - place + seq_ring.size) % seq_ring.size
+            chosen = values[0]
+            for ahead in range(1, seq_ring.size):
+                chosen = jnp.where(behind == ahead, values[ahead], chosen)
+            total = total + chosen
         time_f = step[...].astype(F32)
         time_low = time_f * jax.nn.sigmoid(time_f)
-        at = pl.multiple_of(lax.axis_index("dp") * 16, 16)
-        own = jnp.concatenate([mod_sum[: 3 * slots, :], time_low, mod_sum[4 * slots :, :]], axis=0)
-        own_rows[...] = own.astype(BF16)
-        table[pl.ds(at, 16), :] = own.astype(BF16)
-
-    def start_small(stage):
-        if stage == len(seq_bits):
-            fill_table()
-        if stage < count:
-            small_copy(stage).start()
-
-    def end_small(stage):
-        small_copy(stage).wait()
-        if all_bits[stage][0] == "seq":
-            mod_sum[...] += mod_in[stage]
-
-    segments = [(lambda at, size: out_grad[at : at + size, :], inner)]
-    for lane in range(0, 2 * inner, dim):
-        segments.append((lambda at, size, lane=lane: in_grad[at : at + size, lane : lane + dim], dim))
-    small = []
-    for ref in (xp_grad, dtp_grad, rate_grad, tap_grad):
-        small += [(lambda ref=ref, branch=branch: ref[branch], ref.shape[1]) for branch in range(2)]
-
-    def tail():
-        rows = [ref[branch] for ref in (tapb_grad, skip_grad, dtb_grad) for branch in range(2)]
-        return jnp.concatenate(rows + [jnp.zeros((2, inner), F32)], axis=0)
-
-    small.append((tail, 8))
-    for lane in range(0, inner, dim):
-        for get, size in small:
-            segments.append((lambda at, size, get=get, lane=lane: get()[at : at + size, lane : lane + dim], size))
-    total = sum(size for _, size in segments)
-    segments.append((lambda at, size: jnp.zeros((size, dim), F32), total_rows - total))
-
-    def assemble(part):
-        low, high = part * part_rows, (part + 1) * part_rows
-        at = 0
-        for get, size in segments:
-            first, last = max(at, low), min(at + size, high)
-            if first < last:
-                acc[first:last, :] = get(first - at, last - first)
-            at += size
-
-    starts = [part * part_rows for part in range(PARTS)]
-    sizes = [part_rows] * PARTS
-    history = [[] for _ in range(PARTS)]
-    offsets = [part * (part_rows + LAST_ROWS * count) for part in range(PARTS)]
-    flying = [None] * PARTS
-
-    def scatter(part, stage):
-        mine, target = links[orders[part][stage]]
-        start, size = starts[part], sizes[part]
-        split = size >= 2 * LAST_ROWS
-        moved = size // 2 if split else size
-        away = keep = start
-        if split:
-            away = pl.multiple_of(start + (1 - mine) * moved, LAST_ROWS)
-            keep = pl.multiple_of(start + mine * moved, LAST_ROWS)
-        history[part].append((start, size, split))
-        at = offsets[part]
-        offsets[part] += moved
-        sends[at : at + moved, :] = acc[pl.ds(away, moved), :].astype(BF16)
-        copy = remote(
-            sends.at[pl.ds(at, moved), :], arrivals.at[pl.ds(at, moved), :], send_sem.at[part, stage],
-            recv_sem.at[part, stage], target,
-        )
-        copy.start()
-        starts[part], sizes[part] = keep, moved
-        flying[part] = (copy, keep, moved, at, split)
-
-    def settle(part):
-        copy, keep, moved, at, split = flying[part]
-        copy.wait()
-        held = acc[pl.ds(keep, moved), :]
-        if not split:
-            held = held.astype(BF16).astype(F32)
-        acc[pl.ds(keep, moved), :] = held + arrivals[at : at + moved, :].astype(F32)
-
-    def gather(part, stage):
-        start, size, split = history[part][stage]
-        flying[part] = None
-        if split:
-            here = gathered.at[pl.ds(starts[part], sizes[part]), :]
-            target = links[orders[part][stage]][1]
-            flying[part] = remote(
-                here, here, send_sem.at[part, count + stage], recv_sem.at[part, count + stage], target
-            )
-            flying[part].start()
-            starts[part], sizes[part] = start, size
-
-    mod_sum[...] = jnp.zeros(mod_sum.shape, F32)
-    for i in range(slots):
-        mod_sum[3 * i : 3 * i + 3, :] = d_mod[i]
-    greet([links[key][1] for key in all_bits])
-    start_small(0)
-    for part in range(PARTS):
-        assemble(part)
-        scatter(part, 0)
-    for stage in range(1, count):
-        end_small(stage - 1)
-        start_small(stage)
-        for part in range(PARTS):
-            settle(part)
-            scatter(part, stage)
-    end_small(count - 1)
-    if not dp_bits:
-        fill_table()
-    for part in range(PARTS):
-        settle(part)
-        where = pl.ds(starts[part], sizes[part])
-        gathered[where, :] = acc[where, :].astype(BF16)
-        gather(part, count - 1)
-    for stage in reversed(range(count - 1)):
-        for part in range(PARTS):
-            if flying[part] is not None:
-                flying[part].wait()
-            gather(part, stage)
-    for part in range(PARTS):
-        if flying[part] is not None:
-            flying[part].wait()
-        result[part * part_rows : (part + 1) * part_rows, :] = gathered[part * part_rows : (part + 1) * part_rows, :]
-    factors[...] = table[...]
+        lines = [total[8 * item : 8 * item + 3] for item in range(slots)] + [time_low]
+        lines.append(jnp.zeros((16 - 4 * slots, dim), F32))
+        own = jnp.concatenate(lines, axis=0).astype(BF16)
+        own_rows[...] = own
+        table[pl.ds(pl.multiple_of(dp_ring.place * 16, 16), 16), :] = own
+        for copy in table_copies():
+            copy.start()
+
+    def end_small():
+        for copy in table_copies():
+            copy.wait()
+        factors[...] = table[...]
+
+    @pl.when(now == 2 * slots - 1)
+    def _():
+        start_small()
+        rest_points[0]()
+        rest_points[1]()
+        for at in range(2, len(main_points)):
+            main_points[at]()
+            if at == 2:
+                turn_small()
+            rest_points[at]()
+        end_small()
+        result[...] = main.gathered[...]
+        x_result[...] = rest.gathered[...]
 
 
 def finish_kernel(
-    ranks, result, factors, own, step, ada,
+    result, x_result, factors, own, step, ada,
     grad_time, grad_ada, grad_ada_bias, in_grad, tap_grad, tapb_grad, xp_grad, dtp_grad, dtb_grad, rate_grad, skip_grad, out_grad,
 ):
-    rank, wide_rank = ranks
-    dim = in_grad.shape[0]
-    inner = out_grad.shape[0]
+    dim, inner = in_grad.shape[0], rate_grad.shape[2]
     slots = step.shape[0]
-    states = rate_grad.shape[1]
-    taps = tap_grad.shape[1]
+
+    now = pl.program_id(0)
 
     def rows(at, size):
         return result[at : at + size, :].astype(F32)
 
-    out_grad[...] = rows(0, inner)
-    at = inner
-    for lane in range(0, 2 * inner, dim):
-        in_grad[:, lane : lane + dim] = rows(at, dim)
-        at += dim
-    wide = wide_rank + 2 * states
-    for first in range(0, inner, dim):
-        lanes = slice(first, first + dim)
-        for branch in range(2):
-            part = rows(at, wide)
-            xp_grad[branch, :, lanes] = jnp.concatenate([part[:rank], part[wide_rank:]], axis=0)
-            at += wide
-        for branch in range(2):
-            dtp_grad[branch, :, lanes] = rows(at, wide_rank)[:rank]
-            at += wide_rank
-        for branch in range(2):
-            rate_grad[branch, :, lanes] = rows(at, states)
-            at += states
-        tail = rows(at, 16)
-        for branch in range(2):
-            tap_grad[branch, :, lanes] = tail[branch * taps : (branch + 1) * taps]
-        tapb_grad[:, lanes] = tail[2 * taps : 2 * taps + 2]
-        skip_grad[:, lanes] = tail[2 * taps + 2 : 2 * taps + 4]
-        dtb_grad[:, lanes] = tail[2 * taps + 4 : 2 * taps + 6]
-        at += 16
+    out_rows = out_grad.shape[0]
+    out_grad[...] = result[pl.ds(pl.multiple_of(now * out_rows, out_rows), out_rows), :].astype(F32)
+    pieces = inner // dim
+
+    @pl.when(now < pieces)
+    def _():
+        in_grad[...] = x_result[pl.ds(pl.multiple_of(now * dim, dim), dim), :].astype(F32)
+
+    @pl.when(now >= pieces)
+    def _():
+        in_grad[...] = result[pl.ds(pl.multiple_of(inner + (now - pieces) * dim, dim), dim), :].astype(F32)
+
 
     table = factors[...]
     length = table.shape[0]
-    groups = length // 16
-    items = groups * 8
+    items = length // 16 * 8
 
     def pick(place):
         row = lax.broadcasted_iota(jnp.int32, (items, length), 0)
@@ -869,19 +986,38 @@
         wanted = row // 8 * 16 + place(slot)
         return dot(((col == wanted) & (slot < slots)).astype(BF16), table)
 
-    times = pick(lambda slot: 3 * slots + slot).astype(BF16)
-    time_f = step[...].astype(F32)
-    time_sig = jax.nn.sigmoid(time_f)
-    d_time = jnp.zeros((slots, dim), F32)
-    mine = own[...].astype(F32)
     for part in range(3):
-        mods = pick(lambda slot: 3 * slot + part)
-        lanes = slice(part * dim, (part + 1) * dim)
-        grad_ada[:, lanes] = dot_tn(times, mods.astype(BF16))
-        grad_ada_bias[lanes] = jnp.sum(mods, axis=0)
-        picked = jnp.concatenate([mine[3 * i + part : 3 * i + part + 1] for i in range(slots)], axis=0)
-        d_time = d_time + dot_nt(picked.astype(BF16), ada[:, lanes])
-    grad_time[...] = d_time * time_sig * (1.0 + time_f * (1.0 - time_sig))
+
+        @pl.when(now == part)
+        def _():
+            times = pick(lambda slot: 3 * slots + slot).astype(BF16)
+            mods = pick(lambda slot: 3 * slot + part)
+            lanes = slice(part * dim, (part + 1) * dim)
+            grad_ada[...] = dot_tn(times, mods.astype(BF16))
+            grad_ada_bias[lanes] = jnp.sum(mods, axis=0)
+            mine = own[...].astype(F32)
+            picked = jnp.concatenate([mine[3 * i + part : 3 * i + part + 1] for i in range(slots)], axis=0)
+            d_time = dot_nt(picked.astype(BF16), ada[:, lanes])
+            grad_time[...] = d_time if part == 0 else grad_time[...] + d_time
+
+    @pl.when(now == 3)
+    def _():
+        time_f = step[...].astype(F32)
+        time_sig = jax.nn.sigmoid(time_f)
+        grad_time[...] = grad_time[...] * time_sig * (1.0 + time_f * (1.0 - time_sig))
+        at = 2 * inner
+        for first in range(0, inner, dim):
+            lanes = slice(first, first + dim)
+            for ref in (xp_grad, dtp_grad, rate_grad, tap_grad):
+                size = ref.shape[1]
+                for branch in range(2):
+                    ref[branch, :, lanes] = rows(at, size)
+                    at += size
+            tail = rows(at, 8)
+            tapb_grad[:, lanes] = tail[0:2]
+            skip_grad[:, lanes] = tail[2:4]
+            dtb_grad[:, lanes] = tail[4:6]
+            at += 8
 
 
 def params(**more):
@@ -933,6 +1069,7 @@
             jax.ShapeDtypeStruct((slots, 1, 3 * dim), F32),
         ],
         scratch_shapes=[
+            pltpu.VMEM((slots, 3 * dim), F32),
             pltpu.VMEM((slots, HALO, dim), BF16), pltpu.VMEM((slots, HALO, dim), BF16), pltpu.VMEM((slots, toks), jnp.int32),
             pltpu.VMEM((slots, toks), jnp.int32), pltpu.SemaphoreType.DMA((4,)), pltpu.SemaphoreType.DMA((4,)),
         ],
@@ -999,12 +1136,12 @@
         ],
         out_specs=[
             unit(toks, inner), unit(toks, inner), whole(2, slots, 8, inner), branch(states, inner), branch(1, inner), branch(1, inner),
-            branch(wide_rank, inner), branch(proj_rows, inner), branch(tap_count, inner), branch(1, inner),
+            branch(rank, inner), branch(rank + 2 * states, inner), branch(tap_count, inner), branch(1, inner),
         ],
         out_shape=[
             unit_shape(toks, inner), unit_shape(toks, inner), jax.ShapeDtypeStruct((2, slots, 8, inner), F32),
         ] + [
-            jax.ShapeDtypeStruct((2, rows, inner), F32) for rows in (states, 1, 1, wide_rank, proj_rows, tap_count, 1)
+            jax.ShapeDtypeStruct((2, rows, inner), F32) for rows in (states, 1, 1, rank, rank + 2 * states, tap_count, 1)
         ],
         scratch_shapes=[
             pltpu.VMEM((states, inner), F32), pltpu.VMEM((states, inner), F32), pltpu.VMEM((toks + BLK, inner), F32), pltpu.VMEM((toks + BLK, BLK * states), BF16),
@@ -1016,8 +1153,8 @@
             pltpu.VMEM((toks + BLK, inner), F32), pltpu.VMEM((toks + BLK, inner), F32),
             pltpu.VMEM((toks + BLK, BLK * states), BF16), pltpu.VMEM((toks + BLK, BLK * states), BF16),
             pltpu.VMEM((2, slots, 8, inner), F32), pltpu.VMEM((2, slots, 8, inner), F32),
-            pltpu.SemaphoreType.DMA((2,)), pltpu.SemaphoreType.DMA((2,)), pltpu.VMEM((states, inner), F32),
-            pltpu.VMEM((slots, states, inner), F32), pltpu.VMEM((slots, states, inner), F32),
+            pltpu.SemaphoreType.DMA((2,)), pltpu.SemaphoreType.DMA((2,)), pltpu.VMEM((toks, inner), BF16),
+            pltpu.VMEM((states, inner), F32), pltpu.VMEM((slots, states, inner), F32), pltpu.VMEM((slots, states, inner), F32),
             *exchange_shapes(runs, slots, states, inner),
         ],
         compiler_params=params(collective_id=3, has_side_effects=True),
@@ -1027,58 +1164,66 @@
         sig, dy, proj, xwt, dtw, conv_weight, skip_gain,
     )
 
-    mixed, d_tokens, d_mod, out_grad, in_grad = pl.pallas_call(
-        third_kernel,
-        grid=(slots,),
+    def now(*block):
+        return spec((None,) + block, lambda s: (s % slots,) + (0,) * len(block))
+
+    def early(*block):
+        return spec((None,) + block, lambda s: (jnp.minimum(s, slots - 1),) + (0,) * len(block))
+
+    def after(*block):
+        return spec((None,) + block, lambda s: (jnp.maximum(s - slots, 0),) + (0,) * len(block))
+
+    smalls = (xp_grad, dtp_grad, rate_grad, tap_grad, tapb_grad, skip_grad, dtb_grad)
+    small_rows = (2 * sum(ref.shape[1] for ref in smalls[:4]) + 8) * (inner // dim)
+    main_parts = part_count(inner + dim * (inner // dim) + small_rows)
+    rest_parts = part_count(dim * (inner // dim))
+    mixed, d_tokens, result, x_result, factors, own = pl.pallas_call(
+        functools.partial(tail_kernel, (runs, groups, slots)),
+        grid=(2 * slots,),
         in_specs=[
-            item(toks, dim), item(toks, dim), item(1, 3 * dim), whole(slots, toks), whole(1, 1), item(toks, dim),
-            item(toks, inner), item(2, toks, inner), item(2, toks, inner), whole(2, slots, 8, inner), whole(dim, 2 * inner),
-            whole(inner, dim),
-        ],
-        out_specs=[item(toks, dim), item(toks, dim), item(3, dim), whole(inner, dim), whole(dim, 2 * inner)],
+            now(toks, dim), now(toks, dim), now(1, 3 * dim), whole(slots, toks), whole(1, 1), now(toks, dim),
+            early(toks, inner), early(2, toks, inner), after(2, toks, inner), whole(2, slots, 8, inner),
+            whole(dim, 2 * inner), whole(inner, dim), whole(slots, dim), *[whole(*ref.shape) for ref in smalls],
+        ],
+        out_specs=[
+            early(toks, dim), after(toks, dim), whole(main_parts * PART_ROWS, dim), whole(rest_parts * PART_ROWS, dim),
+            whole(16 * groups, dim), whole(16, dim),
+        ],
         out_shape=[
             jax.ShapeDtypeStruct((slots, toks, dim), BF16), jax.ShapeDtypeStruct((slots, toks, dim), F32),
-            jax.ShapeDtypeStruct((slots, 3, dim), F32), jax.ShapeDtypeStruct((inner, dim), F32),
-            jax.ShapeDtypeStruct((dim, 2 * inner), F32),
-        ],
-        compiler_params=params(),
-        name="third",
+            jax.ShapeDtypeStruct((main_parts * PART_ROWS, dim), BF16), jax.ShapeDtypeStruct((rest_parts * PART_ROWS, dim), BF16),
+            jax.ShapeDtypeStruct((16 * groups, dim), BF16), jax.ShapeDtypeStruct((16, dim), BF16),
+        ],
+        scratch_shapes=[
+            pltpu.VMEM((slots, toks, inner), BF16), pltpu.VMEM((inner, dim), F32), pltpu.VMEM((dim, inner), F32),
+            pltpu.VMEM((dim, inner), F32), pltpu.VMEM((8 * slots, dim), F32), pltpu.VMEM((max(runs - 1, 1), 8 * slots, dim), F32),
+            pltpu.VMEM((16 * groups, dim), BF16), pltpu.SemaphoreType.DMA((runs + groups,)),
+            pltpu.SemaphoreType.DMA((runs + groups,)), *reduce_shapes(main_parts, dim, runs, groups),
+            *reduce_shapes(rest_parts, dim, runs, groups),
+        ],
+        compiler_params=params(collective_id=4, has_side_effects=True),
+        name="tail",
     )(
-        tokens, cotangent, modulate, token_mask, counts2, hid, z_gate, y, dx, late, input_weight, output_weight,
-    )
-
-    small = 2 * (proj_rows + wide_rank + states + tap_count) + 8
-    rows = reduce_rows(dim, inner, small)
-    stages = int(math.log2(runs)) + int(math.log2(groups))
-    result, factors, own = pl.pallas_call(
-        functools.partial(reduce_kernel, (runs, groups, rows)),
-        in_specs=[vmem] * 11,
-        out_specs=[vmem] * 3,
-        out_shape=[
-            jax.ShapeDtypeStruct((rows, dim), BF16), jax.ShapeDtypeStruct((16 * groups, dim), BF16),
-            jax.ShapeDtypeStruct((16, dim), BF16),
-        ],
-        scratch_shapes=[
-            pltpu.VMEM((rows, dim), F32), pltpu.VMEM((rows + PARTS * LAST_ROWS * stages, dim), BF16),
-            pltpu.VMEM((rows + PARTS * LAST_ROWS * stages, dim), BF16),
-            pltpu.VMEM((rows, dim), BF16), pltpu.VMEM((16, dim), F32),
-            pltpu.VMEM((max(int(math.log2(runs)), 1), 16, dim), F32), pltpu.VMEM((16 * groups, dim), BF16),
-            pltpu.SemaphoreType.DMA((PARTS, 2 * stages)), pltpu.SemaphoreType.DMA((PARTS, 2 * stages)),
-            pltpu.SemaphoreType.DMA((stages,)), pltpu.SemaphoreType.DMA((stages,)),
-        ],
-        compiler_params=params(collective_id=4, has_side_effects=True),
-        name="reduce",
-    )(
-        in_grad, out_grad, xp_grad, dtp_grad, rate_grad, tap_grad, tapb_grad, skip_grad, dtb_grad, d_mod, timestep,
+        tokens, cotangent, modulate, token_mask, counts2, hid, z_gate, y, dx, late, input_weight, output_weight, timestep,
+        *smalls,
     )
 
     (
         d_time, grad_ada, grad_ada_bias, in_grad, tap_grad, tapb_grad, xp_grad, dtp_grad, dtb_grad, rate_grad, skip_grad,
         out_grad,
     ) = pl.pallas_call(
-        functools.partial(finish_kernel, (rank, wide_rank)),
-        in_specs=[vmem] * 5,
-        out_specs=[vmem] * 12,
+        finish_kernel,
+        grid=(4,),
+        in_specs=[
+            whole(main_parts * PART_ROWS, dim), whole(rest_parts * PART_ROWS, dim), whole(16 * groups, dim), whole(16, dim),
+            whole(slots, dim), whole(dim, 3 * dim),
+        ],
+        out_specs=[
+            whole(slots, dim), spec((dim, dim), lambda s: (0, jnp.minimum(s, 2))), whole(3 * dim),
+            spec((dim, 2 * inner // 4), lambda s: (0, s)), whole(2, tap_count, inner), whole(2, inner),
+            whole(2, rank + 2 * states, inner), whole(2, rank, inner), whole(2, inner), whole(2, states, inner), whole(2, inner),
+            spec((inner // 4, dim), lambda s: (s, 0)),
+        ],
         out_shape=[
             jax.ShapeDtypeStruct(shape, F32)
             for shape in (
@@ -1088,7 +1233,7 @@
         ],
         compiler_params=params(),
         name="finish",
-    )(result, factors, own, timestep, ada_weight)
+    )(result, x_result, factors, own, timestep, ada_weight)
     return (
         mixed, d_tokens, d_time, grad_ada, grad_ada_bias, in_grad, tap_grad, tapb_grad, jnp.swapaxes(xp_grad, 1, 2), dtp_grad, dtb_grad,
         rate_grad, skip_grad, out_grad,

time: 204 us -> 199 us (0.975)
  Pallas kernels: 202 us -> 195 us
    pallas_call x3 -> x2, Pallas kernels: 62.6 us -> 58.4 us  [the longest x1 52.5 us: per_device(): pl.pallas_call(functools.partial(tail_kernel, (runs, groups, slots)), gri...]
where the time goes in v6:
time: 199 us; the launch traced here: 198 us
  Pallas kernels  195 us (98%)
    pallas_call x1, Pallas kernels, per_device(): pl.pallas_call(functools.partial(second_kernel, runs), grid=(2, slots), i...  80.8 us
    pallas_call x1, Pallas kernels, per_device(): pl.pallas_call(functools.partial(tail_kernel, (runs, groups, slots)), gri...  52.5 us
    pallas_call x1, Pallas kernels, per_device(): pl.pallas_call(functools.partial(first_kernel, runs, slots), grid=(2, slo...  45.4 us
    pallas_call x1, Pallas kernels, per_device(): pl.pallas_call(functools.partial(enter_kernel, runs), grid=(slots,), in_s...  10.7 us
    pallas_call x1, Pallas kernels, per_device(): pl.pallas_call(finish_kernel, grid=(4,), in_specs=[whole(main_parts * PAR...  5.89 us

profile of v6, /device:TPU:0, one launch (start us, length us, event | category | flops | bytes accessed | tf_op | source)
XLA Modules:
  0.0 198.5 jit_solution(3410932696522503101)
XLA Ops:
  1.3 10.7 %enter.1 = (bf16[3,2,272,768]{3,2,1,0:T(8,128)(2,1)}, f32[3,2,256,768]{3,2,1,0:T(8,128)}, f32[3,256,768]{2,1,0:T(8,128)}, bf16[3,256,384]{2,1,0:T(8,128)(2,1)}, f32[3,1,1152]{2,1,0:T(1,128)}) custom-call(bf16[3,256,384]{2,1,0:T(8,128)(2,1)} %tok.3, bf16[3,256,384]{2,1,0:T(8,128)(2,1)} %cot.3, s32[3,256]{1,0:T(4,128)} %mask.3, s32[1,1]{1,0:T(1,128)} %bitcast.3.counts, ...), custom_call_target="tpu_custom_call" | custom-call | tf_op jit(solution)/shard_map/enter/pallas_call | solution.py:1054
  12.0 45.4 %first.1 = (bf16[3,2,256,768]{3,2,1,0:T(8,128)(2,1)}, f32[3,2,256,768]{3,2,1,0:T(8,128)}, f32[3,2,256,768]{3,2,1,0:T(8,128)}, f32[3,2,256,768]{3,2,1,0:T(8,128)}...) custom-call(bf16[3,2,272,768]{3,2,1,0:T(8,128)(2,1)} %get-tuple-elem, ...), custom_call_target="tpu_custom_call" | custom-call | tf_op jit(solution)/shard_map/first/pallas_call | solution.py:1091
  57.4 80.8 %second.1 = (f32[3,2,256,768]{3,2,1,0:T(8,128)}, f32[3,2,256,768]{3,2,1,0:T(8,128)}, f32[2,3,8,768]{3,2,1,0:T(8,128)}, f32[2,16,768]{2,1,0:T(8,128)}, f32[2,1,76...) custom-call(f32[3,16,768]{2,1,0:T(8,128)} %get-tuple-element.67.s_fi, ...), custom_call_target="tpu_custom_call" | custom-call | tf_op jit(solution)/shard_map/second/pallas_call | solution.py:1127
  138.2 52.5 %tail.1 = (bf16[3,256,384]{2,1,0:T(8,128)(2,1)}, f32[3,256,384]{2,1,0:T(8,128)}, bf16[2048,384]{1,0:T(8,128)(2,1)}, bf16[1024,384]{1,0:T(8,128)(2,1)}, bf16[128,...) custom-call(bf16[3,256,384]{2,1,0:T(8,128)(2,1)} %tok.3, bf16[3,256,384]{2,1,0:T(8,128)(2,1)} %cot.3, ...), custom_call_target="tpu_custom_call" | custom-call | tf_op jit(solution)/shard_map/tail/pallas_call | solution.py:1180
  190.8 0.0 copy-start.1
  190.8 0.0 copy-start
  190.8 5.9 %finish.1 = (f32[3,384]{1,0:T(4,128)}, f32[384,1152]{1,0:T(8,128)}, f32[1152]{0:T(1024)}, f32[384,1536]{1,0:T(8,128)}, f32[2,4,768]{2,1,0:T(4,128)}, /*index=5*/...) custom-call(bf16[2048,384]{1,0:T(8,128)(2,1)} %get-tuple-element.94., ...), custom_call_target="tpu_custom_call" | custom-call | tf_op jit(solution)/shard_map/finish/pallas_call | solution.py:1214
  196.7 0.0 copy-done.1
  196.7 0.8 copy.33
  197.5 0.0 copy-done
  197.5 1.0 copy.34
Async XLA Ops:
  190.8 5.9 %copy-start.1 = (bf16[3,256,384]{2,1,0:T(8,128)(2,1)S(1)}, bf16[3,256,384]{2,1,0:T(8,128)(2,1)}, u32[]{:S(2)}) copy-start(bf16[3,256,384]{2,1,0:T(8,128)(2,1)} %get-tuple-element.124) | copy-start | bytes 1769476
  190.8 6.7 %copy-start = (f32[3,256,384]{2,1,0:T(8,128)S(1)}, f32[3,256,384]{2,1,0:T(8,128)}, u32[]{:S(2)}) copy-start(f32[3,256,384]{2,1,0:T(8,128)} %get-tuple-element.125) | copy-start | bytes 3538948

commit v7 on v6

--- a/solution.py
+++ b/solution.py
@@ -10,6 +10,7 @@
 
 EPSILON = 1e-06
 BLK = 16
+WIDE_RANK = 32
 HALO = 16
 LOG2E = math.log2(math.e)
 F32, BF16 = jnp.float32, jnp.bfloat16
@@ -83,7 +84,7 @@
     def _():
         pl.semaphore_signal(barrier, inc=1, device_id={"seq": me + 1}, device_id_type=MESH)
 
-    neighbours = (me + runs - 1) // runs + (2 * runs - 2 - me) // runs
+    neighbours = lax.div(me + runs - 1, runs) + lax.div(2 * runs - 2 - me, runs)
     pl.semaphore_wait(barrier, neighbours + len(others))
 
 
@@ -229,7 +230,7 @@
 
 
 def bit_of(index, bit):
-    return (index // (1 << bit)) % 2
+    return lax.rem(lax.div(index, 1 << bit), 2)
 
 
 def across(axis, bit):
@@ -245,7 +246,8 @@
         self.group, self.span, self.pre, self.pre_span = group, span, pre, pre_span
         self.sends, self.arrivals, self.sems = sends, arrivals, sems
         self.links = [across("seq", bit) for bit in range(int(math.log2(runs)))]
-        self.slots, self.states, self.inner = ends.shape
+        self.slots = ends.shape[0]
+        self.states, self.inner = rate.shape
 
     def flow(self, kind):
         return kind if self.branch == 0 else 1 - kind
@@ -300,7 +302,7 @@
             for kind in range(2):
                 for i in range(self.slots):
                     self.group[kind, i] = self.sources[kind][i]
-                    self.span[kind, i : i + 1, :] = self.totals[i]
+                    self.span[kind, i : i + 1, :] = self.totals[i][:1]
                 if count:
                     self.send(0, kind)
 
@@ -343,16 +345,20 @@
 
 def first_kernel(
     runs, slots, xe, dy, taps, tap_bias, x_rows, dt_rows, dt_bias, rate,
-    act_out, dsilu_out, delta_out, sig_out, proj_out, end_out, back_out, total_out, starts_out, sums_out, tiles, xwt, dtw, s_in, lam_in,
+    act_out, planes, proj_out, last_out, starts_out, tiles, weights, first_in,
     dx, decay, through, rate2, wide, picks, ends, backs, totals, first_rate, *exchange_scratch,
 ):
     toks, inner = dy.shape
     states = rate.shape[0]
     blocks = toks // BLK
-    rank = dtw.shape[0]
+    rank = WIDE_RANK
+    xwt, dtw = weights.at[: weights.shape[0] - rank], weights.at[weights.shape[0] - rank :]
+    delta_out, sig_out, dsilu_out = (planes.at[at] for at in range(3))
+    end_out, back_out = last_out.at[:states], last_out.at[states : 2 * states]
     tap_count = taps.shape[0]
     branch, item = pl.program_id(0), pl.program_id(1)
-    exchange = Exchange(runs, 0, ends, backs, totals, first_rate, (s_in, lam_in), *exchange_scratch)
+    results = (first_in.at[0], first_in.at[1])
+    exchange = Exchange(runs, 0, ends, backs, totals, first_rate, results, *exchange_scratch)
 
     @pl.when((branch == 0) & (item == 0))
     def _():
@@ -371,8 +377,8 @@
         held = dt_rows.shape[0]
         rows = x_rows[...].astype(F32)
         gap = jnp.zeros((rank - held, inner), F32)
-        xwt[...] = jnp.concatenate([rows[:held], gap, rows[held:]], axis=0).astype(BF16)
-        dtw[...] = jnp.concatenate([dt_rows[...].astype(F32), gap], axis=0).astype(BF16)
+        wide = [rows[:held], gap, rows[held:], dt_rows[...].astype(F32), gap]
+        weights[...] = jnp.concatenate(wide, axis=0).astype(BF16)
 
     tap_row, dt_row = tap_bias[pl.ds(branch, 1), :], dt_bias[pl.ds(branch, 1), :]
     for cols in columns(inner):
@@ -404,9 +410,8 @@
         count = 2 * states
         wide_rows = wide.at[pl.ds(pl.multiple_of(j * (BLK * count), BLK * count), BLK * count), :]
         s = end_out[...]
-        starts_out[j] = s
         before = through[...]
-        sums_out[j] = before[:1, :]
+        starts_out[j] = jnp.concatenate([s, before], axis=0)
         rates = rate2[...]
         for i in range(BLK):
             a = jnp.exp2(spread(dr, i) * rates)
@@ -427,7 +432,7 @@
         return 0
 
     lax.fori_loop(0, blocks // 2, block_step, 0)
-    total_out[...] = through[:1, :]
+    last_out[2 * states :, :] = through[...]
 
     @pl.when(branch == 0)
     def _():
@@ -437,16 +442,23 @@
 
 
 def second_kernel(
-    runs, s_first, lam_first, ends, backs, totals, last_rate, starts, sums, tiles, rate, xe, act, dsilu, delta, sig, dy, proj, xwt, dtw, taps, skip,
-    y_out, dx_out, late_out, rate_grad, skip_grad, dtb_grad, dtp_grad, xp_grad, tap_grad, tapb_grad,
+    runs, first_in, lasts, last_rate, starts, tiles, rate, xe, act, planes, dy, proj, weights, taps, skip,
+    y_out, dx_out, late_out, grads,
     rate2, carry, dxs, bdiag, cdiag, decay, states_low, lam_low, rq_low, qd_low, dots, racc, gsum, hsum, db, dc,
     rims, late, send_sem, recv_sem, d_pre_low, s_in, s_last, lam_last, *exchange_scratch,
 ):
     toks, inner = dy.shape
     states = rate.shape[0]
     blocks = toks // BLK
-    rank = dtw.shape[0]
+    rank = WIDE_RANK
+    xwt, dtw = weights.at[: weights.shape[0] - rank], weights.at[weights.shape[0] - rank :]
+    delta, sig, dsilu = (planes.at[at] for at in range(3))
     tap_count = taps.shape[0]
+    held = (grads.shape[0] - 3 * states - 8) // 2
+    xp_grad, dtp_grad = grads.at[: held + 2 * states], grads.at[held + 2 * states : 2 * held + 2 * states]
+    at = 2 * held + 2 * states
+    rate_grad, row_grads = grads.at[at : at + states], grads.at[at + states : at + states + 8]
+    tapb_at, skip_at, dtb_at = (slice(tap_count + row, tap_count + row + 1) for row in range(3))
     item = pl.program_id(1)
     last_item = item == pl.num_programs(1) - 1
     me = lax.axis_index("seq")
@@ -454,7 +466,9 @@
     ups = [(rims.at[1], late.at[1], send_sem.at[1], recv_sem.at[1])]
 
     branch = pl.program_id(0)
-    slots = ends.shape[0]
+    slots = lasts.shape[0]
+    ends, backs = lasts.at[:, :states], lasts.at[:, states : 2 * states]
+    totals = lasts.at[:, 2 * states :]
     exchange = Exchange(runs, 1, ends, backs, totals, last_rate, (s_last, lam_last), *exchange_scratch)
 
     @pl.when((item == 0) & (branch == 0))
@@ -465,8 +479,8 @@
 
     @pl.when(branch == 0)
     def _():
-        s_in[...] = s_first[item]
-        carry[...] = lam_first[item]
+        s_in[...] = first_in[0, item]
+        carry[...] = first_in[1, item]
 
     @pl.when(branch == 1)
     def _():
@@ -479,8 +493,7 @@
 
     @pl.when(item == 0)
     def _():
-        for ref in (rate_grad, skip_grad, dtb_grad, dtp_grad, xp_grad, tap_grad, tapb_grad):
-            ref[...] = jnp.zeros(ref.shape, ref.dtype)
+        grads[...] = jnp.zeros(grads.shape, F32)
 
     for cols in columns(inner):
         dxs[:toks, cols] = delta[:, cols] * act[:, cols].astype(F32)
@@ -519,7 +532,8 @@
         tile = tiles.at[pl.ds(t0, BLK)]
         r2 = rate2[...]
         r_low = rate[...].astype(BF16)
-        s = starts[j] + s_in[...] * jnp.exp2(twice(jnp.broadcast_to(sums[j], (8, inner))) * r2)
+        begin = starts[j]
+        s = begin[:states] + s_in[...] * jnp.exp2(twice(begin[states:]) * r2)
         states_low[slot, :states, :] = s.astype(BF16)
         for i in range(BLK):
             a = jnp.exp2(spread(dr, i) * r2)
@@ -559,12 +573,11 @@
     rate_grad[...] += -racc[...]
     for cols in columns(inner):
         act_f = act[:, cols].astype(F32)
-        skip_grad[:, cols] += jnp.sum(dy[:, cols] * act_f, axis=0, keepdims=True)
+        row_grads[skip_at, cols] += jnp.sum(dy[:, cols] * act_f, axis=0, keepdims=True)
         y_out[:, cols] += gain[:, cols] * act_f
         d_pre = (act_f * gsum[:toks, cols] - hsum[:toks, cols]) * sig[:, cols]
-        dtb_grad[:, cols] += jnp.sum(d_pre, axis=0, keepdims=True)
+        row_grads[dtb_at, cols] += jnp.sum(d_pre, axis=0, keepdims=True)
         d_pre_low[:, cols] = d_pre.astype(BF16)
-    held = dtp_grad.shape[0]
     dtp_grad[...] += dot(proj[:rank, :].astype(BF16), d_pre_low[...])[:held]
     d_proj = jnp.concatenate(
         [dot_nt(dtw[...], d_pre_low[...]), dot_nt(fold, db[:toks, :]), dot_nt(fold, dc[:toks, :])], axis=0
@@ -579,14 +592,14 @@
             cols = slice(wide_cols.start + at.start, wide_cols.start + at.stop)
             d_act = delta[:, cols] * gsum[:toks, cols] + gain[:, cols] * dy[:, cols] + through[:, at]
             d_conv = d_act * dsilu[:, cols]
-            tapb_grad[:, cols] += jnp.sum(d_conv, axis=0, keepdims=True)
+            row_grads[tapb_at, cols] += jnp.sum(d_conv, axis=0, keepdims=True)
             x_f = xe[:, cols].astype(F32)
             base = jnp.concatenate([jnp.zeros((HALO, 128), F32), d_conv], axis=0)
             d_window = taps[tap_count - 1 : tap_count, cols] * base
-            tap_grad[tap_count - 1 : tap_count, cols] += jnp.sum(d_conv * x_f[HALO:], axis=0, keepdims=True)
+            row_grads[tap_count - 1 : tap_count, cols] += jnp.sum(d_conv * x_f[HALO:], axis=0, keepdims=True)
             for k in range(tap_count - 1):
                 moved = pltpu.roll(base, window - (tap_count - 1 - k), 0)
-                tap_grad[k : k + 1, cols] += jnp.sum(moved * x_f, axis=0, keepdims=True)
+                row_grads[k : k + 1, cols] += jnp.sum(moved * x_f, axis=0, keepdims=True)
                 d_window = d_window + taps[k : k + 1, cols] * moved
             rims[branch, item, :, cols] = d_window[HALO - 8 : HALO]
             dx_out[:, cols] = d_window[HALO:]
@@ -623,7 +636,7 @@
         self.place = sum(digit * (1 << at) for at, digit in enumerate(self.digits))
 
     def target(self, ahead):
-        place = (self.place + ahead) % self.size
+        place = lax.rem(self.place + ahead, self.size)
         where = {}
         for at, (axis, bit) in enumerate(self.bits):
             base = where.get(axis, lax.axis_index(axis))
@@ -732,7 +745,7 @@
             values = [held.astype(BF16).astype(F32)] + came
             total = jnp.zeros_like(held)
             for place in range(ring.size):
-                behind = (ring.place - place + ring.size) % ring.size
+                behind = lax.rem(ring.place - place + ring.size, ring.size)
                 chosen = values[0]
                 for ahead in range(1, ring.size):
                     chosen = jnp.where(behind == ahead, values[ahead], chosen)
@@ -792,25 +805,17 @@
     ]
 
 
-def small_segments(refs, tails, dim):
-    inner = refs[0].shape[2]
-    blocks = [(lambda ref=ref, branch=branch: ref[branch], ref.shape[1]) for ref in refs for branch in range(2)]
-
-    def tail():
-        lines = [ref[branch] for ref in tails for branch in range(2)]
-        return jnp.concatenate(lines + [jnp.zeros((8 - len(lines), inner), F32)], axis=0)
-
-    blocks.append((tail, 8))
+def small_segments(ref, dim):
     return [
-        (lambda at, size, get=get, lane=lane: get()[at : at + size, lane : lane + dim], size)
-        for lane in range(0, inner, dim)
-        for get, size in blocks
+        (lambda at, size, branch=branch, lane=lane: ref[branch, at : at + size, lane : lane + dim], ref.shape[1])
+        for lane in range(0, ref.shape[2], dim)
+        for branch in range(2)
     ]
 
 
 def tail_kernel(
     plan, tok, cot, mod, mask, counts, hid, z_in, y, dx, late, win, wout, step,
-    xp_grad, dtp_grad, rate_grad, tap_grad, tapb_grad, skip_grad, dtb_grad,
+    grads,
     mixed, d_tokens, result, x_result, factors, own_rows,
     dz, out_grad, z_grad, x_grad, mod_sum, mod_in, table, small_send, small_recv, *reduce_scratch,
 ):
@@ -818,12 +823,12 @@
     dim = tok.shape[-1]
     toks, inner = z_in.shape
     now = pl.program_id(0)
-    i = now % slots
+    i = lax.rem(now, slots)
     rings = stage_rings(runs, groups)
     seq_ring = Ring([("seq", bit) for bit in range(int(math.log2(runs)))])
     dp_ring = Ring([("dp", bit) for bit in range(int(math.log2(groups)))])
     half = len(reduce_scratch) // 2
-    smalls = small_segments((xp_grad, dtp_grad, rate_grad, tap_grad), (tapb_grad, skip_grad, dtb_grad), dim)
+    smalls = small_segments(grads, dim)
     segments = big_segments(out_grad, dim) + big_segments(z_grad, dim) + smalls
     main = Reduction(rings, [part % 3 // 2 for part in range(result.shape[0] // PART_ROWS)], segments, *reduce_scratch[:half])
     rest = Reduction(rings, [part % 2 for part in range(x_result.shape[0] // PART_ROWS)], big_segments(x_grad, dim), *reduce_scratch[half:])
@@ -915,7 +920,7 @@
         values = [mod_sum[...]] + [mod_in[ahead - 1] for ahead in range(1, seq_ring.size)]
         total = jnp.zeros(mod_sum.shape, F32)
         for place in range(seq_ring.size):
-            behind = (seq_ring.place - place + seq_ring.size) % seq_ring.size
+            behind = lax.rem(seq_ring.place - place + seq_ring.size, seq_ring.size)
             chosen = values[0]
             for ahead in range(1, seq_ring.size):
                 chosen = jnp.where(behind == ahead, values[ahead], chosen)
@@ -951,53 +956,32 @@
 
 
 def finish_kernel(
-    result, x_result, factors, own, step, ada,
+    outs, zs, xs, smalls, factors, own, step, ada,
     grad_time, grad_ada, grad_ada_bias, in_grad, tap_grad, tapb_grad, xp_grad, dtp_grad, dtb_grad, rate_grad, skip_grad, out_grad,
 ):
     dim, inner = in_grad.shape[0], rate_grad.shape[2]
     slots = step.shape[0]
-
     now = pl.program_id(0)
-
-    def rows(at, size):
-        return result[at : at + size, :].astype(F32)
-
-    out_rows = out_grad.shape[0]
-    out_grad[...] = result[pl.ds(pl.multiple_of(now * out_rows, out_rows), out_rows), :].astype(F32)
-    pieces = inner // dim
-
-    @pl.when(now < pieces)
-    def _():
-        in_grad[...] = x_result[pl.ds(pl.multiple_of(now * dim, dim), dim), :].astype(F32)
-
-    @pl.when(now >= pieces)
-    def _():
-        in_grad[...] = result[pl.ds(pl.multiple_of(inner + (now - pieces) * dim, dim), dim), :].astype(F32)
-
-
+    out_grad[...] = outs[...].astype(F32)
+    in_grad[...] = jnp.where(now < inner // dim, xs[...], zs[...]).astype(F32)
     table = factors[...]
     length = table.shape[0]
-    items = length // 16 * 8
-
-    def pick(place):
-        row = lax.broadcasted_iota(jnp.int32, (items, length), 0)
-        col = lax.broadcasted_iota(jnp.int32, (items, length), 1)
-        slot = row % 8
-        wanted = row // 8 * 16 + place(slot)
-        return dot(((col == wanted) & (slot < slots)).astype(BF16), table)
 
     for part in range(3):
 
         @pl.when(now == part)
         def _():
-            times = pick(lambda slot: 3 * slots + slot).astype(BF16)
-            mods = pick(lambda slot: 3 * slot + part)
+            row = lax.broadcasted_iota(jnp.int32, (length, length), 0)
+            col = lax.broadcasted_iota(jnp.int32, (length, length), 1)
+            item = row % 16 - 3 * slots
+            wanted = row // 16 * 16 + 3 * item + part
+            mods = dot(((col == wanted) & (item >= 0) & (item < slots)).astype(BF16), table)
             lanes = slice(part * dim, (part + 1) * dim)
-            grad_ada[...] = dot_tn(times, mods.astype(BF16))
+            grad_ada[...] = dot_tn(table, mods.astype(BF16))
             grad_ada_bias[lanes] = jnp.sum(mods, axis=0)
             mine = own[...].astype(F32)
             picked = jnp.concatenate([mine[3 * i + part : 3 * i + part + 1] for i in range(slots)], axis=0)
-            d_time = dot_nt(picked.astype(BF16), ada[:, lanes])
+            d_time = dot_nt(picked.astype(BF16), ada[...])
             grad_time[...] = d_time if part == 0 else grad_time[...] + d_time
 
     @pl.when(now == 3)
@@ -1005,19 +989,18 @@
         time_f = step[...].astype(F32)
         time_sig = jax.nn.sigmoid(time_f)
         grad_time[...] = grad_time[...] * time_sig * (1.0 + time_f * (1.0 - time_sig))
-        at = 2 * inner
+        at = 0
         for first in range(0, inner, dim):
             lanes = slice(first, first + dim)
-            for ref in (xp_grad, dtp_grad, rate_grad, tap_grad):
-                size = ref.shape[1]
-                for branch in range(2):
-                    ref[branch, :, lanes] = rows(at, size)
+            for branch in range(2):
+                for ref in (xp_grad, dtp_grad, rate_grad, tap_grad):
+                    size = ref.shape[1]
+                    ref[branch, :, lanes] = smalls[at : at + size, :].astype(F32)
                     at += size
-            tail = rows(at, 8)
-            tapb_grad[:, lanes] = tail[0:2]
-            skip_grad[:, lanes] = tail[2:4]
-            dtb_grad[:, lanes] = tail[4:6]
-            at += 8
+                for ref in (tapb_grad, skip_grad, dtb_grad):
+                    ref[branch : branch + 1, lanes] = smalls[at : at + 1, :].astype(F32)
+                    at += 1
+                at += 1
 
 
 def params(**more):
@@ -1037,7 +1020,7 @@
     rank = dt_weight.shape[1]
     states = decay_rate.shape[1]
     tap_count = conv_weight.shape[1]
-    wide_rank = 32
+    wide_rank = WIDE_RANK
     proj_rows = wide_rank + 2 * states
     blocks = toks // BLK
     runs = lax.axis_size("seq")
@@ -1088,7 +1071,7 @@
     def unit_shape(*block, kind=F32):
         return jax.ShapeDtypeStruct((slots, 2) + block, kind)
 
-    act, dsilu, delta, sig, proj, end, back, total, starts, sums, tiles, xwt, dtw, s_first, lam_first = pl.pallas_call(
+    act, planes, proj, lasts, starts, tiles, weights, first_in = pl.pallas_call(
         functools.partial(first_kernel, runs, slots),
         grid=(2, slots),
         in_specs=[
@@ -1096,17 +1079,15 @@
             branch(rank + 2 * states, inner), branch(rank, inner), whole(2, inner), branch(states, inner),
         ],
         out_specs=[
-            unit(toks, inner), unit(toks, inner), unit(toks, inner), unit(toks, inner), unit(proj_rows, toks),
-            unit(states, inner), unit(states, inner), unit(1, inner), unit(blocks, states, inner), unit(blocks, 1, inner),
-            unit(toks, 2 * states, 128), branch(proj_rows, inner), branch(wide_rank, inner),
-            whole(slots, states, inner), whole(slots, states, inner),
+            unit(toks, inner), unit(3, toks, inner), unit(proj_rows, toks), unit(2 * states + 8, inner),
+            unit(blocks, states + 8, inner), unit(toks, 2 * states, 128), branch(proj_rows + wide_rank, inner),
+            whole(2, slots, states, inner),
         ],
         out_shape=[
-            unit_shape(toks, inner, kind=BF16), unit_shape(toks, inner), unit_shape(toks, inner), unit_shape(toks, inner),
-            unit_shape(proj_rows, toks), unit_shape(states, inner), unit_shape(states, inner), unit_shape(1, inner),
-            unit_shape(blocks, states, inner), unit_shape(blocks, 1, inner), unit_shape(toks, 2 * states, 128),
-            jax.ShapeDtypeStruct((2, proj_rows, inner), BF16), jax.ShapeDtypeStruct((2, wide_rank, inner), BF16),
-            jax.ShapeDtypeStruct((slots, states, inner), F32), jax.ShapeDtypeStruct((slots, states, inner), F32),
+            unit_shape(toks, inner, kind=BF16), unit_shape(3, toks, inner), unit_shape(proj_rows, toks),
+            unit_shape(2 * states + 8, inner), unit_shape(blocks, states + 8, inner), unit_shape(toks, 2 * states, 128),
+            jax.ShapeDtypeStruct((2, proj_rows + wide_rank, inner), BF16),
+            jax.ShapeDtypeStruct((2, slots, states, inner), F32),
         ],
         scratch_shapes=[
             pltpu.VMEM((toks, inner), F32), pltpu.VMEM((2, BLK, states, inner), F32), pltpu.VMEM((8, inner), F32),
@@ -1120,28 +1101,22 @@
     )(xe, dy, conv_weight, conv_bias, x_rows, dt_weight, dt_bias, decay_rate)
 
     vmem = pl.BlockSpec(memory_space=pltpu.VMEM)
-    last = spec((slots, None, states, inner), lambda b, i: (0, 1, 0, 0))
-    last_total = spec((slots, None, 1, inner), lambda b, i: (0, 1, 0, 0))
+    last = spec((slots, None, 2 * states + 8, inner), lambda b, i: (0, 1, 0, 0))
     last_branch = spec((None, states, inner), lambda b, i: (1, 0, 0))
 
-    y, dx, late, rate_grad, skip_grad, dtb_grad, dtp_grad, xp_grad, tap_grad, tapb_grad = pl.pallas_call(
+    grad_rows = 2 * rank + 3 * states + 8
+    y, dx, late, grads = pl.pallas_call(
         functools.partial(second_kernel, runs),
         grid=(2, slots),
         in_specs=[
-            whole(slots, states, inner), whole(slots, states, inner), last, last, last_total, last_branch,
-            unit(blocks, states, inner), unit(blocks, 1, inner), unit(toks, 2 * states, 128), branch(states, inner), unit(HALO + toks, inner), unit(toks, inner),
-            unit(toks, inner), unit(toks, inner), unit(toks, inner), unit(toks, inner), unit(proj_rows, toks),
-            branch(proj_rows, inner), branch(wide_rank, inner),
-            branch(tap_count, inner), whole(2, inner),
-        ],
-        out_specs=[
-            unit(toks, inner), unit(toks, inner), whole(2, slots, 8, inner), branch(states, inner), branch(1, inner), branch(1, inner),
-            branch(rank, inner), branch(rank + 2 * states, inner), branch(tap_count, inner), branch(1, inner),
-        ],
+            whole(2, slots, states, inner), last, last_branch, unit(blocks, states + 8, inner), unit(toks, 2 * states, 128),
+            branch(states, inner), unit(HALO + toks, inner), unit(toks, inner), unit(3, toks, inner), unit(toks, inner),
+            unit(proj_rows, toks), branch(proj_rows + wide_rank, inner), branch(tap_count, inner), whole(2, inner),
+        ],
+        out_specs=[unit(toks, inner), unit(toks, inner), whole(2, slots, 8, inner), branch(grad_rows, inner)],
         out_shape=[
             unit_shape(toks, inner), unit_shape(toks, inner), jax.ShapeDtypeStruct((2, slots, 8, inner), F32),
-        ] + [
-            jax.ShapeDtypeStruct((2, rows, inner), F32) for rows in (states, 1, 1, rank, rank + 2 * states, tap_count, 1)
+            jax.ShapeDtypeStruct((2, grad_rows, inner), F32),
         ],
         scratch_shapes=[
             pltpu.VMEM((states, inner), F32), pltpu.VMEM((states, inner), F32), pltpu.VMEM((toks + BLK, inner), F32), pltpu.VMEM((toks + BLK, BLK * states), BF16),
@@ -1160,8 +1135,7 @@
         compiler_params=params(collective_id=3, has_side_effects=True),
         name="second",
     )(
-        s_first, lam_first, end, back, total, decay_rate, starts, sums, tiles, decay_rate, xe, act, dsilu, delta,
-        sig, dy, proj, xwt, dtw, conv_weight, skip_gain,
+        first_in, lasts, decay_rate, starts, tiles, decay_rate, xe, act, planes, dy, proj, weights, conv_weight, skip_gain,
     )
 
     def now(*block):
@@ -1173,8 +1147,7 @@
     def after(*block):
         return spec((None,) + block, lambda s: (jnp.maximum(s - slots, 0),) + (0,) * len(block))
 
-    smalls = (xp_grad, dtp_grad, rate_grad, tap_grad, tapb_grad, skip_grad, dtb_grad)
-    small_rows = (2 * sum(ref.shape[1] for ref in smalls[:4]) + 8) * (inner // dim)
+    small_rows = 2 * grad_rows * (inner // dim)
     main_parts = part_count(inner + dim * (inner // dim) + small_rows)
     rest_parts = part_count(dim * (inner // dim))
     mixed, d_tokens, result, x_result, factors, own = pl.pallas_call(
@@ -1183,7 +1156,7 @@
         in_specs=[
             now(toks, dim), now(toks, dim), now(1, 3 * dim), whole(slots, toks), whole(1, 1), now(toks, dim),
             early(toks, inner), early(2, toks, inner), after(2, toks, inner), whole(2, slots, 8, inner),
-            whole(dim, 2 * inner), whole(inner, dim), whole(slots, dim), *[whole(*ref.shape) for ref in smalls],
+            whole(dim, 2 * inner), whole(inner, dim), whole(slots, dim), whole(2, grad_rows, inner),
         ],
         out_specs=[
             early(toks, dim), after(toks, dim), whole(main_parts * PART_ROWS, dim), whole(rest_parts * PART_ROWS, dim),
@@ -1204,8 +1177,7 @@
         compiler_params=params(collective_id=4, has_side_effects=True),
         name="tail",
     )(
-        tokens, cotangent, modulate, token_mask, counts2, hid, z_gate, y, dx, late, input_weight, output_weight, timestep,
-        *smalls,
+        tokens, cotangent, modulate, token_mask, counts2, hid, z_gate, y, dx, late, input_weight, output_weight, timestep, grads,
     )
 
     (
@@ -1215,8 +1187,11 @@
         finish_kernel,
         grid=(4,),
         in_specs=[
-            whole(main_parts * PART_ROWS, dim), whole(rest_parts * PART_ROWS, dim), whole(16 * groups, dim), whole(16, dim),
-            whole(slots, dim), whole(dim, 3 * dim),
+            spec((inner // 4, dim), lambda s: (s, 0)),
+            spec((dim, dim), lambda s: (inner // dim + jnp.maximum(s - inner // dim, 0), 0)),
+            spec((dim, dim), lambda s: (jnp.minimum(s, inner // dim - 1), 0)),
+            spec((PART_ROWS, dim), lambda s: (2 * inner // PART_ROWS, 0)),
+            whole(16 * groups, dim), whole(16, dim), whole(slots, dim), spec((dim, dim), lambda s: (0, jnp.minimum(s, 2))),
         ],
         out_specs=[
             whole(slots, dim), spec((dim, dim), lambda s: (0, jnp.minimum(s, 2))), whole(3 * dim),
@@ -1233,7 +1208,7 @@
         ],
         compiler_params=params(),
         name="finish",
-    )(result, x_result, factors, own, timestep, ada_weight)
+    )(result, result, x_result, result, factors, own, timestep, ada_weight)
     return (
         mixed, d_tokens, d_time, grad_ada, grad_ada_bias, in_grad, tap_grad, tapb_grad, jnp.swapaxes(xp_grad, 1, 2), dtp_grad, dtb_grad,
         rate_grad, skip_grad, out_grad,

time: 199 us -> 196 us (0.985)
  Pallas kernels: 195 us -> 193 us
    pallas_call x1, Pallas kernels: 80.8 us -> 78.8 us  [per_device(): pl.pallas_call(functools.partial(second_kernel, runs), grid=(2, slots), i...]
where the time goes in v7:
time: 196 us
  Pallas kernels  193 us (98%)
    pallas_call x1, Pallas kernels, per_device(): pl.pallas_call(functools.partial(second_kernel, runs), grid=(2, slots), i...  78.8 us
    pallas_call x1, Pallas kernels, per_device(): pl.pallas_call(functools.partial(tail_kernel, (runs, groups, slots)), gri...  51.8 us
    pallas_call x1, Pallas kernels, per_device(): pl.pallas_call(functools.partial(first_kernel, runs, slots), grid=(2, slo...  45.4 us
    pallas_call x1, Pallas kernels, per_device(): pl.pallas_call(functools.partial(enter_kernel, runs), grid=(slots,), in_s...  10.7 us
    pallas_call x1, Pallas kernels, per_device(): pl.pallas_call(finish_kernel, grid=(4,), in_specs=[spec((inner // 4, dim)...  5.86 us

profile of v7, /device:TPU:0, one launch (start us, length us, event | category | flops | bytes accessed | tf_op | source)
XLA Modules:
  0.0 195.8 jit_solution(15646128767577524394)
XLA Ops:
  1.3 10.7 %enter.1 = (bf16[3,2,272,768]{3,2,1,0:T(8,128)(2,1)}, f32[3,2,256,768]{3,2,1,0:T(8,128)}, f32[3,256,768]{2,1,0:T(8,128)}, bf16[3,256,384]{2,1,0:T(8,128)(2,1)}, f32[3,1,1152]{2,1,0:T(1,128)}) custom-call(bf16[3,256,384]{2,1,0:T(8,128)(2,1)} %tok.3, bf16[3,256,384]{2,1,0:T(8,128)(2,1)} %cot.3, s32[3,256]{1,0:T(4,128)} %mask.3, s32[1,1]{1,0:T(1,128)} %bitcast.3.counts, ...), custom_call_target="tpu_custom_call" | custom-call | tf_op jit(solution)/shard_map/enter/pallas_call | solution.py:1037
  12.0 45.4 %first.1 = (bf16[3,2,256,768]{3,2,1,0:T(8,128)(2,1)}, f32[3,2,3,256,768]{4,3,2,1,0:T(8,128)}, f32[3,2,64,256]{3,2,1,0:T(8,128)}, f32[3,2,40,768]{3,2,1,0:T(8,128...) custom-call(bf16[3,2,272,768]{3,2,1,0:T(8,128)(2,1)} %get-tuple-elem, ...), custom_call_target="tpu_custom_call" | custom-call | tf_op jit(solution)/shard_map/first/pallas_call | solution.py:1074
  57.4 78.8 %second.1 = (f32[3,2,256,768]{3,2,1,0:T(8,128)}, f32[3,2,256,768]{3,2,1,0:T(8,128)}, f32[2,3,8,768]{3,2,1,0:T(8,128)}, f32[2,104,768]{2,1,0:T(8,128)}) custom-call(f32[2,3,16,768]{3,2,1,0:T(8,128)} %get-tuple-element.54.first_in, f32[3,2,40,768]{3,2,1,0:T(8,128)} %get-tuple-element.55.lasts, f32[2,16,768]{2,1,0:T(8,128)} %rate.3, ...), custom_call_target="tpu_custom_call" | custom-call | tf_op jit(solution)/shard_map/second/pallas_call | solution.py:1108
  136.2 51.8 %tail.1 = (bf16[3,256,384]{2,1,0:T(8,128)(2,1)}, f32[3,256,384]{2,1,0:T(8,128)}, bf16[2048,384]{1,0:T(8,128)(2,1)}, bf16[1024,384]{1,0:T(8,128)(2,1)}, bf16[128,...) custom-call(bf16[3,256,384]{2,1,0:T(8,128)(2,1)} %tok.3, bf16[3,256,384]{2,1,0:T(8,128)(2,1)} %cot.3, ...), custom_call_target="tpu_custom_call" | custom-call | tf_op jit(solution)/shard_map/tail/pallas_call | solution.py:1153
  188.0 0.0 copy-start.1
  188.1 0.0 copy-start
  188.1 5.9 %finish.1 = (f32[3,384]{1,0:T(4,128)}, f32[384,1152]{1,0:T(8,128)}, f32[1152]{0:T(1024)}, f32[384,1536]{1,0:T(8,128)}, f32[2,4,768]{2,1,0:T(4,128)}, /*index=5*/...) custom-call(bf16[2048,384]{1,0:T(8,128)(2,1)} %get-tuple-element.68., ...), custom_call_target="tpu_custom_call" | custom-call | tf_op jit(solution)/shard_map/finish/pallas_call | solution.py:1186
  193.9 0.0 copy-done.1
  193.9 0.8 copy.33
  194.8 0.0 copy-done
  194.8 1.0 copy.34
Async XLA Ops:
  188.0 5.9 %copy-start.1 = (bf16[3,256,384]{2,1,0:T(8,128)(2,1)S(1)}, bf16[3,256,384]{2,1,0:T(8,128)(2,1)}, u32[]{:S(2)}) copy-start(bf16[3,256,384]{2,1,0:T(8,128)(2,1)} %get-tuple-element.98) | copy-start | bytes 1769476
  188.1 6.7 %copy-start = (f32[3,256,384]{2,1,0:T(8,128)S(1)}, f32[3,256,384]{2,1,0:T(8,128)}, u32[]{:S(2)}) copy-start(f32[3,256,384]{2,1,0:T(8,128)} %get-tuple-element.99) | copy-start | bytes 3538948

commit v8 on v7

--- a/solution.py
+++ b/solution.py
@@ -509,7 +509,6 @@
         lax.broadcasted_iota(jnp.int32, (2 * BLK, 256), 0) // BLK == lax.broadcasted_iota(jnp.int32, (2 * BLK, 256), 1) // 128
     ).astype(BF16)
     racc[...] = jnp.zeros((states, inner), F32)
-    qd_low[1] = jnp.zeros(qd_low.shape[1:], BF16)
 
     def lane_sum(wide):
         part = [wide[:, at : at + 128] for at in range(0, inner, 128)]
@@ -519,6 +518,7 @@
 
     def products(slot, j):
         t0 = pl.multiple_of(j * BLK, BLK)
+        y_out[pl.ds(t0, BLK), :] = dot(cdiag[pl.ds(t0, BLK), :], states_low[slot, states:, :])
         gsum[pl.ds(t0, BLK), :] = dot(bdiag[pl.ds(t0, BLK), :], lam_low[slot])
         hsum[pl.ds(t0, BLK), :] = dot(picks, rq_low[slot])
         racc[...] += dot(fold[:, : BLK // 4 * states], qd_low[slot])
@@ -542,7 +542,6 @@
             s_low = s.astype(BF16)
             states_low[slot, (i + 1) * states : (i + 2) * states, :] = s_low
             dots[slot, i * states : (i + 1) * states, :128] = lane_sum(s_low * spread(yr, i).astype(BF16))
-        y_out[pl.ds(t0, BLK), :] = dot(cdiag[pl.ds(t0, BLK), :], states_low[slot, states:, :])
         cr = carry[...]
         qds = []
         for i in reversed(range(BLK)):
@@ -561,15 +560,12 @@
 
     def block_step(k, _):
         j = blocks - 1 - 2 * k
-        products(1, jnp.where(k == 0, blocks, j + 1))
-        one_block(0, j)
-        products(0, j)
-        one_block(1, j - 1)
+        for slot in range(2):
+            one_block(slot, j - slot)
+            products(slot, j - slot)
         return 0
 
     lax.fori_loop(0, blocks // 2, block_step, 0)
-    products(1, 0)
-
     rate_grad[...] += -racc[...]
     for cols in columns(inner):
         act_f = act[:, cols].astype(F32)

time: 196 us -> 190 us (0.969)
  Pallas kernels: 193 us -> 186 us
    pallas_call x1, Pallas kernels: 78.8 us -> 72.1 us  [per_device(): pl.pallas_call(functools.partial(second_kernel, runs), grid=(2, slots), i...]
where the time goes in v8:
time: 190 us; the launch traced here: 189 us
  Pallas kernels  186 us (98%)
    pallas_call x1, Pallas kernels, per_device(): pl.pallas_call(functools.partial(second_kernel, runs), grid=(2, slots), i...  72.1 us
    pallas_call x1, Pallas kernels, per_device(): pl.pallas_call(functools.partial(tail_kernel, (runs, groups, slots)), gri...  52 us
    pallas_call x1, Pallas kernels, per_device(): pl.pallas_call(functools.partial(first_kernel, runs, slots), grid=(2, slo...  45.4 us
    pallas_call x1, Pallas kernels, per_device(): pl.pallas_call(functools.partial(enter_kernel, runs), grid=(slots,), in_s...  10.7 us
    pallas_call x1, Pallas kernels, per_device(): pl.pallas_call(finish_kernel, grid=(4,), in_specs=[spec((inner // 4, dim)...  5.86 us

profile of v8, /device:TPU:0, one launch (start us, length us, event | category | flops | bytes accessed | tf_op | source)
XLA Modules:
  0.0 189.2 jit_solution(13381215685329639616)
XLA Ops:
  1.3 10.7 %enter.1 = (bf16[3,2,272,768]{3,2,1,0:T(8,128)(2,1)}, f32[3,2,256,768]{3,2,1,0:T(8,128)}, f32[3,256,768]{2,1,0:T(8,128)}, bf16[3,256,384]{2,1,0:T(8,128)(2,1)}, f32[3,1,1152]{2,1,0:T(1,128)}) custom-call(bf16[3,256,384]{2,1,0:T(8,128)(2,1)} %tok.3, bf16[3,256,384]{2,1,0:T(8,128)(2,1)} %cot.3, s32[3,256]{1,0:T(4,128)} %mask.3, s32[1,1]{1,0:T(1,128)} %bitcast.3.counts, ...), custom_call_target="tpu_custom_call" | custom-call | tf_op jit(solution)/shard_map/enter/pallas_call | solution.py:1033
  12.0 45.4 %first.1 = (bf16[3,2,256,768]{3,2,1,0:T(8,128)(2,1)}, f32[3,2,3,256,768]{4,3,2,1,0:T(8,128)}, f32[3,2,64,256]{3,2,1,0:T(8,128)}, f32[3,2,40,768]{3,2,1,0:T(8,128...) custom-call(bf16[3,2,272,768]{3,2,1,0:T(8,128)(2,1)} %get-tuple-elem, ...), custom_call_target="tpu_custom_call" | custom-call | tf_op jit(solution)/shard_map/first/pallas_call | solution.py:1070
  57.4 72.1 %second.1 = (f32[3,2,256,768]{3,2,1,0:T(8,128)}, f32[3,2,256,768]{3,2,1,0:T(8,128)}, f32[2,3,8,768]{3,2,1,0:T(8,128)}, f32[2,104,768]{2,1,0:T(8,128)}) custom-call(f32[2,3,16,768]{3,2,1,0:T(8,128)} %get-tuple-element.54.first_in, f32[3,2,40,768]{3,2,1,0:T(8,128)} %get-tuple-element.55.lasts, f32[2,16,768]{2,1,0:T(8,128)} %rate.3, ...), custom_call_target="tpu_custom_call" | custom-call | tf_op jit(solution)/shard_map/second/pallas_call | solution.py:1104
  129.5 52.0 %tail.1 = (bf16[3,256,384]{2,1,0:T(8,128)(2,1)}, f32[3,256,384]{2,1,0:T(8,128)}, bf16[2048,384]{1,0:T(8,128)(2,1)}, bf16[1024,384]{1,0:T(8,128)(2,1)}, bf16[128,...) custom-call(bf16[3,256,384]{2,1,0:T(8,128)(2,1)} %tok.3, bf16[3,256,384]{2,1,0:T(8,128)(2,1)} %cot.3, ...), custom_call_target="tpu_custom_call" | custom-call | tf_op jit(solution)/shard_map/tail/pallas_call | solution.py:1149
  181.5 0.0 copy-start.1
  181.5 0.0 copy-start
  181.5 5.9 %finish.1 = (f32[3,384]{1,0:T(4,128)}, f32[384,1152]{1,0:T(8,128)}, f32[1152]{0:T(1024)}, f32[384,1536]{1,0:T(8,128)}, f32[2,4,768]{2,1,0:T(4,128)}, /*index=5*/...) custom-call(bf16[2048,384]{1,0:T(8,128)(2,1)} %get-tuple-element.68., ...), custom_call_target="tpu_custom_call" | custom-call | tf_op jit(solution)/shard_map/finish/pallas_call | solution.py:1182
  187.3 0.0 copy-done.1
  187.4 0.8 copy.33
  188.2 0.0 copy-done
  188.2 1.0 copy.34
Async XLA Ops:
  181.5 5.9 %copy-start.1 = (bf16[3,256,384]{2,1,0:T(8,128)(2,1)S(1)}, bf16[3,256,384]{2,1,0:T(8,128)(2,1)}, u32[]{:S(2)}) copy-start(bf16[3,256,384]{2,1,0:T(8,128)(2,1)} %get-tuple-element.98) | copy-start | bytes 1769476
  181.5 6.7 %copy-start = (f32[3,256,384]{2,1,0:T(8,128)S(1)}, f32[3,256,384]{2,1,0:T(8,128)}, u32[]{:S(2)}) copy-start(f32[3,256,384]{2,1,0:T(8,128)} %get-tuple-element.99) | copy-start | bytes 3538948

commit v9 on v8

--- a/solution.py
+++ b/solution.py
@@ -117,7 +117,7 @@
 
 def enter_kernel(
     runs, tok, cot, mask, counts, step, ada, ada_bias, win, wout,
-    xe, dy, z_out, hid_out, mod_out,
+    xe, dy, z_out, hid_out, mod_out, rim_out,
     mods, prev_tok, next_tok, prev_mask, next_mask, send_sem, recv_sem,
 ):
     slots, toks, dim = tok.shape
@@ -148,7 +148,7 @@
             next_tok[...] = jnp.zeros(next_tok.shape, BF16)
             next_mask[...] = jnp.zeros(next_mask.shape, jnp.int32)
 
-    live = (counts[...] > i).astype(F32)
+    live = jnp.where(counts[0] > i, 1.0, 0.0)
 
     @pl.when(i == 0)
     def _():
@@ -160,11 +160,11 @@
     mod_out[...] = mod
     shift, scale, gate = mod[:, :dim], mod[:, dim : 2 * dim], mod[:, 2 * dim :]
 
-    def hidden_of(part):
+    def hidden_of(part, scale, shift):
         normed, _ = normalise(part.astype(F32))
         return (normed * (1.0 + scale) + shift).astype(BF16)
 
-    hid = hidden_of(tok[i])
+    hid = hidden_of(tok[i], scale, shift)
     hid_out[...] = hid
     xz = dot(hid, win[...]) * (as_column(mask[pl.ds(i, 1), :]) * live)
     x_low = xz[:, :inner].astype(BF16)
@@ -174,20 +174,26 @@
     d_summed = dot_nt(d_branch, wout[...]) * z * jax.nn.sigmoid(z)
     dy[0] = d_summed
     dy[1] = flip_full(d_summed)
-    xe[0, HALO:, :] = x_low
-    xe[1, HALO:, :] = flip_low(x_low)
-
-    @pl.when(i == 0)
+    xe[0] = x_low
+    xe[1] = flip_low(x_low)
+
+    @pl.when(i == slots - 1)
     def _():
         swap_along_line(me, runs, ups, downs, False)
-
-    rims = jnp.concatenate([prev_tok[i], next_tok[i]], axis=0)
-    prev_col = as_column(prev_mask[pl.ds(i, 1), :])[toks - HALO :]
-    next_col = as_column(next_mask[pl.ds(i, 1), :])[:HALO]
-    rim_x = dot(hidden_of(rims), win[:, :inner]) * (jnp.concatenate([prev_col, next_col], axis=0) * live)
-    rim_x = rim_x.astype(BF16)
-    xe[0, :HALO, :] = rim_x[:HALO]
-    xe[1, :HALO, :] = flip_low(rim_x[HALO:])
+        hidden, seen = [], []
+        for item in range(slots):
+            row = mods[item : item + 1, :]
+            rims = jnp.concatenate([prev_tok[item], next_tok[item]], axis=0)
+            hidden.append(hidden_of(rims, row[:, dim : 2 * dim], row[:, :dim]))
+            prev_col = as_column(prev_mask[item : item + 1, :])[toks - HALO :]
+            next_col = as_column(next_mask[item : item + 1, :])[:HALO]
+            live = jnp.where(counts[0] > item, 1.0, 0.0)
+            seen.append(jnp.concatenate([prev_col, next_col], axis=0) * live)
+        rim_x = dot(jnp.concatenate(hidden, axis=0), win[:, :inner]) * jnp.concatenate(seen, axis=0)
+        for item in range(slots):
+            part = rim_x[2 * HALO * item : 2 * HALO * (item + 1)]
+            rim_out[item, 0] = part[:HALO].astype(BF16)
+            rim_out[item, 1] = flip_full(part[HALO:]).astype(BF16)
 
 
 def columns(inner, width=128):
@@ -344,7 +350,7 @@
 
 
 def first_kernel(
-    runs, slots, xe, dy, taps, tap_bias, x_rows, dt_rows, dt_bias, rate,
+    runs, slots, ahead, xe, dy, taps, tap_bias, x_rows, dt_rows, dt_bias, rate,
     act_out, planes, proj_out, last_out, starts_out, tiles, weights, first_in,
     dx, decay, through, rate2, wide, picks, ends, backs, totals, first_rate, *exchange_scratch,
 ):
@@ -382,7 +388,7 @@
 
     tap_row, dt_row = tap_bias[pl.ds(branch, 1), :], dt_bias[pl.ds(branch, 1), :]
     for cols in columns(inner):
-        x_f = xe[:, cols].astype(F32)
+        x_f = jnp.concatenate([ahead[:, cols], xe[:, cols]], axis=0).astype(F32)
         conv = tap_row[:, cols] + taps[tap_count - 1 : tap_count, cols] * x_f[HALO:]
         for k in range(tap_count - 1):
             conv = conv + taps[k : k + 1, cols] * pltpu.roll(x_f, tap_count - 1 - k, 0)[HALO:]
@@ -442,10 +448,10 @@
 
 
 def second_kernel(
-    runs, first_in, lasts, last_rate, starts, tiles, rate, xe, act, planes, dy, proj, weights, taps, skip,
-    y_out, dx_out, late_out, grads,
+    runs, first_in, lasts, last_rate, starts, tiles, rate, ahead, xe, act, planes, dy, proj, weights, taps, skip,
+    y_out, dx_out, rims, grads,
     rate2, carry, dxs, bdiag, cdiag, decay, states_low, lam_low, rq_low, qd_low, dots, racc, gsum, hsum, db, dc,
-    rims, late, send_sem, recv_sem, d_pre_low, s_in, s_last, lam_last, *exchange_scratch,
+    d_pre_low, s_in, s_last, lam_last, *exchange_scratch,
 ):
     toks, inner = dy.shape
     states = rate.shape[0]
@@ -460,11 +466,6 @@
     rate_grad, row_grads = grads.at[at : at + states], grads.at[at + states : at + states + 8]
     tapb_at, skip_at, dtb_at = (slice(tap_count + row, tap_count + row + 1) for row in range(3))
     item = pl.program_id(1)
-    last_item = item == pl.num_programs(1) - 1
-    me = lax.axis_index("seq")
-    downs = [(rims.at[0], late.at[0], send_sem.at[0], recv_sem.at[0])]
-    ups = [(rims.at[1], late.at[1], send_sem.at[1], recv_sem.at[1])]
-
     branch = pl.program_id(0)
     slots = lasts.shape[0]
     ends, backs = lasts.at[:, :states], lasts.at[:, states : 2 * states]
@@ -473,7 +474,7 @@
 
     @pl.when((item == 0) & (branch == 0))
     def _():
-        greet_line(me, runs, exchange.targets())
+        greet(exchange.targets())
 
     beside(exchange.points(), branch * slots + item, 0, slots)
 
@@ -589,7 +590,7 @@
             d_act = delta[:, cols] * gsum[:toks, cols] + gain[:, cols] * dy[:, cols] + through[:, at]
             d_conv = d_act * dsilu[:, cols]
             row_grads[tapb_at, cols] += jnp.sum(d_conv, axis=0, keepdims=True)
-            x_f = xe[:, cols].astype(F32)
+            x_f = jnp.concatenate([ahead[:, cols], xe[:, cols]], axis=0).astype(F32)
             base = jnp.concatenate([jnp.zeros((HALO, 128), F32), d_conv], axis=0)
             d_window = taps[tap_count - 1 : tap_count, cols] * base
             row_grads[tap_count - 1 : tap_count, cols] += jnp.sum(d_conv * x_f[HALO:], axis=0, keepdims=True)
@@ -599,25 +600,6 @@
                 d_window = d_window + taps[k : k + 1, cols] * moved
             rims[branch, item, :, cols] = d_window[HALO - 8 : HALO]
             dx_out[:, cols] = d_window[HALO:]
-
-    @pl.when(last_item & (pl.program_id(0) == 0))
-    def _():
-        swap_along_line(me, runs, [], downs, True)
-
-    @pl.when(last_item & (pl.program_id(0) == 1))
-    def _():
-        swap_along_line(me, runs, ups, [], True)
-        swap_along_line(me, runs, ups, downs, False)
-
-        @pl.when(me == 0)
-        def _():
-            late[1] = jnp.zeros(late.shape[1:], F32)
-
-        @pl.when(me == runs - 1)
-        def _():
-            late[0] = jnp.zeros(late.shape[1:], F32)
-
-        late_out[...] = late[...]
 
 
 LAST_ROWS = 16
@@ -810,12 +792,15 @@
 
 
 def tail_kernel(
-    plan, tok, cot, mod, mask, counts, hid, z_in, y, dx, late, win, wout, step,
+    plan, tok, cot, mod, mask, counts, hid, z_in, y, dx, rims, win, wout, step,
     grads,
     mixed, d_tokens, result, x_result, factors, own_rows,
-    dz, out_grad, z_grad, x_grad, mod_sum, mod_in, table, small_send, small_recv, *reduce_scratch,
+    late, rim_send, rim_recv, dz, out_grad, z_grad, x_grad, mod_sum, mod_in, table, small_send, small_recv, *reduce_scratch,
 ):
     runs, groups, slots = plan
+    me = lax.axis_index("seq")
+    downs = [(rims.at[0], late.at[0], rim_send.at[0], rim_recv.at[0])]
+    ups = [(rims.at[1], late.at[1], rim_send.at[1], rim_recv.at[1])]
     dim = tok.shape[-1]
     toks, inner = z_in.shape
     now = pl.program_id(0)
@@ -832,14 +817,24 @@
 
     @pl.when(now == 0)
     def _():
-        greet([target for ring in rings + [seq_ring, dp_ring] for target in ring.targets()])
+        greet_line(me, runs, [target for ring in rings + [seq_ring, dp_ring] for target in ring.targets()])
+        swap_along_line(me, runs, ups, downs, True)
+
+        @pl.when(me == 0)
+        def _():
+            late[1] = jnp.zeros(late.shape[1:], F32)
+
+        @pl.when(me == runs - 1)
+        def _():
+            late[0] = jnp.zeros(late.shape[1:], F32)
+
         out_grad[...] = jnp.zeros(out_grad.shape, F32)
         z_grad[...] = jnp.zeros(z_grad.shape, F32)
         x_grad[...] = jnp.zeros(x_grad.shape, F32)
         mod_sum[...] = jnp.zeros(mod_sum.shape, F32)
 
     scale, gate = mod[:, dim : 2 * dim], mod[:, 2 * dim :]
-    valid = as_column(mask[pl.ds(i, 1), :]) * (counts[...] > i).astype(F32)
+    valid = as_column(mask[pl.ds(i, 1), :]) * jnp.where(counts[0] > i, 1.0, 0.0)
     mod_rows = pl.ds(pl.multiple_of(8 * i, 8), 8)
 
     @pl.when(now < slots)
@@ -864,6 +859,7 @@
     @pl.when(now == slots)
     def _():
         main_points[0]()
+        swap_along_line(me, runs, ups, downs, False)
 
     @pl.when(now >= slots)
     def _():
@@ -1021,7 +1017,6 @@
     blocks = toks // BLK
     runs = lax.axis_size("seq")
     groups = lax.axis_size("dp")
-    counts2 = counts[:, None]
     x_rows = jnp.swapaxes(x_weight, 1, 2)
 
     def item(*block):
@@ -1030,22 +1025,24 @@
     def whole(*block):
         return spec(block, lambda *_: (0,) * len(block))
 
-    xe, dy, z_gate, hid, modulate = pl.pallas_call(
+    xe, dy, z_gate, hid, modulate, ahead = pl.pallas_call(
         functools.partial(enter_kernel, runs),
         grid=(slots,),
         in_specs=[
-            whole(slots, toks, dim), item(toks, dim), whole(slots, toks), whole(1, 1), whole(slots, dim), whole(dim, 3 * dim),
+            whole(slots, toks, dim), item(toks, dim), whole(slots, toks), pl.BlockSpec(memory_space=pltpu.SMEM), whole(slots, dim), whole(dim, 3 * dim),
             whole(3 * dim), whole(dim, 2 * inner), whole(inner, dim),
         ],
         out_specs=[
-            item(2, HALO + toks, inner), item(2, toks, inner), item(toks, inner), item(toks, dim), item(1, 3 * dim),
+            item(2, toks, inner), item(2, toks, inner), item(toks, inner), item(toks, dim), item(1, 3 * dim),
+            whole(slots, 2, HALO, inner),
         ],
         out_shape=[
-            jax.ShapeDtypeStruct((slots, 2, HALO + toks, inner), BF16),
+            jax.ShapeDtypeStruct((slots, 2, toks, inner), BF16),
             jax.ShapeDtypeStruct((slots, 2, toks, inner), F32),
             jax.ShapeDtypeStruct((slots, toks, inner), F32),
             jax.ShapeDtypeStruct((slots, toks, dim), BF16),
             jax.ShapeDtypeStruct((slots, 1, 3 * dim), F32),
+            jax.ShapeDtypeStruct((slots, 2, HALO, inner), BF16),
         ],
         scratch_shapes=[
             pltpu.VMEM((slots, 3 * dim), F32),
@@ -1055,7 +1052,7 @@
         compiler_params=params(collective_id=1, has_side_effects=True),
         name="enter",
     )(
-        tokens, cotangent, token_mask, counts2, timestep, ada_weight, ada_bias, input_weight, output_weight,
+        tokens, cotangent, token_mask, counts, timestep, ada_weight, ada_bias, input_weight, output_weight,
     )
 
     def unit(*block):
@@ -1071,7 +1068,7 @@
         functools.partial(first_kernel, runs, slots),
         grid=(2, slots),
         in_specs=[
-            unit(HALO + toks, inner), unit(toks, inner), branch(tap_count, inner), whole(2, inner),
+            unit(HALO, inner), unit(toks, inner), unit(toks, inner), branch(tap_count, inner), whole(2, inner),
             branch(rank + 2 * states, inner), branch(rank, inner), whole(2, inner), branch(states, inner),
         ],
         out_specs=[
@@ -1094,19 +1091,19 @@
         ],
         compiler_params=params(collective_id=2, has_side_effects=True),
         name="first",
-    )(xe, dy, conv_weight, conv_bias, x_rows, dt_weight, dt_bias, decay_rate)
+    )(ahead, xe, dy, conv_weight, conv_bias, x_rows, dt_weight, dt_bias, decay_rate)
 
     vmem = pl.BlockSpec(memory_space=pltpu.VMEM)
     last = spec((slots, None, 2 * states + 8, inner), lambda b, i: (0, 1, 0, 0))
     last_branch = spec((None, states, inner), lambda b, i: (1, 0, 0))
 
     grad_rows = 2 * rank + 3 * states + 8
-    y, dx, late, grads = pl.pallas_call(
+    y, dx, rims, grads = pl.pallas_call(
         functools.partial(second_kernel, runs),
         grid=(2, slots),
         in_specs=[
             whole(2, slots, states, inner), last, last_branch, unit(blocks, states + 8, inner), unit(toks, 2 * states, 128),
-            branch(states, inner), unit(HALO + toks, inner), unit(toks, inner), unit(3, toks, inner), unit(toks, inner),
+            branch(states, inner), unit(HALO, inner), unit(toks, inner), unit(toks, inner), unit(3, toks, inner), unit(toks, inner),
             unit(proj_rows, toks), branch(proj_rows + wide_rank, inner), branch(tap_count, inner), whole(2, inner),
         ],
         out_specs=[unit(toks, inner), unit(toks, inner), whole(2, slots, 8, inner), branch(grad_rows, inner)],
@@ -1123,15 +1120,14 @@
             pltpu.VMEM((2, BLK * states, 256), BF16), pltpu.VMEM((states, inner), F32),
             pltpu.VMEM((toks + BLK, inner), F32), pltpu.VMEM((toks + BLK, inner), F32),
             pltpu.VMEM((toks + BLK, BLK * states), BF16), pltpu.VMEM((toks + BLK, BLK * states), BF16),
-            pltpu.VMEM((2, slots, 8, inner), F32), pltpu.VMEM((2, slots, 8, inner), F32),
-            pltpu.SemaphoreType.DMA((2,)), pltpu.SemaphoreType.DMA((2,)), pltpu.VMEM((toks, inner), BF16),
+            pltpu.VMEM((toks, inner), BF16),
             pltpu.VMEM((states, inner), F32), pltpu.VMEM((slots, states, inner), F32), pltpu.VMEM((slots, states, inner), F32),
             *exchange_shapes(runs, slots, states, inner),
         ],
         compiler_params=params(collective_id=3, has_side_effects=True),
         name="second",
     )(
-        first_in, lasts, decay_rate, starts, tiles, decay_rate, xe, act, planes, dy, proj, weights, conv_weight, skip_gain,
+        first_in, lasts, decay_rate, starts, tiles, decay_rate, ahead, xe, act, planes, dy, proj, weights, conv_weight, skip_gain,
     )
 
     def now(*block):
@@ -1150,7 +1146,7 @@
         functools.partial(tail_kernel, (runs, groups, slots)),
         grid=(2 * slots,),
         in_specs=[
-            now(toks, dim), now(toks, dim), now(1, 3 * dim), whole(slots, toks), whole(1, 1), now(toks, dim),
+            now(toks, dim), now(toks, dim), now(1, 3 * dim), whole(slots, toks), pl.BlockSpec(memory_space=pltpu.SMEM), now(toks, dim),
             early(toks, inner), early(2, toks, inner), after(2, toks, inner), whole(2, slots, 8, inner),
             whole(dim, 2 * inner), whole(inner, dim), whole(slots, dim), whole(2, grad_rows, inner),
         ],
@@ -1164,6 +1160,7 @@
             jax.ShapeDtypeStruct((16 * groups, dim), BF16), jax.ShapeDtypeStruct((16, dim), BF16),
         ],
         scratch_shapes=[
+            pltpu.VMEM((2, slots, 8, inner), F32), pltpu.SemaphoreType.DMA((2,)), pltpu.SemaphoreType.DMA((2,)),
             pltpu.VMEM((slots, toks, inner), BF16), pltpu.VMEM((inner, dim), F32), pltpu.VMEM((dim, inner), F32),
             pltpu.VMEM((dim, inner), F32), pltpu.VMEM((8 * slots, dim), F32), pltpu.VMEM((max(runs - 1, 1), 8 * slots, dim), F32),
             pltpu.VMEM((16 * groups, dim), BF16), pltpu.SemaphoreType.DMA((runs + groups,)),
@@ -1173,7 +1170,7 @@
         compiler_params=params(collective_id=4, has_side_effects=True),
         name="tail",
     )(
-        tokens, cotangent, modulate, token_mask, counts2, hid, z_gate, y, dx, late, input_weight, output_weight, timestep, grads,
+        tokens, cotangent, modulate, token_mask, counts, hid, z_gate, y, dx, rims, input_weight, output_weight, timestep, grads,
     )
 
     (

time: 190 us -> 186 us (0.979)
  Pallas kernels: 186 us -> 182 us
where the time goes in v9:
time: 186 us
  Pallas kernels  182 us (98%)
    pallas_call x1, Pallas kernels, per_device(): pl.pallas_call(functools.partial(second_kernel, runs), grid=(2, slots), i...  71.5 us
    pallas_call x1, Pallas kernels, per_device(): pl.pallas_call(functools.partial(tail_kernel, (runs, groups, slots)), gri...  50.8 us
    pallas_call x1, Pallas kernels, per_device(): pl.pallas_call(functools.partial(first_kernel, runs, slots), grid=(2, slo...  45.3 us
    pallas_call x1, Pallas kernels, per_device(): pl.pallas_call(functools.partial(enter_kernel, runs), grid=(slots,), in_s...  8.99 us
    pallas_call x1, Pallas kernels, per_device(): pl.pallas_call(finish_kernel, grid=(4,), in_specs=[spec((inner // 4, dim)...  5.86 us

profile of v9, /device:TPU:0, one launch (start us, length us, event | category | flops | bytes accessed | tf_op | source)
XLA Modules:
  0.0 185.7 jit_solution(1925982040864720376)
XLA Ops:
  1.3 9.0 %enter.1 = (bf16[3,2,256,768]{3,2,1,0:T(8,128)(2,1)}, f32[3,2,256,768]{3,2,1,0:T(8,128)}, f32[3,256,768]{2,1,0:T(8,128)}, bf16[3,256,384]{2,1,0:T(8,128)(2,1)}, ...) custom-call(bf16[3,256,384]{2,1,0:T(8,128)(2,1)} %tok.3, bf16[3,256,384]{2,1,0:T(8,128)(2,1)} %cot.3, ...), custom_call_target="tpu_custom_call" | custom-call | tf_op jit(solution)/shard_map/enter/pallas_call | solution.py:1028
  10.3 45.3 %first.1 = (bf16[3,2,256,768]{3,2,1,0:T(8,128)(2,1)}, f32[3,2,3,256,768]{4,3,2,1,0:T(8,128)}, f32[3,2,64,256]{3,2,1,0:T(8,128)}, f32[3,2,40,768]{3,2,1,0:T(8,128...) custom-call(bf16[3,2,16,768]{3,2,1,0:T(8,128)(2,1)} %get-tuple-eleme, ...), custom_call_target="tpu_custom_call" | custom-call | tf_op jit(solution)/shard_map/first/pallas_call | solution.py:1067
  55.6 71.5 %second.1 = (f32[3,2,256,768]{3,2,1,0:T(8,128)}, f32[3,2,256,768]{3,2,1,0:T(8,128)}, f32[2,3,8,768]{3,2,1,0:T(8,128)}, f32[2,104,768]{2,1,0:T(8,128)}) custom-call(f32[2,3,16,768]{3,2,1,0:T(8,128)} %get-tuple-element.56.first_in, f32[3,2,40,768]{3,2,1,0:T(8,128)} %get-tuple-element.57.lasts, f32[2,16,768]{2,1,0:T(8,128)} %rate.3, ...), custom_call_target="tpu_custom_call" | custom-call | tf_op jit(solution)/shard_map/second/pallas_call | solution.py:1101
  127.2 50.8 %tail.1 = (bf16[3,256,384]{2,1,0:T(8,128)(2,1)}, f32[3,256,384]{2,1,0:T(8,128)}, bf16[2048,384]{1,0:T(8,128)(2,1)}, bf16[1024,384]{1,0:T(8,128)(2,1)}, bf16[128,...) custom-call(bf16[3,256,384]{2,1,0:T(8,128)(2,1)} %tok.3, bf16[3,256,384]{2,1,0:T(8,128)(2,1)} %cot.3, ...), custom_call_target="tpu_custom_call" | custom-call | tf_op jit(solution)/shard_map/tail/pallas_call | solution.py:1145
  178.0 0.0 copy-start.1
  178.0 0.0 copy-start
  178.0 5.9 %finish.1 = (f32[3,384]{1,0:T(4,128)}, f32[384,1152]{1,0:T(8,128)}, f32[1152]{0:T(1024)}, f32[384,1536]{1,0:T(8,128)}, f32[2,4,768]{2,1,0:T(4,128)}, /*index=5*/...) custom-call(bf16[2048,384]{1,0:T(8,128)(2,1)} %get-tuple-element.70., ...), custom_call_target="tpu_custom_call" | custom-call | tf_op jit(solution)/shard_map/finish/pallas_call | solution.py:1179
  183.8 0.0 copy-done.1
  183.9 0.8 copy.33
  184.7 0.0 copy-done
  184.7 1.0 copy.34
Async XLA Ops:
  178.0 5.9 %copy-start.1 = (bf16[3,256,384]{2,1,0:T(8,128)(2,1)S(1)}, bf16[3,256,384]{2,1,0:T(8,128)(2,1)}, u32[]{:S(2)}) copy-start(bf16[3,256,384]{2,1,0:T(8,128)(2,1)} %get-tuple-element.100) | copy-start | bytes 1769476
  178.0 6.7 %copy-start = (f32[3,256,384]{2,1,0:T(8,128)S(1)}, f32[3,256,384]{2,1,0:T(8,128)}, u32[]{:S(2)}) copy-start(f32[3,256,384]{2,1,0:T(8,128)} %get-tuple-element.101) | copy-start | bytes 3538948

commit v10 on v9

--- a/solution.py
+++ b/solution.py
@@ -352,7 +352,7 @@
 def first_kernel(
     runs, slots, ahead, xe, dy, taps, tap_bias, x_rows, dt_rows, dt_bias, rate,
     act_out, planes, proj_out, last_out, starts_out, tiles, weights, first_in,
-    dx, decay, through, rate2, wide, picks, ends, backs, totals, first_rate, *exchange_scratch,
+    x_cols, dx, decay, through, rate2, wide, picks, ends, backs, totals, first_rate, *exchange_scratch,
 ):
     toks, inner = dy.shape
     states = rate.shape[0]
@@ -388,10 +388,15 @@
 
     tap_row, dt_row = tap_bias[pl.ds(branch, 1), :], dt_bias[pl.ds(branch, 1), :]
     for cols in columns(inner):
-        x_f = jnp.concatenate([ahead[:, cols], xe[:, cols]], axis=0).astype(F32)
-        conv = tap_row[:, cols] + taps[tap_count - 1 : tap_count, cols] * x_f[HALO:]
-        for k in range(tap_count - 1):
-            conv = conv + taps[k : k + 1, cols] * pltpu.roll(x_f, tap_count - 1 - k, 0)[HALO:]
+        at_col = cols.start // 128
+        x_cols[at_col] = jnp.concatenate([ahead[:, cols], xe[:, cols]], axis=0).astype(F32)
+        parts = []
+        for row in range(0, toks, 8):
+            part = tap_row[:, cols]
+            for k in range(tap_count):
+                part = part + taps[k : k + 1, cols] * x_cols[at_col, pl.ds(HALO - tap_count + 1 + k + row, 8), :]
+            parts.append(part)
+        conv = jnp.concatenate(parts, axis=0)
         open_part = jax.nn.sigmoid(conv)
         act_f = conv * open_part
         act_out[:, cols] = act_f.astype(BF16)
@@ -451,7 +456,7 @@
     runs, first_in, lasts, last_rate, starts, tiles, rate, ahead, xe, act, planes, dy, proj, weights, taps, skip,
     y_out, dx_out, rims, grads,
     rate2, carry, dxs, bdiag, cdiag, decay, states_low, lam_low, rq_low, qd_low, dots, racc, gsum, hsum, db, dc,
-    d_pre_low, s_in, s_last, lam_last, *exchange_scratch,
+    d_cols, d_pre_low, s_in, s_last, lam_last, *exchange_scratch,
 ):
     toks, inner = dy.shape
     states = rate.shape[0]
@@ -582,7 +587,8 @@
     xp_new = dot(d_proj, act[...])
     xp_grad[:held, :] += xp_new[:held]
     xp_grad[held:, :] += xp_new[rank:]
-    window = HALO + toks
+    d_cols[:, :HALO, :] = jnp.zeros((inner // 128, HALO, 128), F32)
+    d_cols[:, HALO + toks :, :] = jnp.zeros((inner // 128, HALO, 128), F32)
     for wide_cols in columns(inner, 256):
         through = dot_tn(d_proj, xwt[:, wide_cols])
         for at in columns(256):
@@ -591,15 +597,21 @@
             d_conv = d_act * dsilu[:, cols]
             row_grads[tapb_at, cols] += jnp.sum(d_conv, axis=0, keepdims=True)
             x_f = jnp.concatenate([ahead[:, cols], xe[:, cols]], axis=0).astype(F32)
-            base = jnp.concatenate([jnp.zeros((HALO, 128), F32), d_conv], axis=0)
-            d_window = taps[tap_count - 1 : tap_count, cols] * base
-            row_grads[tap_count - 1 : tap_count, cols] += jnp.sum(d_conv * x_f[HALO:], axis=0, keepdims=True)
-            for k in range(tap_count - 1):
-                moved = pltpu.roll(base, window - (tap_count - 1 - k), 0)
-                row_grads[k : k + 1, cols] += jnp.sum(moved * x_f, axis=0, keepdims=True)
-                d_window = d_window + taps[k : k + 1, cols] * moved
-            rims[branch, item, :, cols] = d_window[HALO - 8 : HALO]
-            dx_out[:, cols] = d_window[HALO:]
+            at_col = cols.start // 128
+            d_cols[at_col, HALO : HALO + toks, :] = d_conv
+            sums = [jnp.zeros((8, 128), F32) for _ in range(tap_count)]
+            for row in range(HALO - 8, HALO + toks, 8):
+                part = jnp.zeros((8, 128), F32)
+                for k in range(tap_count):
+                    moved = d_cols[at_col, pl.ds(row + tap_count - 1 - k, 8), :]
+                    part = part + taps[k : k + 1, cols] * moved
+                    sums[k] = sums[k] + moved * x_f[row : row + 8]
+                if row < HALO:
+                    rims[branch, item, :, cols] = part
+                else:
+                    dx_out[row - HALO : row - HALO + 8, cols] = part
+            for k in range(tap_count):
+                row_grads[k : k + 1, cols] += jnp.sum(sums[k], axis=0, keepdims=True)
 
 
 LAST_ROWS = 16
@@ -795,7 +807,7 @@
     plan, tok, cot, mod, mask, counts, hid, z_in, y, dx, rims, win, wout, step,
     grads,
     mixed, d_tokens, result, x_result, factors, own_rows,
-    late, rim_send, rim_recv, dz, out_grad, z_grad, x_grad, mod_sum, mod_in, table, small_send, small_recv, *reduce_scratch,
+    late, rim_send, rim_recv, dz, d_xs, hids, out_grad, z_grad, x_grad, mod_sum, mod_in, table, small_send, small_recv, *reduce_scratch,
 ):
     runs, groups, slots = plan
     me = lax.axis_index("seq")
@@ -853,6 +865,7 @@
         d_low = (d_zgate * valid).astype(BF16)
         dz[i] = d_low
         z_grad[...] += dot_tn(hid[...], d_low)
+        hids[i] = hid[...]
         d_gate = jnp.sum(cot_f * branch_out, axis=0, keepdims=True)
         mod_sum[mod_rows, :] = jnp.concatenate([jnp.zeros((2, dim), F32), d_gate, jnp.zeros((5, dim), F32)], axis=0)
 
@@ -860,18 +873,23 @@
     def _():
         main_points[0]()
         swap_along_line(me, runs, ups, downs, False)
-
-    @pl.when(now >= slots)
-    def _():
         edge = late.shape[2]
 
         def with_late(part, extra):
             return jnp.concatenate([part[: toks - edge], part[toks - edge :] + extra], axis=0)
 
-        d_x = with_late(dx[0], late[0, i]) + flip_full(with_late(dx[1], late[1, i]))
-        d_x = (d_x * valid).astype(BF16)
-        x_grad[...] += dot_tn(hid[...], d_x)
-        d_hidden = dot_nt(d_x, win[:, :inner]) + dot_nt(dz[i], win[:, inner:])
+        for item in range(slots):
+            seen = as_column(mask[item : item + 1, :]) * jnp.where(counts[0] > item, 1.0, 0.0)
+            d_x = with_late(dx[item, 0], late[0, item]) + flip_full(with_late(dx[item, 1], late[1, item]))
+            d_low = (d_x * seen).astype(BF16)
+            d_xs[item] = d_low
+            x_grad[...] += dot_tn(hids[item], d_low)
+        rest_points[0]()
+        main_points[1]()
+
+    @pl.when(now >= slots)
+    def _():
+        d_hidden = dot_nt(d_xs[i], win[:, :inner]) + dot_nt(dz[i], win[:, inner:])
         normed, inv_std = normalise(tok[...].astype(F32))
         d_shift = jnp.sum(d_hidden, axis=0, keepdims=True)
         d_scale = jnp.sum(d_hidden * normed, axis=0, keepdims=True)
@@ -885,7 +903,7 @@
 
     @pl.when(now == slots)
     def _():
-        main_points[1]()
+        rest_points[1]()
 
     def sum_copies():
         return [
@@ -935,8 +953,6 @@
     @pl.when(now == 2 * slots - 1)
     def _():
         start_small()
-        rest_points[0]()
-        rest_points[1]()
         for at in range(2, len(main_points)):
             main_points[at]()
             if at == 2:
@@ -948,12 +964,14 @@
 
 
 def finish_kernel(
-    outs, zs, xs, smalls, factors, own, step, ada,
-    grad_time, grad_ada, grad_ada_bias, in_grad, tap_grad, tapb_grad, xp_grad, dtp_grad, dtb_grad, rate_grad, skip_grad, out_grad,
+    mixed_in, tokens_in, outs, zs, xs, smalls, factors, own, step, ada,
+    mixed, d_tokens, grad_time, grad_ada, grad_ada_bias, in_grad, tap_grad, tapb_grad, xp_grad, dtp_grad, dtb_grad, rate_grad, skip_grad, out_grad,
 ):
     dim, inner = in_grad.shape[0], rate_grad.shape[2]
     slots = step.shape[0]
     now = pl.program_id(0)
+    mixed[...] = mixed_in[...]
+    d_tokens[...] = tokens_in[...]
     out_grad[...] = outs[...].astype(F32)
     in_grad[...] = jnp.where(now < inner // dim, xs[...], zs[...]).astype(F32)
     table = factors[...]
@@ -1083,7 +1101,8 @@
             jax.ShapeDtypeStruct((2, slots, states, inner), F32),
         ],
         scratch_shapes=[
-            pltpu.VMEM((toks, inner), F32), pltpu.VMEM((2, BLK, states, inner), F32), pltpu.VMEM((8, inner), F32),
+            pltpu.VMEM((inner // 128, HALO + toks, 128), F32), pltpu.VMEM((toks, inner), F32),
+            pltpu.VMEM((2, BLK, states, inner), F32), pltpu.VMEM((8, inner), F32),
             pltpu.VMEM((states, inner), F32), pltpu.VMEM((2 * states * toks, 128), F32),
             pltpu.VMEM((4 * states, 2 * states * 128), BF16), pltpu.VMEM((slots, states, inner), F32),
             pltpu.VMEM((slots, states, inner), F32), pltpu.VMEM((slots, 1, inner), F32), pltpu.VMEM((states, inner), F32),
@@ -1120,7 +1139,7 @@
             pltpu.VMEM((2, BLK * states, 256), BF16), pltpu.VMEM((states, inner), F32),
             pltpu.VMEM((toks + BLK, inner), F32), pltpu.VMEM((toks + BLK, inner), F32),
             pltpu.VMEM((toks + BLK, BLK * states), BF16), pltpu.VMEM((toks + BLK, BLK * states), BF16),
-            pltpu.VMEM((toks, inner), BF16),
+            pltpu.VMEM((inner // 128, toks + 2 * HALO, 128), F32), pltpu.VMEM((toks, inner), BF16),
             pltpu.VMEM((states, inner), F32), pltpu.VMEM((slots, states, inner), F32), pltpu.VMEM((slots, states, inner), F32),
             *exchange_shapes(runs, slots, states, inner),
         ],
@@ -1147,7 +1166,7 @@
         grid=(2 * slots,),
         in_specs=[
             now(toks, dim), now(toks, dim), now(1, 3 * dim), whole(slots, toks), pl.BlockSpec(memory_space=pltpu.SMEM), now(toks, dim),
-            early(toks, inner), early(2, toks, inner), after(2, toks, inner), whole(2, slots, 8, inner),
+            early(toks, inner), early(2, toks, inner), whole(slots, 2, toks, inner), whole(2, slots, 8, inner),
             whole(dim, 2 * inner), whole(inner, dim), whole(slots, dim), whole(2, grad_rows, inner),
         ],
         out_specs=[
@@ -1161,7 +1180,8 @@
         ],
         scratch_shapes=[
             pltpu.VMEM((2, slots, 8, inner), F32), pltpu.SemaphoreType.DMA((2,)), pltpu.SemaphoreType.DMA((2,)),
-            pltpu.VMEM((slots, toks, inner), BF16), pltpu.VMEM((inner, dim), F32), pltpu.VMEM((dim, inner), F32),
+            pltpu.VMEM((slots, toks, inner), BF16), pltpu.VMEM((slots, toks, inner), BF16), pltpu.VMEM((slots, toks, dim), BF16),
+            pltpu.VMEM((inner, dim), F32), pltpu.VMEM((dim, inner), F32),
             pltpu.VMEM((dim, inner), F32), pltpu.VMEM((8 * slots, dim), F32), pltpu.VMEM((max(runs - 1, 1), 8 * slots, dim), F32),
             pltpu.VMEM((16 * groups, dim), BF16), pltpu.SemaphoreType.DMA((runs + groups,)),
             pltpu.SemaphoreType.DMA((runs + groups,)), *reduce_shapes(main_parts, dim, runs, groups),
@@ -1173,35 +1193,39 @@
         tokens, cotangent, modulate, token_mask, counts, hid, z_gate, y, dx, rims, input_weight, output_weight, timestep, grads,
     )
 
+    def part(*block):
+        return spec((None,) + block, lambda s: (jnp.minimum(s, slots - 1),) + (0,) * len(block))
+
     (
-        d_time, grad_ada, grad_ada_bias, in_grad, tap_grad, tapb_grad, xp_grad, dtp_grad, dtb_grad, rate_grad, skip_grad,
+        mixed, d_tokens, d_time, grad_ada, grad_ada_bias, in_grad, tap_grad, tapb_grad, xp_grad, dtp_grad, dtb_grad, rate_grad, skip_grad,
         out_grad,
     ) = pl.pallas_call(
         finish_kernel,
         grid=(4,),
         in_specs=[
-            spec((inner // 4, dim), lambda s: (s, 0)),
+            part(toks, dim), part(toks, dim), spec((inner // 4, dim), lambda s: (s, 0)),
             spec((dim, dim), lambda s: (inner // dim + jnp.maximum(s - inner // dim, 0), 0)),
             spec((dim, dim), lambda s: (jnp.minimum(s, inner // dim - 1), 0)),
             spec((PART_ROWS, dim), lambda s: (2 * inner // PART_ROWS, 0)),
             whole(16 * groups, dim), whole(16, dim), whole(slots, dim), spec((dim, dim), lambda s: (0, jnp.minimum(s, 2))),
         ],
         out_specs=[
-            whole(slots, dim), spec((dim, dim), lambda s: (0, jnp.minimum(s, 2))), whole(3 * dim),
+            part(toks, dim), part(toks, dim), whole(slots, dim), spec((dim, dim), lambda s: (0, jnp.minimum(s, 2))), whole(3 * dim),
             spec((dim, 2 * inner // 4), lambda s: (0, s)), whole(2, tap_count, inner), whole(2, inner),
             whole(2, rank + 2 * states, inner), whole(2, rank, inner), whole(2, inner), whole(2, states, inner), whole(2, inner),
             spec((inner // 4, dim), lambda s: (s, 0)),
         ],
-        out_shape=[
+        out_shape=[jax.ShapeDtypeStruct((slots, toks, dim), BF16)]
+        + [
             jax.ShapeDtypeStruct(shape, F32)
             for shape in (
-                (slots, dim), (dim, 3 * dim), (3 * dim,), (dim, 2 * inner), (2, tap_count, inner), (2, inner),
+                (slots, toks, dim), (slots, dim), (dim, 3 * dim), (3 * dim,), (dim, 2 * inner), (2, tap_count, inner), (2, inner),
                 (2, rank + 2 * states, inner), (2, rank, inner), (2, inner), (2, states, inner), (2, inner), (inner, dim),
             )
         ],
         compiler_params=params(),
         name="finish",
-    )(result, result, x_result, result, factors, own, timestep, ada_weight)
+    )(mixed, d_tokens, result, result, x_result, result, factors, own, timestep, ada_weight)
     return (
         mixed, d_tokens, d_time, grad_ada, grad_ada_bias, in_grad, tap_grad, tapb_grad, jnp.swapaxes(xp_grad, 1, 2), dtp_grad, dtb_grad,
         rate_grad, skip_grad, out_grad,

time: 186 us -> 184 us (0.989)
  no operation moved by 1% of the time
where the time goes in v10:
time: 184 us
  Pallas kernels  183 us (99%)
    pallas_call x1, Pallas kernels, per_device(): pl.pallas_call(functools.partial(second_kernel, runs), grid=(2, slots), i...  71.2 us
    pallas_call x1, Pallas kernels, per_device(): pl.pallas_call(functools.partial(tail_kernel, (runs, groups, slots)), gri...  50.9 us
    pallas_call x1, Pallas kernels, per_device(): pl.pallas_call(functools.partial(first_kernel, runs, slots), grid=(2, slo...  44.7 us
    pallas_call x1, Pallas kernels, per_device(): pl.pallas_call(functools.partial(enter_kernel, runs), grid=(slots,), in_s...  9.02 us
    pallas_call x1, Pallas kernels, per_device(): pl.pallas_call(finish_kernel, grid=(4,), in_specs=[part(toks, dim), part(...  6.71 us

profile of v10, /device:TPU:0, one launch (start us, length us, event | category | flops | bytes accessed | tf_op | source)
XLA Modules:
  0.0 184.1 jit_solution(5535387968933242038)
XLA Ops:
  1.3 9.0 %enter.1 = (bf16[3,2,256,768]{3,2,1,0:T(8,128)(2,1)}, f32[3,2,256,768]{3,2,1,0:T(8,128)}, f32[3,256,768]{2,1,0:T(8,128)}, bf16[3,256,384]{2,1,0:T(8,128)(2,1)}, ...) custom-call(bf16[3,256,384]{2,1,0:T(8,128)(2,1)} %tok.3, bf16[3,256,384]{2,1,0:T(8,128)(2,1)} %cot.3, ...), custom_call_target="tpu_custom_call" | custom-call | tf_op jit(solution)/shard_map/enter/pallas_call | solution.py:1046
  10.3 44.7 %first.1 = (bf16[3,2,256,768]{3,2,1,0:T(8,128)(2,1)}, f32[3,2,3,256,768]{4,3,2,1,0:T(8,128)}, f32[3,2,64,256]{3,2,1,0:T(8,128)}, f32[3,2,40,768]{3,2,1,0:T(8,128...) custom-call(bf16[3,2,16,768]{3,2,1,0:T(8,128)(2,1)} %get-tuple-eleme, ...), custom_call_target="tpu_custom_call" | custom-call | tf_op jit(solution)/shard_map/first/pallas_call | solution.py:1085
  55.0 71.2 %second.1 = (f32[3,2,256,768]{3,2,1,0:T(8,128)}, f32[3,2,256,768]{3,2,1,0:T(8,128)}, f32[2,3,8,768]{3,2,1,0:T(8,128)}, f32[2,104,768]{2,1,0:T(8,128)}) custom-call(f32[2,3,16,768]{3,2,1,0:T(8,128)} %get-tuple-element.58.first_in, f32[3,2,40,768]{3,2,1,0:T(8,128)} %get-tuple-element.59.lasts, f32[2,16,768]{2,1,0:T(8,128)} %rate.3, ...), custom_call_target="tpu_custom_call" | custom-call | tf_op jit(solution)/shard_map/second/pallas_call | solution.py:1120
  126.3 50.9 %tail.1 = (bf16[3,256,384]{2,1,0:T(8,128)(2,1)}, f32[3,256,384]{2,1,0:T(8,128)}, bf16[2048,384]{1,0:T(8,128)(2,1)}, bf16[1024,384]{1,0:T(8,128)(2,1)}, bf16[128,...) custom-call(bf16[3,256,384]{2,1,0:T(8,128)(2,1)} %tok.3, bf16[3,256,384]{2,1,0:T(8,128)(2,1)} %cot.3, ...), custom_call_target="tpu_custom_call" | custom-call | tf_op jit(solution)/shard_map/tail/pallas_call | solution.py:1164
  177.2 6.7 %finish.1 = (bf16[3,256,384]{2,1,0:T(8,128)(2,1)}, f32[3,256,384]{2,1,0:T(8,128)}, f32[3,384]{1,0:T(4,128)}, f32[384,1152]{1,0:T(8,128)}, f32[1152]{0:T(1024)}, ...) custom-call(bf16[3,256,384]{2,1,0:T(8,128)(2,1)} %get-tuple-element., ...), custom_call_target="tpu_custom_call" | custom-call | tf_op jit(solution)/shard_map/finish/pallas_call | solution.py:1202

commit v11 on v10

--- a/solution.py
+++ b/solution.py
@@ -511,26 +511,26 @@
     cdiag[...] = jnp.where(own, dot_tn(proj[rank + states :, :].astype(BF16), fold), 0.0).astype(BF16)
     mine = own[:BLK]
     picks = mine.astype(BF16)
-    sides = (
-        lax.broadcasted_iota(jnp.int32, (2 * BLK, 256), 0) // BLK == lax.broadcasted_iota(jnp.int32, (2 * BLK, 256), 1) // 128
-    ).astype(BF16)
+    ones = jnp.ones((BLK, 128), BF16)
     racc[...] = jnp.zeros((states, inner), F32)
 
     def lane_sum(wide):
         part = [wide[:, at : at + 128] for at in range(0, inner, 128)]
         while len(part) > 1:
-            part = [sum(part[at : at + 2]) for at in range(0, len(part), 2)]
+            pairs = [part[at] + part[at + 1] for at in range(0, len(part) - 1, 2)]
+            part = pairs + part[2 * len(pairs) :]
         return part[0]
 
     def products(slot, j):
         t0 = pl.multiple_of(j * BLK, BLK)
         y_out[pl.ds(t0, BLK), :] = dot(cdiag[pl.ds(t0, BLK), :], states_low[slot, states:, :])
-        gsum[pl.ds(t0, BLK), :] = dot(bdiag[pl.ds(t0, BLK), :], lam_low[slot])
-        hsum[pl.ds(t0, BLK), :] = dot(picks, rq_low[slot])
+        half = width // 2
+        rows = bdiag[pl.ds(t0, BLK), :]
+        gsum[pl.ds(t0, BLK), :] = dot(rows[:, half:], lam_low[slot, half:]) + dot(rows[:, :half], lam_low[slot, :half])
+        hsum[pl.ds(t0, BLK), :] = dot(picks[:, half:], rq_low[slot, half:]) + dot(picks[:, :half], rq_low[slot, :half])
         racc[...] += dot(fold[:, : BLK // 4 * states], qd_low[slot])
-        both = dot_nt(sides, dots[slot])
-        dc[pl.ds(t0, BLK), :] = jnp.where(mine, both[:BLK], 0.0).astype(BF16)
-        db[pl.ds(t0, BLK), :] = jnp.where(mine, both[BLK:], 0.0).astype(BF16)
+        dc[pl.ds(t0, BLK), :] = jnp.where(mine, dot_nt(ones, dots[slot, :, :128]), 0.0).astype(BF16)
+        db[pl.ds(t0, BLK), :] = jnp.where(mine, dot_nt(ones, dots[slot, :, 128:]), 0.0).astype(BF16)
 
     def one_block(slot, j):
         t0 = pl.multiple_of(j * BLK, BLK)
@@ -730,7 +730,8 @@
             self.arrivals[at + (ahead - 1) * moved : at + ahead * moved, :].astype(F32) for ahead in range(1, ring.size)
         ]
         if split:
-            held = held + sum(came)
+            for part in came:
+                held = held + part
         else:
             values = [held.astype(BF16).astype(F32)] + came
             total = jnp.zeros_like(held)

time: 184 us -> 183 us (level)
  Pallas kernels: 183 us -> 181 us
where the time goes in v11:
time: 183 us; the launch traced here: 182 us
  Pallas kernels  181 us (99%)
    pallas_call x1, Pallas kernels, per_device(): pl.pallas_call(functools.partial(second_kernel, runs), grid=(2, slots), i...  69.5 us
    pallas_call x1, Pallas kernels, per_device(): pl.pallas_call(functools.partial(tail_kernel, (runs, groups, slots)), gri...  50.9 us
    pallas_call x1, Pallas kernels, per_device(): pl.pallas_call(functools.partial(first_kernel, runs, slots), grid=(2, slo...  44.7 us
    pallas_call x1, Pallas kernels, per_device(): pl.pallas_call(functools.partial(enter_kernel, runs), grid=(slots,), in_s...  9.02 us
    pallas_call x1, Pallas kernels, per_device(): pl.pallas_call(finish_kernel, grid=(4,), in_specs=[part(toks, dim), part(...  6.71 us

profile of v11, /device:TPU:0, one launch (start us, length us, event | category | flops | bytes accessed | tf_op | source)
XLA Modules:
  0.0 182.3 jit_solution(2630571382033328782)
XLA Ops:
  1.3 9.0 %enter.1 = (bf16[3,2,256,768]{3,2,1,0:T(8,128)(2,1)}, f32[3,2,256,768]{3,2,1,0:T(8,128)}, f32[3,256,768]{2,1,0:T(8,128)}, bf16[3,256,384]{2,1,0:T(8,128)(2,1)}, ...) custom-call(bf16[3,256,384]{2,1,0:T(8,128)(2,1)} %tok.3, bf16[3,256,384]{2,1,0:T(8,128)(2,1)} %cot.3, ...), custom_call_target="tpu_custom_call" | custom-call | tf_op jit(solution)/shard_map/enter/pallas_call | solution.py:1047
  10.3 44.7 %first.1 = (bf16[3,2,256,768]{3,2,1,0:T(8,128)(2,1)}, f32[3,2,3,256,768]{4,3,2,1,0:T(8,128)}, f32[3,2,64,256]{3,2,1,0:T(8,128)}, f32[3,2,40,768]{3,2,1,0:T(8,128...) custom-call(bf16[3,2,16,768]{3,2,1,0:T(8,128)(2,1)} %get-tuple-eleme, ...), custom_call_target="tpu_custom_call" | custom-call | tf_op jit(solution)/shard_map/first/pallas_call | solution.py:1086
  55.0 69.5 %second.1 = (f32[3,2,256,768]{3,2,1,0:T(8,128)}, f32[3,2,256,768]{3,2,1,0:T(8,128)}, f32[2,3,8,768]{3,2,1,0:T(8,128)}, f32[2,104,768]{2,1,0:T(8,128)}) custom-call(f32[2,3,16,768]{3,2,1,0:T(8,128)} %get-tuple-element.58.first_in, f32[3,2,40,768]{3,2,1,0:T(8,128)} %get-tuple-element.59.lasts, f32[2,16,768]{2,1,0:T(8,128)} %rate.3, ...), custom_call_target="tpu_custom_call" | custom-call | tf_op jit(solution)/shard_map/second/pallas_call | solution.py:1121
  124.5 50.9 %tail.1 = (bf16[3,256,384]{2,1,0:T(8,128)(2,1)}, f32[3,256,384]{2,1,0:T(8,128)}, bf16[2048,384]{1,0:T(8,128)(2,1)}, bf16[1024,384]{1,0:T(8,128)(2,1)}, bf16[128,...) custom-call(bf16[3,256,384]{2,1,0:T(8,128)(2,1)} %tok.3, bf16[3,256,384]{2,1,0:T(8,128)(2,1)} %cot.3, ...), custom_call_target="tpu_custom_call" | custom-call | tf_op jit(solution)/shard_map/tail/pallas_call | solution.py:1165
  175.4 6.7 %finish.1 = (bf16[3,256,384]{2,1,0:T(8,128)(2,1)}, f32[3,256,384]{2,1,0:T(8,128)}, f32[3,384]{1,0:T(4,128)}, f32[384,1152]{1,0:T(8,128)}, f32[1152]{0:T(1024)}, ...) custom-call(bf16[3,256,384]{2,1,0:T(8,128)(2,1)} %get-tuple-element., ...), custom_call_target="tpu_custom_call" | custom-call | tf_op jit(solution)/shard_map/finish/pallas_call | solution.py:1203

commit v12 on v11

--- a/solution.py
+++ b/solution.py
@@ -12,6 +12,7 @@
 BLK = 16
 WIDE_RANK = 32
 HALO = 16
+SPARE = 8
 LOG2E = math.log2(math.e)
 F32, BF16 = jnp.float32, jnp.bfloat16
 NT = (((1,), (1,)), ((), ()))
@@ -172,8 +173,9 @@
     z_out[...] = z
     d_branch = (cot[...].astype(F32) * gate).astype(BF16)
     d_summed = dot_nt(d_branch, wout[...]) * z * jax.nn.sigmoid(z)
-    dy[0] = d_summed
-    dy[1] = flip_full(d_summed)
+    dy[0, :toks] = d_summed
+    dy[1, :toks] = flip_full(d_summed)
+    dy[:, toks:] = jnp.zeros((2, SPARE, inner), F32)
     xe[0] = x_low
     xe[1] = flip_low(x_low)
 
@@ -354,7 +356,7 @@
     act_out, planes, proj_out, last_out, starts_out, tiles, weights, first_in,
     x_cols, dx, decay, through, rate2, wide, picks, ends, backs, totals, first_rate, *exchange_scratch,
 ):
-    toks, inner = dy.shape
+    toks, inner = xe.shape
     states = rate.shape[0]
     blocks = toks // BLK
     rank = WIDE_RANK
@@ -409,7 +411,7 @@
         delta, slope = softplus_parts(pre)
         delta_out[:, cols] = delta
         sig_out[:, cols] = slope
-        dx[:, cols] = delta * act_out[:, cols].astype(F32)
+        dx[:toks, cols] = delta * act_out[:, cols].astype(F32)
     lay_out(wide, proj[rank:, :], picks)
     end_out[...] = jnp.zeros((states, inner), F32)
     back_out[...] = jnp.zeros((states, inner), F32)
@@ -455,10 +457,10 @@
 def second_kernel(
     runs, first_in, lasts, last_rate, starts, tiles, rate, ahead, xe, act, planes, dy, proj, weights, taps, skip,
     y_out, dx_out, rims, grads,
-    rate2, carry, dxs, bdiag, cdiag, decay, states_low, lam_low, rq_low, qd_low, dots, racc, gsum, hsum, db, dc,
+    rate2, carry, dxs, bdiag, cdiag, decay, states_low, kept_low, lam_low, rq_low, qd_low, dots, racc, gsum, hsum, db, dc,
     d_cols, d_pre_low, s_in, s_last, lam_last, *exchange_scratch,
 ):
-    toks, inner = dy.shape
+    toks, inner = xe.shape
     states = rate.shape[0]
     blocks = toks // BLK
     rank = WIDE_RANK
@@ -503,10 +505,15 @@
 
     for cols in columns(inner):
         dxs[:toks, cols] = delta[:, cols] * act[:, cols].astype(F32)
-    fold = (
-        lax.broadcasted_iota(jnp.int32, (states, width), 1) % states == lax.broadcasted_iota(jnp.int32, (states, width), 0)
-    ).astype(BF16)
-    own = lax.broadcasted_iota(jnp.int32, (toks, width), 0) % BLK == lax.broadcasted_iota(jnp.int32, (toks, width), 1) // states
+    pair_rows = 2 * states
+
+    def inner_index(rows):
+        at = lax.broadcasted_iota(jnp.int32, (rows, width), 1)
+        token = lax.div(at, pair_rows) * 2 + lax.div(lax.rem(at, 16), 8)
+        return token, lax.div(lax.rem(at, pair_rows), 16) * 8 + lax.rem(at, 8)
+
+    fold = (inner_index(states)[1] == lax.broadcasted_iota(jnp.int32, (states, width), 0)).astype(BF16)
+    own = lax.rem(lax.broadcasted_iota(jnp.int32, (toks, width), 0), BLK) == inner_index(toks)[0]
     bdiag[:toks, :] = jnp.where(own, dot_tn(proj[rank : rank + states, :].astype(BF16), fold), 0.0).astype(BF16)
     cdiag[...] = jnp.where(own, dot_tn(proj[rank + states :, :].astype(BF16), fold), 0.0).astype(BF16)
     mine = own[:BLK]
@@ -523,7 +530,7 @@
 
     def products(slot, j):
         t0 = pl.multiple_of(j * BLK, BLK)
-        y_out[pl.ds(t0, BLK), :] = dot(cdiag[pl.ds(t0, BLK), :], states_low[slot, states:, :])
+        y_out[pl.ds(t0, BLK), :] = dot(cdiag[pl.ds(t0, BLK), :], states_low[slot])
         half = width // 2
         rows = bdiag[pl.ds(t0, BLK), :]
         gsum[pl.ds(t0, BLK), :] = dot(rows[:, half:], lam_low[slot, half:]) + dot(rows[:, :half], lam_low[slot, :half])
@@ -537,31 +544,54 @@
         dr, xr, yr = (ref.at[pl.ds(t0, BLK), :] for ref in (delta, dxs, dy))
         tile = tiles.at[pl.ds(t0, BLK)]
         r2 = rate2[...]
-        r_low = rate[...].astype(BF16)
+        groups = [slice(at, at + 8) for at in range(0, states, 8)]
         begin = starts[j]
         s = begin[:states] + s_in[...] * jnp.exp2(twice(begin[states:]) * r2)
-        states_low[slot, :states, :] = s.astype(BF16)
-        for i in range(BLK):
-            a = jnp.exp2(spread(dr, i) * r2)
-            decay[slot, i] = a
-            s = a * s + spread(xr, i) * across_lanes(tile[i, :states], inner)
-            s_low = s.astype(BF16)
-            states_low[slot, (i + 1) * states : (i + 2) * states, :] = s_low
-            dots[slot, i * states : (i + 1) * states, :128] = lane_sum(s_low * spread(yr, i).astype(BF16))
+
+        def both(first, second):
+            return jnp.concatenate([first, second], axis=0).astype(BF16)
+
+        def pair(ref, i):
+            return both(ref[pl.ds(i, 8, stride=0), :], ref[pl.ds(i + 1, 8, stride=0), :])
+
+        for i in range(0, BLK, 2):
+            kept, after = [], []
+            for t in (i, i + 1):
+                a = jnp.exp2(spread(dr, t) * r2)
+                decay[slot, t] = a
+                kept.append(a * s)
+                s = kept[-1] + spread(xr, t) * across_lanes(tile[t, :states], inner)
+                after.append(s)
+            y_pair = pair(yr, i)
+            for number, group in enumerate(groups):
+                rows = slice(i * states + 16 * number, i * states + 16 * (number + 1))
+                s_low = both(after[0][group], after[1][group])
+                states_low[slot, rows, :] = s_low
+                kept_low[slot, rows, :] = both(kept[0][group], kept[1][group])
+                dots[slot, rows, :128] = lane_sum(s_low * y_pair)
         cr = carry[...]
-        qds = []
-        for i in reversed(range(BLK)):
-            lam = cr + spread(yr, i) * across_lanes(tile[i, states:], inner)
-            l_low = lam.astype(BF16)
-            lam_low[slot, i * states : (i + 1) * states, :] = l_low
-            dots[slot, i * states : (i + 1) * states, 128:] = lane_sum(l_low * spread(xr, i).astype(BF16))
-            cr = decay[slot, i] * lam
-            q = cr.astype(BF16) * states_low[slot, i * states : (i + 1) * states, :]
-            rq_low[slot, i * states : (i + 1) * states, :] = q * r_low
-            qds.append(q * spread(dr, i).astype(BF16))
-            if i % 4 == 0:
-                qd_low[slot, i // 4 * states : (i // 4 + 1) * states, :] = (qds[0] + qds[1]) + (qds[2] + qds[3])
-                qds = []
+        r_low = [both(rate[group, :], rate[group, :]) for group in groups]
+        qds = [[] for _ in groups]
+        for i in reversed(range(0, BLK, 2)):
+            lams = []
+            for t in (i + 1, i):
+                lam = cr + spread(yr, t) * across_lanes(tile[t, states:], inner)
+                cr = decay[slot, t] * lam
+                lams.append(lam)
+            x_pair, d_pair = pair(xr, i), pair(dr, i)
+            for number, group in enumerate(groups):
+                rows = slice(i * states + 16 * number, i * states + 16 * (number + 1))
+                l_low = both(lams[1][group], lams[0][group])
+                lam_low[slot, rows, :] = l_low
+                dots[slot, rows, 128:] = lane_sum(l_low * x_pair)
+                q = l_low * kept_low[slot, rows, :]
+                rq_low[slot, rows, :] = q * r_low[number]
+                qds[number].append(q * d_pair)
+                if i % 8 == 0:
+                    at = i // 8 * pair_rows + 16 * number
+                    part = qds[number]
+                    qd_low[slot, at : at + 16, :] = (part[0] + part[1]) + (part[2] + part[3])
+                    qds[number] = []
         carry[...] = cr
 
     def block_step(k, _):
@@ -575,7 +605,7 @@
     rate_grad[...] += -racc[...]
     for cols in columns(inner):
         act_f = act[:, cols].astype(F32)
-        row_grads[skip_at, cols] += jnp.sum(dy[:, cols] * act_f, axis=0, keepdims=True)
+        row_grads[skip_at, cols] += jnp.sum(dy[:toks, cols] * act_f, axis=0, keepdims=True)
         y_out[:, cols] += gain[:, cols] * act_f
         d_pre = (act_f * gsum[:toks, cols] - hsum[:toks, cols]) * sig[:, cols]
         row_grads[dtb_at, cols] += jnp.sum(d_pre, axis=0, keepdims=True)
@@ -593,7 +623,7 @@
         through = dot_tn(d_proj, xwt[:, wide_cols])
         for at in columns(256):
             cols = slice(wide_cols.start + at.start, wide_cols.start + at.stop)
-            d_act = delta[:, cols] * gsum[:toks, cols] + gain[:, cols] * dy[:, cols] + through[:, at]
+            d_act = delta[:, cols] * gsum[:toks, cols] + gain[:, cols] * dy[:toks, cols] + through[:, at]
             d_conv = d_act * dsilu[:, cols]
             row_grads[tapb_at, cols] += jnp.sum(d_conv, axis=0, keepdims=True)
             x_f = jnp.concatenate([ahead[:, cols], xe[:, cols]], axis=0).astype(F32)
@@ -1052,12 +1082,12 @@
             whole(3 * dim), whole(dim, 2 * inner), whole(inner, dim),
         ],
         out_specs=[
-            item(2, toks, inner), item(2, toks, inner), item(toks, inner), item(toks, dim), item(1, 3 * dim),
+            item(2, toks, inner), item(2, toks + SPARE, inner), item(toks, inner), item(toks, dim), item(1, 3 * dim),
             whole(slots, 2, HALO, inner),
         ],
         out_shape=[
             jax.ShapeDtypeStruct((slots, 2, toks, inner), BF16),
-            jax.ShapeDtypeStruct((slots, 2, toks, inner), F32),
+            jax.ShapeDtypeStruct((slots, 2, toks + SPARE, inner), F32),
             jax.ShapeDtypeStruct((slots, toks, inner), F32),
             jax.ShapeDtypeStruct((slots, toks, dim), BF16),
             jax.ShapeDtypeStruct((slots, 1, 3 * dim), F32),
@@ -1087,7 +1117,7 @@
         functools.partial(first_kernel, runs, slots),
         grid=(2, slots),
         in_specs=[
-            unit(HALO, inner), unit(toks, inner), unit(toks, inner), branch(tap_count, inner), whole(2, inner),
+            unit(HALO, inner), unit(toks, inner), unit(toks + SPARE, inner), branch(tap_count, inner), whole(2, inner),
             branch(rank + 2 * states, inner), branch(rank, inner), whole(2, inner), branch(states, inner),
         ],
         out_specs=[
@@ -1102,7 +1132,7 @@
             jax.ShapeDtypeStruct((2, slots, states, inner), F32),
         ],
         scratch_shapes=[
-            pltpu.VMEM((inner // 128, HALO + toks, 128), F32), pltpu.VMEM((toks, inner), F32),
+            pltpu.VMEM((inner // 128, HALO + toks, 128), F32), pltpu.VMEM((toks + SPARE, inner), F32),
             pltpu.VMEM((2, BLK, states, inner), F32), pltpu.VMEM((8, inner), F32),
             pltpu.VMEM((states, inner), F32), pltpu.VMEM((2 * states * toks, 128), F32),
             pltpu.VMEM((4 * states, 2 * states * 128), BF16), pltpu.VMEM((slots, states, inner), F32),
@@ -1123,7 +1153,7 @@
         grid=(2, slots),
         in_specs=[
             whole(2, slots, states, inner), last, last_branch, unit(blocks, states + 8, inner), unit(toks, 2 * states, 128),
-            branch(states, inner), unit(HALO, inner), unit(toks, inner), unit(toks, inner), unit(3, toks, inner), unit(toks, inner),
+            branch(states, inner), unit(HALO, inner), unit(toks, inner), unit(toks, inner), unit(3, toks, inner), unit(toks + SPARE, inner),
             unit(proj_rows, toks), branch(proj_rows + wide_rank, inner), branch(tap_count, inner), whole(2, inner),
         ],
         out_specs=[unit(toks, inner), unit(toks, inner), whole(2, slots, 8, inner), branch(grad_rows, inner)],
@@ -1135,7 +1165,8 @@
             pltpu.VMEM((states, inner), F32), pltpu.VMEM((states, inner), F32), pltpu.VMEM((toks + BLK, inner), F32), pltpu.VMEM((toks + BLK, BLK * states), BF16),
             pltpu.VMEM((toks, BLK * states), BF16),
             pltpu.VMEM((2, BLK, states, inner), F32),
-            pltpu.VMEM((2, (BLK + 1) * states, inner), BF16), pltpu.VMEM((2, BLK * states, inner), BF16),
+            pltpu.VMEM((2, BLK * states, inner), BF16), pltpu.VMEM((2, BLK * states, inner), BF16),
+            pltpu.VMEM((2, BLK * states, inner), BF16),
             pltpu.VMEM((2, BLK * states, inner), BF16), pltpu.VMEM((2, BLK // 4 * states, inner), BF16),
             pltpu.VMEM((2, BLK * states, 256), BF16), pltpu.VMEM((states, inner), F32),
             pltpu.VMEM((toks + BLK, inner), F32), pltpu.VMEM((toks + BLK, inner), F32),

time: 183 us -> 182 us (level)
  no operation moved by 1% of the time
where the time goes in v12:
time: 182 us
  Pallas kernels  180 us (99%)
    pallas_call x1, Pallas kernels, per_device(): pl.pallas_call(functools.partial(second_kernel, runs), grid=(2, slots), i...  69.2 us
    pallas_call x1, Pallas kernels, per_device(): pl.pallas_call(functools.partial(tail_kernel, (runs, groups, slots)), gri...  50.8 us
    pallas_call x1, Pallas kernels, per_device(): pl.pallas_call(functools.partial(first_kernel, runs, slots), grid=(2, slo...  44.6 us
    pallas_call x1, Pallas kernels, per_device(): pl.pallas_call(functools.partial(enter_kernel, runs), grid=(slots,), in_s...  9.1 us
    pallas_call x1, Pallas kernels, per_device(): pl.pallas_call(finish_kernel, grid=(4,), in_specs=[part(toks, dim), part(...  6.7 us

profile of v12, /device:TPU:0, one launch (start us, length us, event | category | flops | bytes accessed | tf_op | source)
XLA Modules:
  0.0 181.8 jit_solution(13658204148482231751)
XLA Ops:
  1.3 9.1 %enter.1 = (bf16[3,2,256,768]{3,2,1,0:T(8,128)(2,1)}, f32[3,2,264,768]{3,2,1,0:T(8,128)}, f32[3,256,768]{2,1,0:T(8,128)}, bf16[3,256,384]{2,1,0:T(8,128)(2,1)}, ...) custom-call(bf16[3,256,384]{2,1,0:T(8,128)(2,1)} %tok.3, bf16[3,256,384]{2,1,0:T(8,128)(2,1)} %cot.3, ...), custom_call_target="tpu_custom_call" | custom-call | tf_op jit(solution)/shard_map/enter/pallas_call | solution.py:1077
  10.4 44.6 %first.1 = (bf16[3,2,256,768]{3,2,1,0:T(8,128)(2,1)}, f32[3,2,3,256,768]{4,3,2,1,0:T(8,128)}, f32[3,2,64,256]{3,2,1,0:T(8,128)}, f32[3,2,40,768]{3,2,1,0:T(8,128...) custom-call(bf16[3,2,16,768]{3,2,1,0:T(8,128)(2,1)} %get-tuple-eleme, ...), custom_call_target="tpu_custom_call" | custom-call | tf_op jit(solution)/shard_map/first/pallas_call | solution.py:1116
  55.0 69.2 %second.1 = (f32[3,2,256,768]{3,2,1,0:T(8,128)}, f32[3,2,256,768]{3,2,1,0:T(8,128)}, f32[2,3,8,768]{3,2,1,0:T(8,128)}, f32[2,104,768]{2,1,0:T(8,128)}) custom-call(f32[2,3,16,768]{3,2,1,0:T(8,128)} %get-tuple-element.58.first_in, f32[3,2,40,768]{3,2,1,0:T(8,128)} %get-tuple-element.59.lasts, f32[2,16,768]{2,1,0:T(8,128)} %rate.3, ...), custom_call_target="tpu_custom_call" | custom-call | tf_op jit(solution)/shard_map/second/pallas_call | solution.py:1151
  124.2 50.8 %tail.1 = (bf16[3,256,384]{2,1,0:T(8,128)(2,1)}, f32[3,256,384]{2,1,0:T(8,128)}, bf16[2048,384]{1,0:T(8,128)(2,1)}, bf16[1024,384]{1,0:T(8,128)(2,1)}, bf16[128,...) custom-call(bf16[3,256,384]{2,1,0:T(8,128)(2,1)} %tok.3, bf16[3,256,384]{2,1,0:T(8,128)(2,1)} %cot.3, ...), custom_call_target="tpu_custom_call" | custom-call | tf_op jit(solution)/shard_map/tail/pallas_call | solution.py:1196
  174.9 6.7 %finish.1 = (bf16[3,256,384]{2,1,0:T(8,128)(2,1)}, f32[3,256,384]{2,1,0:T(8,128)}, f32[3,384]{1,0:T(4,128)}, f32[384,1152]{1,0:T(8,128)}, f32[1152]{0:T(1024)}, ...) custom-call(bf16[3,256,384]{2,1,0:T(8,128)(2,1)} %get-tuple-element., ...), custom_call_target="tpu_custom_call" | custom-call | tf_op jit(solution)/shard_map/finish/pallas_call | solution.py:1234

commit v13 on v12

--- a/solution.py
+++ b/solution.py
@@ -72,21 +72,23 @@
     pl.semaphore_wait(barrier, len(targets))
 
 
-def greet_line(me, runs, others=()):
+def greet_line(me, runs, others=(), tell=True, wait=True):
     barrier = pltpu.get_barrier_semaphore()
-    for target in others:
-        pl.semaphore_signal(barrier, inc=1, device_id=target, device_id_type=MESH)
-
-    @pl.when(me > 0)
-    def _():
-        pl.semaphore_signal(barrier, inc=1, device_id={"seq": me - 1}, device_id_type=MESH)
-
-    @pl.when(me < runs - 1)
-    def _():
-        pl.semaphore_signal(barrier, inc=1, device_id={"seq": me + 1}, device_id_type=MESH)
-
-    neighbours = lax.div(me + runs - 1, runs) + lax.div(2 * runs - 2 - me, runs)
-    pl.semaphore_wait(barrier, neighbours + len(others))
+    if tell:
+        for target in others:
+            pl.semaphore_signal(barrier, inc=1, device_id=target, device_id_type=MESH)
+
+        @pl.when(me > 0)
+        def _():
+            pl.semaphore_signal(barrier, inc=1, device_id={"seq": me - 1}, device_id_type=MESH)
+
+        @pl.when(me < runs - 1)
+        def _():
+            pl.semaphore_signal(barrier, inc=1, device_id={"seq": me + 1}, device_id_type=MESH)
+
+    if wait:
+        neighbours = lax.div(me + runs - 1, runs) + lax.div(2 * runs - 2 - me, runs)
+        pl.semaphore_wait(barrier, neighbours + len(others))
 
 
 def swap_along_line(me, runs, ups, downs, start):
@@ -136,8 +138,7 @@
 
     @pl.when(i == 0)
     def _():
-        greet_line(me, runs)
-        swap_along_line(me, runs, ups, downs, True)
+        greet_line(me, runs, wait=False)
 
         @pl.when(me == 0)
         def _():
@@ -178,6 +179,11 @@
     dy[:, toks:] = jnp.zeros((2, SPARE, inner), F32)
     xe[0] = x_low
     xe[1] = flip_low(x_low)
+
+    @pl.when(i == 0)
+    def _():
+        greet_line(me, runs, tell=False)
+        swap_along_line(me, runs, ups, downs, True)
 
     @pl.when(i == slots - 1)
     def _():
@@ -860,8 +866,7 @@
 
     @pl.when(now == 0)
     def _():
-        greet_line(me, runs, [target for ring in rings + [seq_ring, dp_ring] for target in ring.targets()])
-        swap_along_line(me, runs, ups, downs, True)
+        greet_line(me, runs, [target for ring in rings + [seq_ring, dp_ring] for target in ring.targets()], wait=False)
 
         @pl.when(me == 0)
         def _():
@@ -899,6 +904,12 @@
         hids[i] = hid[...]
         d_gate = jnp.sum(cot_f * branch_out, axis=0, keepdims=True)
         mod_sum[mod_rows, :] = jnp.concatenate([jnp.zeros((2, dim), F32), d_gate, jnp.zeros((5, dim), F32)], axis=0)
+
+    @pl.when(now == 0)
+    def _():
+        peers = [target for ring in rings + [seq_ring, dp_ring] for target in ring.targets()]
+        greet_line(me, runs, peers, tell=False)
+        swap_along_line(me, runs, ups, downs, True)
 
     @pl.when(now == slots)
     def _():

time: 182 us -> 180 us (0.989)
  Pallas kernels: 180 us -> 178 us
where the time goes in v13:
time: 180 us
  Pallas kernels  178 us (99%)
    pallas_call x1, Pallas kernels, per_device(): pl.pallas_call(functools.partial(second_kernel, runs), grid=(2, slots), i...  68.6 us
    pallas_call x1, Pallas kernels, per_device(): pl.pallas_call(functools.partial(tail_kernel, (runs, groups, slots)), gri...  49.2 us
    pallas_call x1, Pallas kernels, per_device(): pl.pallas_call(functools.partial(first_kernel, runs, slots), grid=(2, slo...  44.9 us
    pallas_call x1, Pallas kernels, per_device(): pl.pallas_call(functools.partial(enter_kernel, runs), grid=(slots,), in_s...  8.67 us
    pallas_call x1, Pallas kernels, per_device(): pl.pallas_call(finish_kernel, grid=(4,), in_specs=[part(toks, dim), part(...  6.71 us

profile of v13, /device:TPU:0, one launch (start us, length us, event | category | flops | bytes accessed | tf_op | source)
XLA Modules:
  0.0 179.6 jit_solution(12169644292390387092)
XLA Ops:
  1.3 8.7 %enter.1 = (bf16[3,2,256,768]{3,2,1,0:T(8,128)(2,1)}, f32[3,2,264,768]{3,2,1,0:T(8,128)}, f32[3,256,768]{2,1,0:T(8,128)}, bf16[3,256,384]{2,1,0:T(8,128)(2,1)}, ...) custom-call(bf16[3,256,384]{2,1,0:T(8,128)(2,1)} %tok.3, bf16[3,256,384]{2,1,0:T(8,128)(2,1)} %cot.3, ...), custom_call_target="tpu_custom_call" | custom-call | tf_op jit(solution)/shard_map/enter/pallas_call | solution.py:1088
  10.0 44.9 %first.1 = (bf16[3,2,256,768]{3,2,1,0:T(8,128)(2,1)}, f32[3,2,3,256,768]{4,3,2,1,0:T(8,128)}, f32[3,2,64,256]{3,2,1,0:T(8,128)}, f32[3,2,40,768]{3,2,1,0:T(8,128...) custom-call(bf16[3,2,16,768]{3,2,1,0:T(8,128)(2,1)} %get-tuple-eleme, ...), custom_call_target="tpu_custom_call" | custom-call | tf_op jit(solution)/shard_map/first/pallas_call | solution.py:1127
  54.9 68.6 %second.1 = (f32[3,2,256,768]{3,2,1,0:T(8,128)}, f32[3,2,256,768]{3,2,1,0:T(8,128)}, f32[2,3,8,768]{3,2,1,0:T(8,128)}, f32[2,104,768]{2,1,0:T(8,128)}) custom-call(f32[2,3,16,768]{3,2,1,0:T(8,128)} %get-tuple-element.58.first_in, f32[3,2,40,768]{3,2,1,0:T(8,128)} %get-tuple-element.59.lasts, f32[2,16,768]{2,1,0:T(8,128)} %rate.3, ...), custom_call_target="tpu_custom_call" | custom-call | tf_op jit(solution)/shard_map/second/pallas_call | solution.py:1162
  123.5 49.2 %tail.1 = (bf16[3,256,384]{2,1,0:T(8,128)(2,1)}, f32[3,256,384]{2,1,0:T(8,128)}, bf16[2048,384]{1,0:T(8,128)(2,1)}, bf16[1024,384]{1,0:T(8,128)(2,1)}, bf16[128,...) custom-call(bf16[3,256,384]{2,1,0:T(8,128)(2,1)} %tok.3, bf16[3,256,384]{2,1,0:T(8,128)(2,1)} %cot.3, ...), custom_call_target="tpu_custom_call" | custom-call | tf_op jit(solution)/shard_map/tail/pallas_call | solution.py:1207
  172.8 6.7 %finish.1 = (bf16[3,256,384]{2,1,0:T(8,128)(2,1)}, f32[3,256,384]{2,1,0:T(8,128)}, f32[3,384]{1,0:T(4,128)}, f32[384,1152]{1,0:T(8,128)}, f32[1152]{0:T(1024)}, ...) custom-call(bf16[3,256,384]{2,1,0:T(8,128)(2,1)} %get-tuple-element., ...), custom_call_target="tpu_custom_call" | custom-call | tf_op jit(solution)/shard_map/finish/pallas_call | solution.py:1245
